TPU v7x, 32 devices: a whole 2x2x4 slice. The times are simulated.
32 devices in a mesh: adapter: 8 (over z, y), tensor: 4 (over x, core).
Axes of the slice: x: 2, y: 2, z: 4, core: 2. Of those that a mesh axis runs over, the one named last changes fastest.
Arguments:
- queries: bfloat16 [1024, 4, 4096], P('adapter', None, 'tensor'), may hold values from -160 to 160
- shared_prefix_cache: bfloat16 [2, 16, 2048, 1024], P(None, 'adapter', None, 'tensor'), may hold values from -6 to 6
- rollout_suffix_cache: bfloat16 [2, 1024, 32, 1024], P(None, 'adapter', None, 'tensor'), may hold values from -9 to 9
- fresh_key_value: bfloat16 [2, 1024, 4, 1024], P(None, 'adapter', None, 'tensor'), may hold values from -9 to 9
- rollout_prefix_index: int32 [1024], P('adapter'), may hold values from 0 to 15, as said below
- rollout_suffix_length: int32 [1024], P('adapter'), may hold values from 1 to 32, as said below
- rollout_adapter_index: int32 [1024, 1], P('adapter'), may hold values from 0 to 31; in each aligned block of 128 rows (0 to 127, 128 to 255, ...) at most 5 rows name the same one
- output_projection_weight: bfloat16 [4096, 4096], P('tensor'), may hold values from -0.75 to 0.75
- adapter_shrink_weight: bfloat16 [32, 64, 4096], P('adapter', None, 'tensor'), may hold values from -0.75 to 0.75
- adapter_expand_weight: bfloat16 [32, 64, 4096], P('adapter', None, 'tensor'), may hold values from -0.75 to 0.75
Outputs:
- mixed: bfloat16 [1024, 4, 4096], P('adapter', None, 'tensor')
Inputs may be any that keep to these rules, and one draw needn't show every extreme that they name: rollout_prefix_index[r] // 2 == r // 128: a rollout's prefix is held with it, and the rollouts of one device name each of its 2 prefixes. `rollout_suffix_length`: among the rollouts of one device some has generated 32 tokens. `rollout_adapter_index`: within the rollouts of one device (aligned blocks of 128 rows) no adapter is named more than 5 times, a bound that some block reaches.
All inputs are finite; a program needn't handle non-finite values.
Results may differ from a plain program's by a relative error of at most 0.015.
Values may be sent and summed in bfloat16 or wider, within the bound.
No kernel may reach another device: no remote copies, remote signals or barrier semaphores. Data moves between devices by JAX's collectives and lax.ppermute only.
A program may use at most 128 MiB of HBM per device.

v0:
```python
import functools
import math

import jax
import jax.numpy as jnp
from jax import lax
from jax.experimental import pallas as pl
from jax.experimental.pallas import tpu as pltpu
from jax.sharding import PartitionSpec as P

HEAD_SIZE = 128
MOST = 5
FOLD = 2
CUTS = 1
BLOCK_ROLLS = 32
KEY_CHUNK = 512
NEG = float("-inf")
MIB = 1 << 20
BRIEF = pl.CostEstimate(flops=1024, bytes_accessed=1024, transcendentals=0)
LENGTHY = pl.CostEstimate(flops=1 << 36, bytes_accessed=1 << 27, transcendentals=0)
VMEM = pl.BlockSpec(memory_space=pltpu.VMEM)
ANY = pl.BlockSpec(memory_space=pl.ANY)
SMEM = pl.BlockSpec(memory_space=pltpu.SMEM)


def dot_nt(a, b):
    return lax.dot_general(a, b, (((1,), (1,)), ((), ())), preferred_element_type=jnp.float32)


def dot_nn(a, b):
    return jnp.dot(a, b, preferred_element_type=jnp.float32)


def attend_kernel(
    length_hbm, prefix_hbm, q_hbm, kv_hbm, suf_hbm, fr_hbm, o_ref,
    s_ref, m_ref, length_ref, prefix_ref, q_ref, kv_ref, suf_ref, fr_ref, sems,
    *, steps, group, first, blocks
):
    prefix_count, prefix_len = kv_ref.shape[1], kv_ref.shape[2]
    key_heads = kv_ref.shape[3] // HEAD_SIZE
    rolls, suf_len = suf_hbm.shape[1], suf_hbm.shape[2]
    block_rows = BLOCK_ROLLS * steps
    rows = block_rows * group
    last = first + blocks - 1
    suf_rolls = HEAD_SIZE // suf_len
    suf_rows = suf_rolls * steps
    suf_groups = BLOCK_ROLLS // suf_rolls
    window_rolls = HEAD_SIZE // steps
    windows = window_rolls // BLOCK_ROLLS
    factor = HEAD_SIZE ** (-0.5) * math.log2(math.e)
    chunks = prefix_len // KEY_CHUNK
    span = prefix_len

    def row_codes(block):
        shape = (block_rows, rolls)
        mine = block * BLOCK_ROLLS + lax.broadcasted_iota(jnp.int32, shape, 0) // steps
        lane = lax.broadcasted_iota(jnp.int32, shape, 1)
        code = length_ref[...] * prefix_count + prefix_ref[...] % prefix_count
        code = jnp.broadcast_to(code.astype(jnp.float32), shape)
        col = jnp.sum(jnp.where(mine == lane, code, 0.0), axis=1, keepdims=True)
        col = jnp.broadcast_to(col, (block_rows, HEAD_SIZE)).astype(jnp.int32)
        return col // prefix_count, col % prefix_count

    mine = pl.ds(first * BLOCK_ROLLS, blocks * BLOCK_ROLLS)
    loads = []
    for which in range(2):
        loads.append(pltpu.make_async_copy(kv_hbm.at[which], kv_ref.at[which], sems.at[2 * which]))
        loads.append(
            pltpu.make_async_copy(suf_hbm.at[which, mine], suf_ref.at[which], sems.at[2 * which + 1])
        )
    small = [
        pltpu.make_async_copy(src, dst, sems.at[4 + k])
        for k, (src, dst) in enumerate(
            [(q_hbm, q_ref), (fr_hbm, fr_ref), (length_hbm, length_ref), (prefix_hbm, prefix_ref)]
        )
    ]
    for load in [*reversed(small), *loads]:
        load.start()

    def tile_rows(x):
        return jnp.concatenate([x] * group, axis=0)

    def load_q(block, h):
        span = pl.ds(block * BLOCK_ROLLS, BLOCK_ROLLS)
        return [
            q_ref[span, :, pl.ds((h * group + g) * HEAD_SIZE, HEAD_SIZE)].reshape(
                block_rows, HEAD_SIZE
            )
            for g in range(group)
        ]

    def head_lanes(h):
        return pl.ds(h * HEAD_SIZE, HEAD_SIZE)

    def suffix_tile(which, block, i, h):
        start = (block - first) * BLOCK_ROLLS + i * suf_rolls
        tile = suf_ref[which, pl.ds(start, suf_rolls), :, head_lanes(h)]
        return tile.reshape(HEAD_SIZE, HEAD_SIZE)

    def fresh_tile(which, block, h):
        span = pl.ds(block // windows * window_rolls, window_rolls)
        return fr_ref[which, span, :, head_lanes(h)].reshape(HEAD_SIZE, HEAD_SIZE)

    def prefix_tile(which, c, h):
        return jnp.concatenate(
            [
                kv_ref[which, p, pl.ds(c * KEY_CHUNK, KEY_CHUNK), head_lanes(h)]
                for p in range(prefix_count)
            ],
            axis=1,
        )

    def scores(block, h, slot):
        length, local = row_codes(block)
        parts = load_q(block, h)
        stacked = jnp.concatenate(parts, axis=0)
        wide = jnp.concatenate(
            [
                jnp.concatenate(
                    [jnp.where(local == p, x, jnp.zeros_like(x)) for x in parts], axis=0
                )
                for p in range(prefix_count)
            ],
            axis=1,
        )
        shape = (block_rows, HEAD_SIZE)
        row = lax.broadcasted_iota(jnp.int32, shape, 0)
        lane = lax.broadcasted_iota(jnp.int32, shape, 1)
        roll = row // steps
        keep = (roll % suf_rolls == lane // suf_len) & (lane % suf_len < length)
        suf_bias = jnp.where(keep, 0.0, NEG)
        in_window = (block % windows) * BLOCK_ROLLS + roll
        keep = (in_window == lane // steps) & (lane % steps <= row % steps)
        fr_bias = jnp.where(keep, 0.0, NEG)
        suf = []
        for i in range(suf_groups):
            piece = jnp.concatenate(
                [x[i * suf_rows : (i + 1) * suf_rows] for x in parts], axis=0
            )
            suf.append(dot_nt(piece, suffix_tile(0, block, i, h)))
        suf = jnp.concatenate(
            [
                jnp.concatenate([x[g * suf_rows : (g + 1) * suf_rows] for x in suf], axis=0)
                for g in range(group)
            ],
            axis=0,
        ) + tile_rows(suf_bias)
        fr = dot_nt(stacked, fresh_tile(0, block, h)) + tile_rows(fr_bias)
        s_ref[slot, :, pl.ds(span, HEAD_SIZE)] = suf
        s_ref[slot, :, pl.ds(span + HEAD_SIZE, HEAD_SIZE)] = fr
        top = jnp.maximum(suf, fr)
        yield
        for c in range(chunks):
            s = dot_nt(wide, prefix_tile(0, c, h))
            s_ref[slot, :, pl.ds(c * KEY_CHUNK, KEY_CHUNK)] = s
            for j in range(KEY_CHUNK // HEAD_SIZE):
                top = jnp.maximum(top, s[:, j * HEAD_SIZE : (j + 1) * HEAD_SIZE])
            if c == chunks - 1:
                top = jnp.max(top, axis=1, keepdims=True) * factor
                m_ref[slot] = jnp.broadcast_to(top, (rows, HEAD_SIZE))
            yield

    def outputs(block, h, slot):
        top = m_ref[slot]

        def weigh(start, width):
            x = s_ref[slot, :, pl.ds(start, width)]
            wide_top = jnp.concatenate([top] * (width // HEAD_SIZE), axis=1)
            return jnp.exp2(x * factor - wide_top)

        both = weigh(span, 2 * HEAD_SIZE)
        total = both[:, :HEAD_SIZE] + both[:, HEAD_SIZE:]
        both = both.astype(jnp.bfloat16)
        fr = dot_nn(both[:, HEAD_SIZE:], fresh_tile(1, block, h))
        suf = []
        for i in range(suf_groups):
            piece = jnp.concatenate(
                [
                    both[
                        g * block_rows + i * suf_rows : g * block_rows + (i + 1) * suf_rows,
                        :HEAD_SIZE,
                    ]
                    for g in range(group)
                ],
                axis=0,
            )
            suf.append(dot_nn(piece, suffix_tile(1, block, i, h)))
        extra = fr + jnp.concatenate(
            [
                jnp.concatenate([x[g * suf_rows : (g + 1) * suf_rows] for x in suf], axis=0)
                for g in range(group)
            ],
            axis=0,
        )
        yield
        acc = None
        for c in range(chunks):
            p = weigh(c * KEY_CHUNK, KEY_CHUNK)
            for j in range(KEY_CHUNK // HEAD_SIZE):
                total = total + p[:, j * HEAD_SIZE : (j + 1) * HEAD_SIZE]
            part = dot_nn(p.astype(jnp.bfloat16), prefix_tile(1, c, h))
            acc = part if acc is None else acc + part
            if c == chunks - 1:
                _, local = row_codes(block)
                local = tile_rows(local)
                chosen = acc[:, :HEAD_SIZE]
                for q in range(1, prefix_count):
                    chosen = jnp.where(
                        local == q, acc[:, q * HEAD_SIZE : (q + 1) * HEAD_SIZE], chosen
                    )
                weight = 1.0 / jnp.sum(total, axis=1, keepdims=True)
                out = ((chosen + extra) * weight).astype(o_ref.dtype)
                start = pl.multiple_of((block - first) * block_rows, block_rows)
                for g in range(group):
                    o_ref[
                        pl.ds(start, block_rows),
                        pl.ds((h * group + g) * HEAD_SIZE, HEAD_SIZE),
                    ] = out[g * block_rows : (g + 1) * block_rows]
            yield

    def run(*streams):
        for _ in range(chunks + 1):
            for stream in streams:
                next(stream)

    for load in [*reversed(small), *loads[:2]]:
        load.wait()
    run(scores(first, 0, 0))
    for load in loads[2:]:
        load.wait()

    def body(block, carry):
        for h in range(key_heads):
            if h + 1 < key_heads:
                run(scores(block, h + 1, h + 1), outputs(block, h, h))
            elif key_heads > 1:
                following = jnp.minimum(block + 1, last)
                run(scores(following, 0, 0), outputs(block, h, h))
            else:
                run(outputs(block, h, h))
                run(scores(jnp.minimum(block + 1, last), 0, 0))
        return carry

    lax.fori_loop(first, first + blocks, body, 0)


def attend(lengths, prefixes, queries, prefix, suffix, fresh, steps, first, blocks):
    width = queries.shape[-1]
    rows = blocks * BLOCK_ROLLS * steps
    key_heads = prefix.shape[3] // HEAD_SIZE
    group = width // HEAD_SIZE // key_heads
    unit_rows = BLOCK_ROLLS * steps * group
    span = prefix.shape[2] + 2 * HEAD_SIZE
    held = (2, blocks * BLOCK_ROLLS) + suffix.shape[2:]
    return pl.pallas_call(
        functools.partial(attend_kernel, steps=steps, group=group, first=first, blocks=blocks),
        out_shape=jax.ShapeDtypeStruct((rows, width), jnp.bfloat16),
        in_specs=[ANY] * 6,
        out_specs=VMEM,
        scratch_shapes=[
            pltpu.VMEM((key_heads, unit_rows, span), jnp.float32),
            pltpu.VMEM((key_heads, unit_rows, HEAD_SIZE), jnp.float32),
            pltpu.VMEM(lengths.shape, lengths.dtype),
            pltpu.VMEM(prefixes.shape, prefixes.dtype),
            pltpu.VMEM(queries.shape, queries.dtype),
            pltpu.VMEM(prefix.shape, prefix.dtype),
            pltpu.VMEM(held, suffix.dtype),
            pltpu.VMEM(fresh.shape, fresh.dtype),
            pltpu.SemaphoreType.DMA((8,)),
        ],
        compiler_params=pltpu.CompilerParams(vmem_limit_bytes=52 * MIB),
        cost_estimate=LENGTHY,
    )(lengths, prefixes, queries, prefix, suffix, fresh)


def project_kernel(core_ref, a_ref, w_ref, send_ref, keep_ref, *, count):
    step = pl.program_id(0)
    part = dot_nn(a_ref[...], w_ref[...]).astype(jnp.bfloat16)

    @pl.when(step < count)
    def _():
        send_ref[0] = part

    @pl.when(step >= count)
    def _():
        keep_ref[0] = part


def project(core, attended, weight, out_width):
    rows, width = attended.shape
    count = weight.shape[1] // out_width // 2

    def column(j, core):
        parity = jnp.where(j < count, 1 - core[0], core[0])
        return (0, (j % count) * 2 + parity)

    shape = jax.ShapeDtypeStruct((count, rows, out_width), jnp.bfloat16)
    return pl.pallas_call(
        functools.partial(project_kernel, count=count),
        grid_spec=pltpu.PrefetchScalarGridSpec(
            num_scalar_prefetch=1,
            grid=(2 * count,),
            in_specs=[
                pl.BlockSpec((rows, width), lambda j, core: (0, 0)),
                pl.BlockSpec((width, out_width), column),
            ],
            out_specs=[
                pl.BlockSpec((1, rows, out_width), lambda j, core: (jnp.minimum(j, count - 1), 0, 0)),
                pl.BlockSpec((1, rows, out_width), lambda j, core: (jnp.maximum(j - count, 0), 0, 0)),
            ],
        ),
        out_shape=[shape, shape],
        compiler_params=pltpu.CompilerParams(vmem_limit_bytes=8 * MIB),
        cost_estimate=BRIEF,
    )(core, attended, weight)


def pair_kernel(chip_ref, keep_ref, come_ref, own_ref, *outs, cuts):
    chips = keep_ref.shape[0]
    for shift in range(chips):
        index = (chip_ref[0] + shift) % chips
        pair = keep_ref[index].astype(jnp.float32) + come_ref[index].astype(jnp.float32)
        pair = pair.astype(jnp.bfloat16)
        if shift == 0:
            own_ref[...] = pair
        else:
            for k in range(cuts):
                out = outs[(shift - 1) * cuts + k]
                rows = out.shape[0]
                out[...] = pair[k * rows : (k + 1) * rows]


def pair_sums(chip, keep, come, cuts):
    chips, rows, width = keep.shape
    away = [jax.ShapeDtypeStruct((rows // cuts, width), jnp.bfloat16)] * ((chips - 1) * cuts)
    return pl.pallas_call(
        functools.partial(pair_kernel, cuts=cuts),
        out_shape=[jax.ShapeDtypeStruct((rows, width), jnp.bfloat16)] + away,
        in_specs=[SMEM, VMEM, VMEM],
        out_specs=[VMEM] * (1 + len(away)),
        compiler_params=pltpu.CompilerParams(vmem_limit_bytes=12 * MIB),
        cost_estimate=BRIEF,
    )(chip, keep, come)


def slot_of(row, turn, here, resident, holders):
    block = holders // FOLD
    holder = row // resident
    fold = (here // block - holder // block + FOLD) % FOLD
    place = (holder % block - here % block + block) % block
    return ((place * FOLD + fold) * resident + row % resident) * MOST + turn


def row_slots(row_ref, here, resident, holders):
    row = row_ref[...]
    shape = (row.shape[1], row.shape[1])
    across = jnp.broadcast_to(row, shape)
    down, lane = lax.broadcasted_iota(jnp.int32, shape, 0), lax.broadcasted_iota(jnp.int32, shape, 1)
    values = across.astype(jnp.float32)
    col = jnp.sum(jnp.where(down == lane, values, 0.0), axis=1, keepdims=True)
    same = jnp.broadcast_to(col, shape) == values
    turn_row = jnp.sum(jnp.where(same & (down < lane), 1.0, 0.0), axis=0, keepdims=True)
    turn_col = jnp.sum(jnp.where(same & (lane < down), 1.0, 0.0), axis=1, keepdims=True)
    place_row = slot_of(row, turn_row.astype(jnp.int32), here, resident, holders)
    place_col = slot_of(
        jnp.broadcast_to(col, shape).astype(jnp.int32),
        jnp.broadcast_to(turn_col, shape).astype(jnp.int32),
        here,
        resident,
        holders,
    )
    return place_row, place_col[:, :1]


def pack_kernel(here_ref, row_ref, *refs, steps, resident, holders, count):
    parts, outs = refs[:-count], refs[-count:]
    slots, rolls = outs[0].shape[0], row_ref.shape[1]
    place, _ = row_slots(row_ref, here_ref[0], resident, holders)
    for d, out in enumerate(outs):
        shape = (slots, rolls)
        slot = (d * slots + lax.broadcasted_iota(jnp.int32, shape, 0)) // steps
        picked = jnp.where(slot == jnp.broadcast_to(place, shape), 1.0, 0.0).astype(jnp.bfloat16)
        total, start = None, 0
        for part in parts:
            rows = part.shape[0]
            shape = (rolls, rows)
            spread = lax.broadcasted_iota(jnp.int32, shape, 0) == (
                start + lax.broadcasted_iota(jnp.int32, shape, 1)
            ) // steps
            chosen = dot_nn(picked, jnp.where(spread, 1.0, 0.0).astype(jnp.bfloat16))
            shape = (slots, rows)
            step = lax.broadcasted_iota(jnp.int32, shape, 0) % steps
            aligned = step == (start + lax.broadcasted_iota(jnp.int32, shape, 1)) % steps
            chosen = jnp.where(aligned, chosen, 0.0).astype(jnp.bfloat16)
            term = dot_nn(chosen, part[...])
            total = term if total is None else total + term
            start += rows
        out[...] = total.astype(jnp.bfloat16)


def pack(here, adapter_row, parts, count, slots, steps, resident, holders):
    width = parts[0].shape[1]
    return pl.pallas_call(
        functools.partial(
            pack_kernel, steps=steps, resident=resident, holders=holders, count=count
        ),
        out_shape=[jax.ShapeDtypeStruct((slots, width), jnp.bfloat16)] * count,
        in_specs=[SMEM] + [VMEM] * (1 + len(parts)),
        out_specs=[VMEM] * count,
        compiler_params=pltpu.CompilerParams(vmem_limit_bytes=12 * MIB),
        cost_estimate=BRIEF,
    )(here, adapter_row, *parts)


def adapter_mask(rows, per_adapter, rank, tile):
    lane = lax.broadcasted_iota(jnp.int32, (rows, HEAD_SIZE), 1) + tile * HEAD_SIZE
    row = lax.broadcasted_iota(jnp.int32, (rows, HEAD_SIZE), 0)
    return lane // rank == row // per_adapter


def shrink_kernel(*refs, per_adapter, rank, count):
    weights, pieces, out = refs[:FOLD], refs[FOLD : FOLD + count], refs[-1]
    rows = pieces[0].shape[0] // FOLD
    found = []
    for k in range(FOLD):
        span = pl.ds(k * rows, rows)
        every = dot_nt(
            jnp.concatenate([p[span, :] for p in pieces], axis=0),
            weights[k][...],
        )
        for d in range(count):
            total = None
            for tile in range(every.shape[1] // HEAD_SIZE):
                x = every[d * rows : (d + 1) * rows, tile * HEAD_SIZE : (tile + 1) * HEAD_SIZE]
                x = jnp.where(adapter_mask(rows, per_adapter, rank, tile), x, 0.0)
                total = x if total is None else total + x
            summed = total
            for turn in range(1, HEAD_SIZE // rank):
                summed = summed + pltpu.roll(total, turn * rank, axis=1)
            found.append(summed)
    lane = lax.broadcasted_iota(jnp.int32, (rows, HEAD_SIZE), 1)
    for d in range(count):
        both = jnp.where(lane < rank, found[d], found[count + d])
        out[pl.ds(d * rows, rows), :] = both


def shrink_rows(weights, pieces, per_adapter, rank):
    count = len(pieces)
    rows, width = pieces[0].shape
    return pl.pallas_call(
        functools.partial(shrink_kernel, per_adapter=per_adapter, rank=rank, count=count),
        out_shape=jax.ShapeDtypeStruct((count * rows // FOLD, HEAD_SIZE), jnp.float32),
        in_specs=[VMEM] * (FOLD + count),
        out_specs=VMEM,
        compiler_params=pltpu.CompilerParams(vmem_limit_bytes=8 * MIB),
        cost_estimate=LENGTHY,
    )(*weights, *pieces)


def expand_kernel(*refs, per_adapter, rank, count, terms):
    weights, sums, outs = refs[:FOLD], refs[FOLD : FOLD + terms], refs[FOLD + terms :]
    depth = weights[0].shape[0]
    rows = outs[0].shape[0] // FOLD
    for k in range(FOLD):
        spread = []
        for d in range(count):
            span = pl.ds(d * rows, rows)
            code = sums[0][span, :].astype(jnp.float32)
            for other in sums[1:]:
                code = code + other[span, :].astype(jnp.float32)
            lane = lax.broadcasted_iota(jnp.int32, (rows, HEAD_SIZE), 1)
            turned = pltpu.roll(code, rank, axis=1)
            code = jnp.where((lane < rank) == (k == 0), code, turned)
            spread.append(
                jnp.concatenate(
                    [
                        jnp.where(adapter_mask(rows, per_adapter, rank, tile), code, 0.0)
                        for tile in range(depth // HEAD_SIZE)
                    ],
                    axis=1,
                ).astype(jnp.bfloat16)
            )
        wide = dot_nn(jnp.concatenate(spread, axis=0), weights[k][...])
        wide = wide.astype(jnp.bfloat16)
        for d in range(count):
            outs[d][pl.ds(k * rows, rows), :] = wide[d * rows : (d + 1) * rows]


def expand_rows(weights, sums, per_adapter, rank, count):
    rows = sums[0].shape[0] // count * FOLD
    width = weights[0].shape[1]
    return pl.pallas_call(
        functools.partial(
            expand_kernel, per_adapter=per_adapter, rank=rank, count=count, terms=len(sums)
        ),
        out_shape=[jax.ShapeDtypeStruct((rows, width), jnp.bfloat16)] * count,
        in_specs=[VMEM] * (FOLD + len(sums)),
        out_specs=[VMEM] * count,
        compiler_params=pltpu.CompilerParams(vmem_limit_bytes=8 * MIB),
        cost_estimate=LENGTHY,
    )(*weights, *sums)


def choose_kernel(here_ref, row_ref, chosen_ref, *, steps, resident, holders):
    rows, total = chosen_ref.shape
    rolls = row_ref.shape[1]
    _, place = row_slots(row_ref, here_ref[0], resident, holders)
    shape = (rolls, total)
    slot = lax.broadcasted_iota(jnp.int32, shape, 1) // steps
    picked = jnp.where(slot == jnp.broadcast_to(place, shape), 1.0, 0.0).astype(jnp.bfloat16)
    shape = (rows, rolls)
    roll = lax.broadcasted_iota(jnp.int32, shape, 0) // steps
    spread = roll == lax.broadcasted_iota(jnp.int32, shape, 1)
    chosen = dot_nn(jnp.where(spread, 1.0, 0.0).astype(jnp.bfloat16), picked)
    shape = (rows, total)
    step = lax.broadcasted_iota(jnp.int32, shape, 0) % steps
    aligned = step == lax.broadcasted_iota(jnp.int32, shape, 1) % steps
    chosen_ref[...] = jnp.where(aligned, chosen, 0.0).astype(jnp.bfloat16)


def choose(here, adapter_row, total, steps, resident, holders):
    rows = adapter_row.shape[1] * steps
    return pl.pallas_call(
        functools.partial(choose_kernel, steps=steps, resident=resident, holders=holders),
        out_shape=jax.ShapeDtypeStruct((rows, total), jnp.bfloat16),
        in_specs=[SMEM, VMEM],
        out_specs=VMEM,
        compiler_params=pltpu.CompilerParams(vmem_limit_bytes=20 * MIB),
        cost_estimate=BRIEF,
    )(here, adapter_row)


def combine_kernel(chosen_ref, *refs, count, starts):
    pieces, sums, out, total_ref = refs[:count], refs[count:-2], refs[-2], refs[-1]
    stacked = jnp.concatenate([x[...] for x in pieces], axis=0)
    total_ref[...] = dot_nn(chosen_ref[...], stacked)
    for start, x in zip(starts, sums):
        span = pl.ds(start, x.shape[0])
        total_ref[span, :] += x[...].astype(jnp.float32)
    out[...] = total_ref[...].reshape(out.shape).astype(jnp.bfloat16)


def combine(chosen, pieces, sums, steps):
    width = pieces[0].shape[1]
    count = len(pieces)
    starts, flat = zip(*sums)
    rows = chosen.shape[0]
    block = min(width, 2 * HEAD_SIZE)

    def columns(x):
        return pl.BlockSpec((x, block), lambda j: (0, j))

    return pl.pallas_call(
        functools.partial(combine_kernel, count=count, starts=starts),
        grid=(width // block,),
        out_shape=jax.ShapeDtypeStruct((rows // steps, steps, width), jnp.bfloat16),
        in_specs=[pl.BlockSpec(chosen.shape, lambda j: (0, 0))]
        + [columns(x.shape[0]) for x in (*pieces, *flat)],
        out_specs=pl.BlockSpec((rows // steps, steps, block), lambda j: (0, 0, j)),
        scratch_shapes=[pltpu.VMEM((rows, block), jnp.float32)],
        compiler_params=pltpu.CompilerParams(vmem_limit_bytes=20 * MIB),
        cost_estimate=BRIEF,
    )(chosen, *pieces, *flat)


def local(
    queries,
    shared_prefix_cache,
    rollout_suffix_cache,
    fresh_key_value,
    rollout_prefix_index,
    rollout_suffix_length,
    rollout_adapter_index,
    output_projection_weight,
    adapter_shrink_weight,
    adapter_expand_weight,
):
    rolls, steps, width = queries.shape
    rows = rolls * steps
    prefix_count = shared_prefix_cache.shape[1]
    resident, rank, out_width = adapter_expand_weight.shape
    holders, sides = lax.axis_size("adapter"), lax.axis_size("tensor")
    block, chips = holders // FOLD, sides // 2
    here, side = lax.axis_index("adapter"), lax.axis_index("tensor")
    chip, core = side // 2, side % 2

    def in_block(shift):
        return [(i, i // block * block + (i + shift) % block) for i in range(holders)]

    cores = [(t, t // 2 * 2 + (t + 1) % 2) for t in range(sides)]

    def over_chips(shift):
        return [(t, (t // 2 + shift) % chips * 2 + t % 2) for t in range(sides)]

    own_shrink = adapter_shrink_weight.reshape(resident * rank, width)
    own_expand = adapter_expand_weight.reshape(resident * rank, out_width)
    far = [(i, (i + block) % holders) for i in range(holders)]

    slots = FOLD * resident * MOST * steps
    per_adapter = MOST * steps
    adapter_row = rollout_adapter_index.reshape(1, rolls)
    lengths, prefixes = rollout_suffix_length[None, :], rollout_prefix_index[None, :]
    here = here.reshape(1).astype(jnp.int32)
    core = core.reshape(1).astype(jnp.int32)
    chip_index = chip.reshape(1).astype(jnp.int32)
    tie = lax.optimization_barrier

    def send_over_chips(away, cuts):
        return [
            lax.ppermute(x, "tensor", over_chips(1 + k // cuts)) for k, x in enumerate(away)
        ]

    def placed(start, own, came, cuts):
        rows = own.shape[0] // cuts
        return [(start, own)] + [(start + k % cuts * rows, x) for k, x in enumerate(came)]

    shrink = lax.ppermute(own_shrink, "adapter", far)
    attended = attend(
        lengths, prefixes, queries, shared_prefix_cache, rollout_suffix_cache, fresh_key_value,
        steps, 0, rolls // BLOCK_ROLLS,
    )
    packed = list(pack(here, adapter_row, [attended], block, slots, steps, resident, holders))
    attended, packed[0] = tie((attended, packed[0]))
    pieces = [packed[0]] + [
        lax.ppermute(packed[d], "adapter", in_block(d)) for d in range(1, block)
    ]
    send, keep = project(core, attended, output_projection_weight, out_width)
    chosen = choose(here, adapter_row, block * slots, steps, resident, holders)
    send, chosen = tie((send, chosen))
    own, *away = pair_sums(chip_index, keep, lax.ppermute(send, "tensor", cores), 1)
    pieces[0], shrink, moved = tie((pieces[0], shrink, own_expand))
    expand = lax.ppermute(moved, "adapter", far)
    codes = shrink_rows([own_shrink, shrink], pieces, per_adapter, rank)
    codes = codes + lax.ppermute(codes, "tensor", cores)
    brief = codes.astype(jnp.bfloat16)
    codes = [brief] + [lax.ppermute(brief, "tensor", over_chips(s)) for s in range(1, chips)]
    codes, away = tie((codes, away))
    came = send_over_chips(away, 1)
    wide = expand_rows([own_expand, expand], codes, per_adapter, rank, block)
    back = [wide[0]] + [
        lax.ppermute(wide[d], "adapter", in_block(block - d)) for d in range(1, block)
    ]
    return combine(chosen, back, placed(0, own, came, 1), steps)


def solution(mesh):
    placed = (
        P("adapter", None, "tensor"),
        P(None, "adapter", None, "tensor"),
        P(None, "adapter", None, "tensor"),
        P(None, "adapter", None, "tensor"),
        P("adapter"),
        P("adapter"),
        P("adapter", None),
        P("tensor", None),
        P("adapter", None, "tensor"),
        P("adapter", None, "tensor"),
    )
    return jax.shard_map(
        local, mesh=mesh, in_specs=placed, out_specs=P("adapter", None, "tensor"), check_vma=False
    )
```

profile of v0, /device:TPU:0, one launch (start us, length us, event | category | flops | bytes accessed | tf_op | source)
XLA Modules:
  0.0 92.0 jit_solution(2252316406528409543)
XLA Ops:
  0.0 4.0 %collective-permute-start = (bf16[256,1024]{1,0:T(8,128)(2,1)}, bf16[256,1024]{1,0:T(8,128)(2,1)S(1)}, u32[]{:S(2)}, u32[]{:S(2)}) collective-permute-start(bf16[256,1024]{1,0:T(8,128)(2,1)} %bitcast.10), channel_id=1, source_target_pairs={{0,16},{4,20},{8,24},{12,28},{16,0},{20,4},{24,8},{28,12},{1,17},{... | collective-permute-start | bytes 1572872 | tf_op jit(solution)/shard_map/ppermute | solution.py:617
  4.0 0.0 copy-start.4
  4.0 1.0 %copy-done.4 = bf16[2,128,4,256]{3,2,1,0:T(4,128)(2,1)S(1)} copy-done((bf16[2,128,4,256]{3,2,1,0:T(4,128)(2,1)S(1)}, bf16[2,128,4,256]{3,2,1,0:T(4,128)(2,1)}, u32[]{:S(2)}) %copy-start.4) | copy-done | bytes 524312
  5.1 0.0 copy-start.7
  5.1 0.7 copy-done.7
  5.7 0.0 copy-start.8
  5.7 0.7 copy-done.8
  6.4 0.0 copy-start.3
  6.4 20.0 %shard_map.100.refs_0_.a_ref = bf16[512,1024]{1,0:T(8,128)(2,1)S(1)} custom-call(s32[1,128]{1,0:T(1,128)S(1)} %bitcast.14, s32[1,128]{1,0:T(1,128)S(1)} %bitcast.15, bf16[128,4,1024]{2,1,0:T(4,128)(2,1)} %q_hbm.1, bf16[2,2,2048,256]{3,2,1,0:T(8,128)(2,1)} %kv_hbm.1, bf16[2,128,32,256]{3,2,1,0:T(8,128)(2,1)} %suf_hbm.1, bf16[2,128,4,256]{3,2,1,0:T(4,128)(2,1)S(1)} %copy-done.4), custom_call_target="tpu_custom_call" | custom-call | flops 68719476736 | bytes 134217728 | tf_op jit(solution)/shard_map/pallas_call | solution.py:255
  26.4 0.0 copy-done.3
  26.4 2.2 %shard_map.101 = (bf16[160,1024]{1,0:T(8,128)(2,1)S(1)}, bf16[160,1024]{1,0:T(8,128)(2,1)}, bf16[160,1024]{1,0:T(8,128)(2,1)}, bf16[160,1024]{1,0:T(8,128)(2,1)}) custom-call(s32[1]{0:T(128)} %bitcast.3.here_ref, s32[1,128]{1,0:T(1,128)S(1)} %bitcast.8, bf16[512,1024]{1,0:T(8,128)(2,1)S(1)} %shard_map.100.refs_0_.a_ref), custom_call_target="tpu_custom_call" | custom-call | flops 1024 | bytes 1024 | tf_op jit(solution)/shard_map/pallas_call | solution.py:403
  28.6 1.5 %collective-permute-start.2 = (bf16[160,1024]{1,0:T(8,128)(2,1)}, bf16[160,1024]{1,0:T(8,128)(2,1)S(1)}, u32[]{:S(2)}, u32[]{:S(2)}) collective-permute-start(bf16[160,1024]{1,0:T(8,128)(2,1)} %get-tuple-element.35), channel_id=1, source_target_pairs={{0,4},{4,8},{8,12},{12,0},{16,20},{20,24},{24,28},{28,16},{1,5},{5... | collective-permute-start | bytes 983048 | tf_op jit(solution)/shard_map/ppermute | solution.py:625
  30.1 1.6 %collective-permute-start.3 = (bf16[160,1024]{1,0:T(8,128)(2,1)}, bf16[160,1024]{1,0:T(8,128)(2,1)}, u32[]{:S(2)}, u32[]{:S(2)}) collective-permute-start(bf16[160,1024]{1,0:T(8,128)(2,1)} %get-tuple-element.36), channel_id=1, source_target_pairs={{0,8},{4,12},{8,0},{12,4},{16,24},{20,28},{24,16},{28,20},{1,9},{5... | collective-permute-start | bytes 983048 | tf_op jit(solution)/shard_map/ppermute | solution.py:625
  31.7 1.4 %collective-permute-start.4 = (bf16[160,1024]{1,0:T(8,128)(2,1)}, bf16[160,1024]{1,0:T(8,128)(2,1)}, u32[]{:S(2)}, u32[]{:S(2)}) collective-permute-start(bf16[160,1024]{1,0:T(8,128)(2,1)} %get-tuple-element.37), channel_id=1, source_target_pairs={{0,12},{4,0},{8,4},{12,8},{16,28},{20,16},{24,20},{28,24},{1,13},{... | collective-permute-start | bytes 983048 | tf_op jit(solution)/shard_map/ppermute | solution.py:625
  33.1 0.6 shard_map.103.chosen_ref
  33.7 0.0 copy-start
  33.7 3.4 %copy-done = bf16[1024,4096]{1,0:T(8,128)(2,1)S(1)} copy-done((bf16[1024,4096]{1,0:T(8,128)(2,1)S(1)}, bf16[1024,4096]{1,0:T(8,128)(2,1)}, u32[]{:S(2)}) %copy-start) | copy-done | bytes 8388632
  37.1 0.0 copy-start.6
  37.1 0.0 copy-start.5
  37.1 7.0 %shard_map.102 = (bf16[2,512,1024]{2,1,0:T(8,128)(2,1)}, bf16[2,512,1024]{2,1,0:T(8,128)(2,1)S(1)}) custom-call(s32[1]{0:T(128)} %bitcast.core_ref, bf16[512,1024]{1,0:T(8,128)(2,1)S(1)} %shard_map.100.refs_0_.a_ref, bf16[1024,4096]{1,0:T(8,128)(2,1)S(1)} %copy-done), custom_call_target="tpu_custom_call" | custom-call | flops 1024 | bytes 1024 | tf_op jit(solution)/shard_map/pallas_call | solution.py:298
  44.1 0.0 copy-start.1
  44.1 0.0 collective-permute-start.7
  44.1 0.0 collective-permute-done.refs_1_
  44.2 0.0 copy-done.6
  44.2 0.4 collective-permute-start.1
  44.6 0.0 collective-permute-done.2.refs_3_
  44.6 0.0 collective-permute-done.3.refs_4_
  44.6 1.4 %collective-permute-done.4.refs_5_ = bf16[160,1024]{1,0:T(8,128)(2,1)} collective-permute-done((bf16[160,1024]{1,0:T(8,128)(2,1)}, bf16[160,1024]{1,0:T(8,128)(2,1)}, u32[]{:S(2)}, u32[]{:S(2)}) %collective-permute-start.4) | collective-permute-done | bytes 327712 | tf_op jit(solution)/shard_map/ppermute | solution.py:625
  46.0 0.0 copy-done.5
  46.0 1.7 %shard_map.104 = f32[320,128]{1,0:T(8,128)S(1)} custom-call(bf16[256,1024]{1,0:T(8,128)(2,1)S(1)} %bitcast.11, bf16[256,1024]{1,0:T(8,128)(2,1)S(1)} %collective-permute-done.refs_1_, bf16[160,1024]{1,0:T(8,128)(2,1)S(1)} %get-tuple-element.34.refs_2_, bf16[160,1024]{1,0:T(8,128)(2,1)S(1)} %collective-permute-done.2.refs_3_, ...), custom_call_target="tpu_custom_call" | custom-call | flops 68719476736 | bytes 134217728 | tf_op jit(solution)/shard_map/pallas_call | solution.py:450
  47.7 0.0 copy-done.1
  47.7 0.1 collective-permute-start.5
  47.8 1.4 %collective-permute-done.5 = f32[320,128]{1,0:T(8,128)S(1)} collective-permute-done((f32[320,128]{1,0:T(8,128)S(1)}, f32[320,128]{1,0:T(8,128)S(1)}, u32[]{:S(2)}, u32[]{:S(2)}) %collective-permute-start.5) | collective-permute-done | bytes 163872 | tf_op jit(solution)/shard_map/ppermute | solution.py:634
  49.2 1.6 %collective-permute-start.6 = (bf16[320,128]{1,0:T(8,128)(2,1)S(1)}, bf16[320,128]{1,0:T(8,128)(2,1)S(1)}, u32[]{:S(2)}, u32[]{:S(2)}) collective-permute-start(bf16[320,128]{1,0:T(8,128)(2,1)S(1)} %add_convert_fusion.refs_2_), channel_id=1, source_target_pairs={{0,2},{1,3},{2,0},{3,1},{4,6},{5,7},{6,4},{7,5},{8,10},{9,11},{10,... | collective-permute-start | bytes 245768 | tf_op jit(solution)/shard_map/ppermute | solution.py:636
  50.8 0.0 collective-permute-done.7.come_ref
  50.8 0.0 copy-start.2
  50.8 1.6 %copy-done.2 = bf16[2,512,1024]{2,1,0:T(8,128)(2,1)S(1)} copy-done((bf16[2,512,1024]{2,1,0:T(8,128)(2,1)S(1)}, bf16[2,512,1024]{2,1,0:T(8,128)(2,1)}, u32[]{:S(2)}) %copy-start.2) | copy-done | bytes 2097176
  52.4 2.1 %shard_map.105 = (bf16[512,1024]{1,0:T(8,128)(2,1)S(1)}, bf16[512,1024]{1,0:T(8,128)(2,1)S(1)}) custom-call(s32[1]{0:T(128)} %bitcast.7.chip_ref, bf16[2,512,1024]{2,1,0:T(8,128)(2,1)S(1)} %copy-done.2, bf16[2,512,1024]{2,1,0:T(8,128)(2,1)} %collective-permute-done.7.come_ref), custom_call_target="tpu_custom_call" | custom-call | flops 1024 | bytes 1024 | tf_op jit(solution)/shard_map/pallas_call | solution.py:336
  54.4 0.0 collective-permute-done.6.refs_3_
  54.4 0.8 collective-permute-start.11
  55.3 15.3 %collective-permute-done.1.refs_1_ = bf16[256,1024]{1,0:T(8,128)(2,1)S(1)} collective-permute-done((bf16[256,1024]{1,0:T(8,128)(2,1)S(1)}, bf16[256,1024]{1,0:T(8,128)(2,1)S(1)}, u32[]{:S(2)}, u32[]{:S(2)}) %collective-permute-start.1) | collective-permute-done | bytes 524320 | tf_op jit(solution)/shard_map/ppermute | solution.py:632
  70.5 0.6 shard_map.106
  71.1 0.1 collective-permute-start.8
  71.1 2.1 %collective-permute-start.9 = (bf16[160,1024]{1,0:T(8,128)(2,1)S(1)}, bf16[160,1024]{1,0:T(8,128)(2,1)S(1)}, u32[]{:S(2)}, u32[]{:S(2)}) collective-permute-start(bf16[160,1024]{1,0:T(8,128)(2,1)S(1)} %get-tuple-element.45), channel_id=1, source_target_pairs={{0,8},{4,12},{8,0},{12,4},{16,24},{20,28},{24,16},{28,20},{1,9},{5... | collective-permute-start | bytes 983048 | tf_op jit(solution)/shard_map/ppermute | solution.py:641
  73.2 0.0 collective-permute-start.10
  73.2 7.6 %collective-permute-done.8.refs_1_ = bf16[160,1024]{1,0:T(8,128)(2,1)S(1)} collective-permute-done((bf16[160,1024]{1,0:T(8,128)(2,1)S(1)}, bf16[160,1024]{1,0:T(8,128)(2,1)S(1)}, u32[]{:S(2)}, u32[]{:S(2)}) %collective-permute-start.8) | collective-permute-done | bytes 327712 | tf_op jit(solution)/shard_map/ppermute | solution.py:641
  80.8 7.1 %collective-permute-done.9.refs_2_ = bf16[160,1024]{1,0:T(8,128)(2,1)S(1)} collective-permute-done((bf16[160,1024]{1,0:T(8,128)(2,1)S(1)}, bf16[160,1024]{1,0:T(8,128)(2,1)S(1)}, u32[]{:S(2)}, u32[]{:S(2)}) %collective-permute-start.9) | collective-permute-done | bytes 327712 | tf_op jit(solution)/shard_map/ppermute | solution.py:641
  87.9 1.1 %collective-permute-done.10.refs_3_ = bf16[160,1024]{1,0:T(8,128)(2,1)S(1)} collective-permute-done((bf16[160,1024]{1,0:T(8,128)(2,1)S(1)}, bf16[160,1024]{1,0:T(8,128)(2,1)S(1)}, u32[]{:S(2)}, u32[]{:S(2)}) %collective-permute-start.10) | collective-permute-done | bytes 327712 | tf_op jit(solution)/shard_map/ppermute | solution.py:641
  89.0 0.0 collective-permute-done.11.refs_5_
  89.0 3.0 %shard_map.107 = bf16[128,4,1024]{2,1,0:T(4,128)(2,1)} custom-call(bf16[512,640]{1,0:T(8,128)(2,1)S(1)} %shard_map.103.chosen_ref, bf16[160,1024]{1,0:T(8,128)(2,1)S(1)} %get-tuple-element.43.refs_0_, bf16[160,1024]{1,0:T(8,128)(2,1)S(1)} %collective-permute-done.8.refs_1_, bf16[160,1024]{1,0:T(8,128)(2,1)S(1)} %collective-permute-done.9.refs_2_, ...), custom_call_target="tpu_custom_call" | custom-call | flops 1024 | bytes 1024 | tf_op jit(solution)/shard_map/pallas_call | solution.py:553
  (1 shorter events, 0.0 us)
Async XLA Ops:
  0.0 44.1 %collective-permute-start = (bf16[256,1024]{1,0:T(8,128)(2,1)}, bf16[256,1024]{1,0:T(8,128)(2,1)S(1)}, u32[]{:S(2)}, u32[]{:S(2)}) collective-permute-start(bf16[256,1024]{1,0:T(8,128)(2,1)} %bitcast.10), channel_id=1, source_target_pairs={{0,16},{4,20},{8,24},{12,28},{16,0},{20,4},{24,8},{28,12},{1,17},{... | collective-permute-start | bytes 1572872 | tf_op jit(solution)/shard_map/ppermute | solution.py:617
  4.0 1.0 %copy-start.4 = (bf16[2,128,4,256]{3,2,1,0:T(4,128)(2,1)S(1)}, bf16[2,128,4,256]{3,2,1,0:T(4,128)(2,1)}, u32[]{:S(2)}) copy-start(bf16[2,128,4,256]{3,2,1,0:T(4,128)(2,1)} %fr_hbm.1) | copy-start | bytes 1572868
  5.1 0.7 copy-start.7
  5.7 0.7 copy-start.8
  6.4 20.0 %copy-start.3 = (s32[128,1]{0,1:T(1,128)S(1)}, s32[128,1]{0,1:T(1,128)}, u32[]{:S(2)}) copy-start(s32[128,1]{0,1:T(1,128)} %param.16) | copy-start | bytes 1540
  28.6 16.0 %collective-permute-start.2 = (bf16[160,1024]{1,0:T(8,128)(2,1)}, bf16[160,1024]{1,0:T(8,128)(2,1)S(1)}, u32[]{:S(2)}, u32[]{:S(2)}) collective-permute-start(bf16[160,1024]{1,0:T(8,128)(2,1)} %get-tuple-element.35), channel_id=1, source_target_pairs={{0,4},{4,8},{8,12},{12,0},{16,20},{20,24},{24,28},{28,16},{1,5},{5... | collective-permute-start | bytes 983048 | tf_op jit(solution)/shard_map/ppermute | solution.py:625
  30.1 14.4 %collective-permute-start.3 = (bf16[160,1024]{1,0:T(8,128)(2,1)}, bf16[160,1024]{1,0:T(8,128)(2,1)}, u32[]{:S(2)}, u32[]{:S(2)}) collective-permute-start(bf16[160,1024]{1,0:T(8,128)(2,1)} %get-tuple-element.36), channel_id=1, source_target_pairs={{0,8},{4,12},{8,0},{12,4},{16,24},{20,28},{24,16},{28,20},{1,9},{5... | collective-permute-start | bytes 983048 | tf_op jit(solution)/shard_map/ppermute | solution.py:625
  31.7 14.3 %collective-permute-start.4 = (bf16[160,1024]{1,0:T(8,128)(2,1)}, bf16[160,1024]{1,0:T(8,128)(2,1)}, u32[]{:S(2)}, u32[]{:S(2)}) collective-permute-start(bf16[160,1024]{1,0:T(8,128)(2,1)} %get-tuple-element.37), channel_id=1, source_target_pairs={{0,12},{4,0},{8,4},{12,8},{16,28},{20,16},{24,20},{28,24},{1,13},{... | collective-permute-start | bytes 983048 | tf_op jit(solution)/shard_map/ppermute | solution.py:625
  33.7 3.4 %copy-start = (bf16[1024,4096]{1,0:T(8,128)(2,1)S(1)}, bf16[1024,4096]{1,0:T(8,128)(2,1)}, u32[]{:S(2)}) copy-start(bf16[1024,4096]{1,0:T(8,128)(2,1)} %w_ref.1) | copy-start | bytes 25165828
  37.1 7.1 %copy-start.6 = (bf16[4,64,1024]{2,1,0:T(8,128)(2,1)S(1)}, bf16[4,64,1024]{2,1,0:T(8,128)(2,1)}, u32[]{:S(2)}) copy-start(bf16[4,64,1024]{2,1,0:T(8,128)(2,1)} %param.19) | copy-start | bytes 1572868
  37.1 8.9 %copy-start.5 = (bf16[4,64,1024]{2,1,0:T(8,128)(2,1)S(1)}, bf16[4,64,1024]{2,1,0:T(8,128)(2,1)}, u32[]{:S(2)}) copy-start(bf16[4,64,1024]{2,1,0:T(8,128)(2,1)} %param.18) | copy-start | bytes 1572868
  44.1 3.6 %copy-start.1 = (bf16[2,512,1024]{2,1,0:T(8,128)(2,1)}, bf16[2,512,1024]{2,1,0:T(8,128)(2,1)S(1)}, u32[]{:S(2)}) copy-start(bf16[2,512,1024]{2,1,0:T(8,128)(2,1)S(1)} %get-tuple-element.38.keep_ref) | copy-start | bytes 6291460
  44.1 6.6 %collective-permute-start.7 = (bf16[2,512,1024]{2,1,0:T(8,128)(2,1)}, bf16[2,512,1024]{2,1,0:T(8,128)(2,1)}, u32[]{:S(2)}, u32[]{:S(2)}) collective-permute-start(bf16[2,512,1024]{2,1,0:T(8,128)(2,1)} %get-tuple-element.39), channel_id=1, source_target_pairs={{0,1},{1,0},{2,3},{3,2},{4,5},{5,4},{6,7},{7,6},{8,9},{9,8},{10,11... | collective-permute-start | bytes 6291464 | tf_op jit(solution)/shard_map/ppermute | solution.py:630
  44.2 26.4 %collective-permute-start.1 = (bf16[256,1024]{1,0:T(8,128)(2,1)S(1)}, bf16[256,1024]{1,0:T(8,128)(2,1)S(1)}, u32[]{:S(2)}, u32[]{:S(2)}) collective-permute-start(bf16[256,1024]{1,0:T(8,128)(2,1)S(1)} %bitcast.12), channel_id=1, source_target_pairs={{0,16},{4,20},{8,24},{12,28},{16,0},{20,4},{24,8},{28,12},{1,17},{... | collective-permute-start | bytes 1572872 | tf_op jit(solution)/shard_map/ppermute | solution.py:632
  47.7 1.5 %collective-permute-start.5 = (f32[320,128]{1,0:T(8,128)S(1)}, f32[320,128]{1,0:T(8,128)S(1)}, u32[]{:S(2)}, u32[]{:S(2)}) collective-permute-start(f32[320,128]{1,0:T(8,128)S(1)} %shard_map.104), channel_id=1, source_target_pairs={{0,1},{1,0},{2,3},{3,2},{4,5},{5,4},{6,7},{7,6},{8,9},{9,8},{10,11... | collective-permute-start | bytes 491528 | tf_op jit(solution)/shard_map/ppermute | solution.py:634
  49.2 5.2 %collective-permute-start.6 = (bf16[320,128]{1,0:T(8,128)(2,1)S(1)}, bf16[320,128]{1,0:T(8,128)(2,1)S(1)}, u32[]{:S(2)}, u32[]{:S(2)}) collective-permute-start(bf16[320,128]{1,0:T(8,128)(2,1)S(1)} %add_convert_fusion.refs_2_), channel_id=1, source_target_pairs={{0,2},{1,3},{2,0},{3,1},{4,6},{5,7},{6,4},{7,5},{8,10},{9,11},{10,... | collective-permute-start | bytes 245768 | tf_op jit(solution)/shard_map/ppermute | solution.py:636
  50.8 1.6 %copy-start.2 = (bf16[2,512,1024]{2,1,0:T(8,128)(2,1)S(1)}, bf16[2,512,1024]{2,1,0:T(8,128)(2,1)}, u32[]{:S(2)}) copy-start(bf16[2,512,1024]{2,1,0:T(8,128)(2,1)} %copy-done.1) | copy-start | bytes 6291460
  54.4 34.6 %collective-permute-start.11 = (bf16[512,1024]{1,0:T(8,128)(2,1)S(1)}, bf16[512,1024]{1,0:T(8,128)(2,1)S(1)}, u32[]{:S(2)}, u32[]{:S(2)}) collective-permute-start(bf16[512,1024]{1,0:T(8,128)(2,1)S(1)} %get-tuple-element.48), channel_id=1, source_target_pairs={{0,2},{1,3},{2,0},{3,1},{4,6},{5,7},{6,4},{7,5},{8,10},{9,11},{10,... | collective-permute-start | bytes 3145736 | tf_op jit(solution)/shard_map/ppermute | solution.py:610
  71.1 9.8 %collective-permute-start.8 = (bf16[160,1024]{1,0:T(8,128)(2,1)S(1)}, bf16[160,1024]{1,0:T(8,128)(2,1)S(1)}, u32[]{:S(2)}, u32[]{:S(2)}) collective-permute-start(bf16[160,1024]{1,0:T(8,128)(2,1)S(1)} %get-tuple-element.44), channel_id=1, source_target_pairs={{0,12},{4,0},{8,4},{12,8},{16,28},{20,16},{24,20},{28,24},{1,13},{... | collective-permute-start | bytes 983048 | tf_op jit(solution)/shard_map/ppermute | solution.py:641
  71.1 16.8 %collective-permute-start.9 = (bf16[160,1024]{1,0:T(8,128)(2,1)S(1)}, bf16[160,1024]{1,0:T(8,128)(2,1)S(1)}, u32[]{:S(2)}, u32[]{:S(2)}) collective-permute-start(bf16[160,1024]{1,0:T(8,128)(2,1)S(1)} %get-tuple-element.45), channel_id=1, source_target_pairs={{0,8},{4,12},{8,0},{12,4},{16,24},{20,28},{24,16},{28,20},{1,9},{5... | collective-permute-start | bytes 983048 | tf_op jit(solution)/shard_map/ppermute | solution.py:641
  73.2 15.8 %collective-permute-start.10 = (bf16[160,1024]{1,0:T(8,128)(2,1)S(1)}, bf16[160,1024]{1,0:T(8,128)(2,1)S(1)}, u32[]{:S(2)}, u32[]{:S(2)}) collective-permute-start(bf16[160,1024]{1,0:T(8,128)(2,1)S(1)} %get-tuple-element.46), channel_id=1, source_target_pairs={{0,4},{4,8},{8,12},{12,0},{16,20},{20,24},{24,28},{28,16},{1,5},{5... | collective-permute-start | bytes 983048 | tf_op jit(solution)/shard_map/ppermute | solution.py:641
where the time goes:
time: 92.3 us; the launch traced here: 92 us
  Pallas kernels  37.1 us (40%)
  waiting for transfers between devices  33.9 us (37%)
  starting transfers between devices  13.5 us (15%)
  local copies, waits for them, and re-layouts  7.33 us (8%)
    pallas_call x1, Pallas kernels, attend(): pl.pallas_call(functools.partial(attend_kernel, steps=steps, group=group,...  20 us
    ppermute x3, waiting for transfers between devices, local(): lax.ppermute(wide[d], 'adapter', in_block(block - d))  15.8 us
    ppermute x1, waiting for transfers between devices, local(): expand = lax.ppermute(moved, 'adapter', far)  15.3 us
    unnamed x18, local copies, waits for them, and re-layouts  7.33 us
    pallas_call x1, Pallas kernels, project(): pl.pallas_call(functools.partial(project_kernel, count=count), grid_spec=...  7.04 us
    ppermute x3, starting transfers between devices, local(): lax.ppermute(packed[d], 'adapter', in_block(d))  4.5 us
    ppermute x1, starting transfers between devices, local(): shrink = lax.ppermute(own_shrink, 'adapter', far)  4.04 us
    pallas_call x1, Pallas kernels, combine(): pl.pallas_call(functools.partial(combine_kernel, count=count, starts=star...  2.97 us
  transfers between devices with their start and end apart: 12, of which 6 were waited for; matrix products, arithmetic and copies ran while one was open for 0% of the time, Pallas kernels for 37%

commit v1 on v0

--- a/solution.py
+++ b/solution.py
@@ -11,7 +11,6 @@
 HEAD_SIZE = 128
 MOST = 5
 FOLD = 2
-CUTS = 1
 BLOCK_ROLLS = 32
 KEY_CHUNK = 512
 NEG = float("-inf")
@@ -19,7 +18,7 @@
 BRIEF = pl.CostEstimate(flops=1024, bytes_accessed=1024, transcendentals=0)
 LENGTHY = pl.CostEstimate(flops=1 << 36, bytes_accessed=1 << 27, transcendentals=0)
 VMEM = pl.BlockSpec(memory_space=pltpu.VMEM)
-ANY = pl.BlockSpec(memory_space=pl.ANY)
+HBM = pl.BlockSpec(memory_space=pltpu.HBM)
 SMEM = pl.BlockSpec(memory_space=pltpu.SMEM)
 
 
@@ -255,7 +254,7 @@
     return pl.pallas_call(
         functools.partial(attend_kernel, steps=steps, group=group, first=first, blocks=blocks),
         out_shape=jax.ShapeDtypeStruct((rows, width), jnp.bfloat16),
-        in_specs=[ANY] * 6,
+        in_specs=[HBM] * 6,
         out_specs=VMEM,
         scratch_shapes=[
             pltpu.VMEM((key_heads, unit_rows, span), jnp.float32),
@@ -458,7 +457,9 @@
 
 
 def expand_kernel(*refs, per_adapter, rank, count, terms):
-    weights, sums, outs = refs[:FOLD], refs[FOLD : FOLD + terms], refs[FOLD + terms :]
+    held = len(refs) - terms - count
+    sums, outs = refs[held : held + terms], refs[held + terms :]
+    weights = [refs[0][...], jnp.concatenate([x[...] for x in refs[1:held]], axis=0)]
     depth = weights[0].shape[0]
     rows = outs[0].shape[0] // FOLD
     for k in range(FOLD):
@@ -480,7 +481,7 @@
                     axis=1,
                 ).astype(jnp.bfloat16)
             )
-        wide = dot_nn(jnp.concatenate(spread, axis=0), weights[k][...])
+        wide = dot_nn(jnp.concatenate(spread, axis=0), weights[k])
         wide = wide.astype(jnp.bfloat16)
         for d in range(count):
             outs[d][pl.ds(k * rows, rows), :] = wide[d * rows : (d + 1) * rows]
@@ -494,7 +495,7 @@
             expand_kernel, per_adapter=per_adapter, rank=rank, count=count, terms=len(sums)
         ),
         out_shape=[jax.ShapeDtypeStruct((rows, width), jnp.bfloat16)] * count,
-        in_specs=[VMEM] * (FOLD + len(sums)),
+        in_specs=[VMEM] * (len(weights) + len(sums)),
         out_specs=[VMEM] * count,
         compiler_params=pltpu.CompilerParams(vmem_limit_bytes=8 * MIB),
         cost_estimate=LENGTHY,
@@ -620,7 +621,10 @@
         steps, 0, rolls // BLOCK_ROLLS,
     )
     packed = list(pack(here, adapter_row, [attended], block, slots, steps, resident, holders))
-    attended, packed[0] = tie((attended, packed[0]))
+    cut = own_expand.shape[0] // 2
+    halves = [own_expand[:cut], own_expand[cut:]]
+    attended, packed[0], halves = tie((attended, packed[0], halves))
+    expands = [lax.ppermute(halves[0], "adapter", far)]
     pieces = [packed[0]] + [
         lax.ppermute(packed[d], "adapter", in_block(d)) for d in range(1, block)
     ]
@@ -628,15 +632,16 @@
     chosen = choose(here, adapter_row, block * slots, steps, resident, holders)
     send, chosen = tie((send, chosen))
     own, *away = pair_sums(chip_index, keep, lax.ppermute(send, "tensor", cores), 1)
-    pieces[0], shrink, moved = tie((pieces[0], shrink, own_expand))
-    expand = lax.ppermute(moved, "adapter", far)
+    halves[1], expands[0] = tie((halves[1], expands[0]))
+    pieces[0], shrink, halves[1] = tie((pieces[0], shrink, halves[1]))
+    expands.append(lax.ppermute(halves[1], "adapter", far))
     codes = shrink_rows([own_shrink, shrink], pieces, per_adapter, rank)
     codes = codes + lax.ppermute(codes, "tensor", cores)
     brief = codes.astype(jnp.bfloat16)
     codes = [brief] + [lax.ppermute(brief, "tensor", over_chips(s)) for s in range(1, chips)]
     codes, away = tie((codes, away))
     came = send_over_chips(away, 1)
-    wide = expand_rows([own_expand, expand], codes, per_adapter, rank, block)
+    wide = expand_rows([own_expand, *expands], codes, per_adapter, rank, block)
     back = [wide[0]] + [
         lax.ppermute(wide[d], "adapter", in_block(block - d)) for d in range(1, block)
     ]

time: 92.3 us -> 91.7 us (level)
  waiting for transfers between devices: 33.9 us -> 27.7 us
  starting transfers between devices: 13.5 us -> 17.2 us
  Pallas kernels: 37.1 us -> 38.1 us
    ppermute x1 -> x2, waiting for transfers between devices: 15.3 us -> 11.8 us  [the longest x1 6.09 us: local(): expands.append(lax.ppermute(halves[1], 'adapter', far))]
    ppermute x1 -> x2, starting transfers between devices: 0.41 us -> 3.71 us  [the longest x1 3.38 us: local(): expands.append(lax.ppermute(halves[1], 'adapter', far))]
    ppermute x3, waiting for transfers between devices: 1.45 us -> 0.01 us  [local(): lax.ppermute(packed[d], 'adapter', in_block(d))]
    ppermute x1, waiting for transfers between devices: 1.38 us -> 0.01 us  [local(): codes = codes + lax.ppermute(codes, 'tensor', cores)]
    pallas_call x1, Pallas kernels: 0.55 us -> 1.49 us  [expand_rows(): pl.pallas_call(functools.partial(expand_kernel, per_adapter=per_adapter,...]
    unnamed x18 -> x20, local copies, waits for them, and re-layouts: 7.33 us -> 7.34 us
  transfers between devices with their start and end apart: 12 -> 13, of which waited for: 6 -> 5; matrix products, arithmetic and copies ran while one was open for 0% -> 1% of each run, Pallas kernels for 37% -> 38%
where the time goes in v1:
time: 91.7 us; the launch traced here: 91.4 us
  Pallas kernels  38.1 us (42%)
  waiting for transfers between devices  27.7 us (30%)
  starting transfers between devices  17.2 us (19%)
  local copies, waits for them, and re-layouts  8.2 us (9%)
    pallas_call x1, Pallas kernels, attend(): pl.pallas_call(functools.partial(attend_kernel, steps=steps, group=group,...  20 us
    ppermute x3, waiting for transfers between devices, local(): lax.ppermute(wide[d], 'adapter', in_block(block - d))  15.8 us
    unnamed x20, local copies, waits for them, and re-layouts  7.34 us
    pallas_call x1, Pallas kernels, project(): pl.pallas_call(functools.partial(project_kernel, count=count), grid_spec=...  7.02 us
    ppermute x1, waiting for transfers between devices, local(): expands.append(lax.ppermute(halves[1], 'adapter', far))  6.09 us
    ppermute x1, waiting for transfers between devices, local(): expands = [lax.ppermute(halves[0], 'adapter', far)]  5.75 us
    ppermute x3, starting transfers between devices, local(): lax.ppermute(packed[d], 'adapter', in_block(d))  4.5 us
    ppermute x1, starting transfers between devices, local(): shrink = lax.ppermute(own_shrink, 'adapter', far)  4.04 us
  transfers between devices with their start and end apart: 13, of which 5 were waited for; matrix products, arithmetic and copies ran while one was open for 1% of the time, Pallas kernels for 38%

profile of v1, /device:TPU:0, one launch (start us, length us, event | category | flops | bytes accessed | tf_op | source)
XLA Modules:
  0.0 91.4 jit_solution(16867025321617185937)
XLA Ops:
  0.0 4.0 %collective-permute-start.1 = (bf16[256,1024]{1,0:T(8,128)(2,1)}, bf16[256,1024]{1,0:T(8,128)(2,1)S(1)}, u32[]{:S(2)}, u32[]{:S(2)}) collective-permute-start(bf16[256,1024]{1,0:T(8,128)(2,1)} %bitcast.13), channel_id=1, source_target_pairs={{0,16},{4,20},{8,24},{12,28},{16,0},{20,4},{24,8},{28,12},{1,17},{... | collective-permute-start | bytes 1572872 | tf_op jit(solution)/shard_map/ppermute | solution.py:618
  4.0 0.0 copy-start.5
  4.0 1.0 %copy-done.5 = bf16[2,128,4,256]{3,2,1,0:T(4,128)(2,1)S(1)} copy-done((bf16[2,128,4,256]{3,2,1,0:T(4,128)(2,1)S(1)}, bf16[2,128,4,256]{3,2,1,0:T(4,128)(2,1)}, u32[]{:S(2)}) %copy-start.5) | copy-done | bytes 524312
  5.1 0.0 copy-start.7
  5.1 0.7 copy-done.7
  5.7 0.0 copy-start.8
  5.7 0.7 copy-done.8
  6.4 0.0 copy-start.4
  6.4 0.0 copy-start.3
  6.4 20.0 %shard_map.100.refs_0_.a_ref = bf16[512,1024]{1,0:T(8,128)(2,1)S(1)} custom-call(s32[1,128]{1,0:T(1,128)S(1)} %bitcast.15, s32[1,128]{1,0:T(1,128)S(1)} %bitcast.16, bf16[128,4,1024]{2,1,0:T(4,128)(2,1)} %q_hbm.1, bf16[2,2,2048,256]{3,2,1,0:T(8,128)(2,1)} %kv_hbm.1, bf16[2,128,32,256]{3,2,1,0:T(8,128)(2,1)} %suf_hbm.1, bf16[2,128,4,256]{3,2,1,0:T(4,128)(2,1)S(1)} %copy-done.5), custom_call_target="tpu_custom_call" | custom-call | flops 68719476736 | bytes 134217728 | tf_op jit(solution)/shard_map/pallas_call | solution.py:254
  26.4 0.0 copy-done.4
  26.4 2.2 %shard_map.101 = (bf16[160,1024]{1,0:T(8,128)(2,1)S(1)}, bf16[160,1024]{1,0:T(8,128)(2,1)}, bf16[160,1024]{1,0:T(8,128)(2,1)}, bf16[160,1024]{1,0:T(8,128)(2,1)}) custom-call(s32[1]{0:T(128)} %bitcast.3.here_ref, s32[1,128]{1,0:T(1,128)S(1)} %bitcast.11, bf16[512,1024]{1,0:T(8,128)(2,1)S(1)} %shard_map.100.refs_0_.a_ref), custom_call_target="tpu_custom_call" | custom-call | flops 1024 | bytes 1024 | tf_op jit(solution)/shard_map/pallas_call | solution.py:402
  28.7 1.5 %collective-permute-start.3 = (bf16[160,1024]{1,0:T(8,128)(2,1)}, bf16[160,1024]{1,0:T(8,128)(2,1)S(1)}, u32[]{:S(2)}, u32[]{:S(2)}) collective-permute-start(bf16[160,1024]{1,0:T(8,128)(2,1)} %get-tuple-element.43), channel_id=1, source_target_pairs={{0,4},{4,8},{8,12},{12,0},{16,20},{20,24},{24,28},{28,16},{1,5},{5... | collective-permute-start | bytes 983048 | tf_op jit(solution)/shard_map/ppermute | solution.py:629
  30.2 1.6 %collective-permute-start.4 = (bf16[160,1024]{1,0:T(8,128)(2,1)}, bf16[160,1024]{1,0:T(8,128)(2,1)}, u32[]{:S(2)}, u32[]{:S(2)}) collective-permute-start(bf16[160,1024]{1,0:T(8,128)(2,1)} %get-tuple-element.44), channel_id=1, source_target_pairs={{0,8},{4,12},{8,0},{12,4},{16,24},{20,28},{24,16},{28,20},{1,9},{5... | collective-permute-start | bytes 983048 | tf_op jit(solution)/shard_map/ppermute | solution.py:629
  31.8 1.4 %collective-permute-start.5 = (bf16[160,1024]{1,0:T(8,128)(2,1)}, bf16[160,1024]{1,0:T(8,128)(2,1)}, u32[]{:S(2)}, u32[]{:S(2)}) collective-permute-start(bf16[160,1024]{1,0:T(8,128)(2,1)} %get-tuple-element.45), channel_id=1, source_target_pairs={{0,12},{4,0},{8,4},{12,8},{16,28},{20,16},{24,20},{28,24},{1,13},{... | collective-permute-start | bytes 983048 | tf_op jit(solution)/shard_map/ppermute | solution.py:629
  33.2 0.0 copy-done.3
  33.2 0.9 fusion
  34.1 0.3 collective-permute-start
  34.4 0.6 shard_map.103.chosen_ref
  35.0 0.0 copy-start
  35.0 3.4 %copy-done = bf16[1024,4096]{1,0:T(8,128)(2,1)S(1)} copy-done((bf16[1024,4096]{1,0:T(8,128)(2,1)S(1)}, bf16[1024,4096]{1,0:T(8,128)(2,1)}, u32[]{:S(2)}) %copy-start) | copy-done | bytes 8388632
  38.4 0.0 copy-start.6
  38.4 7.0 %shard_map.102 = (bf16[2,512,1024]{2,1,0:T(8,128)(2,1)}, bf16[2,512,1024]{2,1,0:T(8,128)(2,1)S(1)}) custom-call(s32[1]{0:T(128)} %bitcast.core_ref, bf16[512,1024]{1,0:T(8,128)(2,1)S(1)} %shard_map.100.refs_0_.a_ref, bf16[1024,4096]{1,0:T(8,128)(2,1)S(1)} %copy-done), custom_call_target="tpu_custom_call" | custom-call | flops 1024 | bytes 1024 | tf_op jit(solution)/shard_map/pallas_call | solution.py:297
  45.4 0.0 copy-start.1
  45.4 0.0 copy-start.9
  45.4 5.7 %collective-permute-done.refs_1_ = bf16[128,1024]{1,0:T(8,128)(2,1)} collective-permute-done((bf16[128,1024]{1,0:T(8,128)(2,1)}, bf16[128,1024]{1,0:T(8,128)(2,1)}, u32[]{:S(2)}, u32[]{:S(2)}) %collective-permute-start) | collective-permute-done | bytes 262176 | tf_op jit(solution)/shard_map/ppermute | solution.py:627
  51.1 0.0 collective-permute-start.8
  51.1 0.0 collective-permute-done.1.refs_1_
  51.1 0.0 collective-permute-done.3.refs_3_
  51.2 0.0 collective-permute-done.4.refs_4_
  51.2 0.0 collective-permute-done.5.refs_5_
  51.2 0.0 copy-done.6
  51.2 1.7 %shard_map.104 = f32[320,128]{1,0:T(8,128)S(1)} custom-call(bf16[256,1024]{1,0:T(8,128)(2,1)S(1)} %bitcast.14, bf16[256,1024]{1,0:T(8,128)(2,1)S(1)} %collective-permute-done.1.refs_1_, bf16[160,1024]{1,0:T(8,128)(2,1)S(1)} %get-tuple-element.42.refs_2_, bf16[160,1024]{1,0:T(8,128)(2,1)S(1)} %collective-permute-done.3.refs_3_, ...), custom_call_target="tpu_custom_call" | custom-call | flops 68719476736 | bytes 134217728 | tf_op jit(solution)/shard_map/pallas_call | solution.py:449
  52.9 0.0 copy-done.1
  52.9 0.6 collective-permute-start.6
  53.5 0.0 copy-done.9
  53.5 3.4 %collective-permute-start.2 = (bf16[128,1024]{1,0:T(8,128)(2,1)S(1)}, bf16[128,1024]{1,0:T(8,128)(2,1)S(1)}, u32[]{:S(2)}, u32[]{:S(2)}) collective-permute-start(bf16[128,1024]{1,0:T(8,128)(2,1)S(1)} %bitcast.17), channel_id=1, source_target_pairs={{0,16},{4,20},{8,24},{12,28},{16,0},{20,4},{24,8},{28,12},{1,17},{... | collective-permute-start | bytes 786440 | tf_op jit(solution)/shard_map/ppermute | solution.py:637
  56.8 0.0 collective-permute-done.6
  56.9 1.6 %collective-permute-start.7 = (bf16[320,128]{1,0:T(8,128)(2,1)S(1)}, bf16[320,128]{1,0:T(8,128)(2,1)S(1)}, u32[]{:S(2)}, u32[]{:S(2)}) collective-permute-start(bf16[320,128]{1,0:T(8,128)(2,1)S(1)} %add_convert_fusion.refs_3_), channel_id=1, source_target_pairs={{0,2},{1,3},{2,0},{3,1},{4,6},{5,7},{6,4},{7,5},{8,10},{9,11},{10,... | collective-permute-start | bytes 245768 | tf_op jit(solution)/shard_map/ppermute | solution.py:641
  58.4 0.0 collective-permute-done.8.come_ref
  58.4 0.0 copy-start.2
  58.4 1.6 %copy-done.2 = bf16[2,512,1024]{2,1,0:T(8,128)(2,1)S(1)} copy-done((bf16[2,512,1024]{2,1,0:T(8,128)(2,1)S(1)}, bf16[2,512,1024]{2,1,0:T(8,128)(2,1)}, u32[]{:S(2)}) %copy-start.2) | copy-done | bytes 2097176
  60.0 2.1 %shard_map.105 = (bf16[512,1024]{1,0:T(8,128)(2,1)S(1)}, bf16[512,1024]{1,0:T(8,128)(2,1)S(1)}) custom-call(s32[1]{0:T(128)} %bitcast.9.chip_ref, bf16[2,512,1024]{2,1,0:T(8,128)(2,1)S(1)} %copy-done.2, bf16[2,512,1024]{2,1,0:T(8,128)(2,1)} %collective-permute-done.8.come_ref), custom_call_target="tpu_custom_call" | custom-call | flops 1024 | bytes 1024 | tf_op jit(solution)/shard_map/pallas_call | solution.py:335
  62.1 0.0 collective-permute-done.7.refs_4_
  62.1 0.8 collective-permute-start.12
  62.9 6.1 %collective-permute-done.2.refs_2_ = bf16[128,1024]{1,0:T(8,128)(2,1)S(1)} collective-permute-done((bf16[128,1024]{1,0:T(8,128)(2,1)S(1)}, bf16[128,1024]{1,0:T(8,128)(2,1)S(1)}, u32[]{:S(2)}, u32[]{:S(2)}) %collective-permute-start.2) | collective-permute-done | bytes 262176 | tf_op jit(solution)/shard_map/ppermute | solution.py:637
  69.0 1.5 %shard_map.106 = (bf16[160,1024]{1,0:T(8,128)(2,1)S(1)}, bf16[160,1024]{1,0:T(8,128)(2,1)S(1)}, bf16[160,1024]{1,0:T(8,128)(2,1)S(1)}, bf16[160,1024]{1,0:T(8,128)(2,1)S(1)}) custom-call(bf16[256,1024]{1,0:T(8,128)(2,1)S(1)} %bitcast.10, bf16[128,1024]{1,0:T(8,128)(2,1)} %collective-permute-done.refs_1_, ...), custom_call_target="tpu_custom_call" | custom-call | flops 68719476736 | bytes 134217728 | tf_op jit(solution)/shard_map/pallas_call | solution.py:493
  70.5 0.1 collective-permute-start.9
  70.5 1.7 %collective-permute-start.10 = (bf16[160,1024]{1,0:T(8,128)(2,1)S(1)}, bf16[160,1024]{1,0:T(8,128)(2,1)S(1)}, u32[]{:S(2)}, u32[]{:S(2)}) collective-permute-start(bf16[160,1024]{1,0:T(8,128)(2,1)S(1)} %get-tuple-element.53), channel_id=1, source_target_pairs={{0,8},{4,12},{8,0},{12,4},{16,24},{20,28},{24,16},{28,20},{1,9},{5... | collective-permute-start | bytes 983048 | tf_op jit(solution)/shard_map/ppermute | solution.py:646
  72.2 0.3 collective-permute-start.11
  72.5 7.7 %collective-permute-done.9.refs_1_ = bf16[160,1024]{1,0:T(8,128)(2,1)S(1)} collective-permute-done((bf16[160,1024]{1,0:T(8,128)(2,1)S(1)}, bf16[160,1024]{1,0:T(8,128)(2,1)S(1)}, u32[]{:S(2)}, u32[]{:S(2)}) %collective-permute-start.9) | collective-permute-done | bytes 327712 | tf_op jit(solution)/shard_map/ppermute | solution.py:646
  80.2 6.8 %collective-permute-done.10.refs_2_ = bf16[160,1024]{1,0:T(8,128)(2,1)S(1)} collective-permute-done((bf16[160,1024]{1,0:T(8,128)(2,1)S(1)}, bf16[160,1024]{1,0:T(8,128)(2,1)S(1)}, u32[]{:S(2)}, u32[]{:S(2)}) %collective-permute-start.10) | collective-permute-done | bytes 327712 | tf_op jit(solution)/shard_map/ppermute | solution.py:646
  87.0 1.4 %collective-permute-done.11.refs_3_ = bf16[160,1024]{1,0:T(8,128)(2,1)S(1)} collective-permute-done((bf16[160,1024]{1,0:T(8,128)(2,1)S(1)}, bf16[160,1024]{1,0:T(8,128)(2,1)S(1)}, u32[]{:S(2)}, u32[]{:S(2)}) %collective-permute-start.11) | collective-permute-done | bytes 327712 | tf_op jit(solution)/shard_map/ppermute | solution.py:646
  88.4 0.0 collective-permute-done.12.refs_5_
  88.4 3.0 %shard_map.107 = bf16[128,4,1024]{2,1,0:T(4,128)(2,1)} custom-call(bf16[512,640]{1,0:T(8,128)(2,1)S(1)} %shard_map.103.chosen_ref, bf16[160,1024]{1,0:T(8,128)(2,1)S(1)} %get-tuple-element.51.refs_0_, bf16[160,1024]{1,0:T(8,128)(2,1)S(1)} %collective-permute-done.9.refs_1_, bf16[160,1024]{1,0:T(8,128)(2,1)S(1)} %collective-permute-done.10.refs_2_, ...), custom_call_target="tpu_custom_call" | custom-call | flops 1024 | bytes 1024 | tf_op jit(solution)/shard_map/pallas_call | solution.py:554
  (1 shorter events, 0.0 us)
Async XLA Ops:
  0.0 51.1 %collective-permute-start.1 = (bf16[256,1024]{1,0:T(8,128)(2,1)}, bf16[256,1024]{1,0:T(8,128)(2,1)S(1)}, u32[]{:S(2)}, u32[]{:S(2)}) collective-permute-start(bf16[256,1024]{1,0:T(8,128)(2,1)} %bitcast.13), channel_id=1, source_target_pairs={{0,16},{4,20},{8,24},{12,28},{16,0},{20,4},{24,8},{28,12},{1,17},{... | collective-permute-start | bytes 1572872 | tf_op jit(solution)/shard_map/ppermute | solution.py:618
  4.0 1.0 %copy-start.5 = (bf16[2,128,4,256]{3,2,1,0:T(4,128)(2,1)S(1)}, bf16[2,128,4,256]{3,2,1,0:T(4,128)(2,1)}, u32[]{:S(2)}) copy-start(bf16[2,128,4,256]{3,2,1,0:T(4,128)(2,1)} %fr_hbm.1) | copy-start | bytes 1572868
  5.1 0.7 copy-start.7
  5.7 0.7 copy-start.8
  6.4 20.0 %copy-start.4 = (s32[128,1]{0,1:T(1,128)S(1)}, s32[128,1]{0,1:T(1,128)}, u32[]{:S(2)}) copy-start(s32[128,1]{0,1:T(1,128)} %param.16) | copy-start | bytes 1540
  6.4 26.8 %copy-start.3 = (bf16[4,64,1024]{2,1,0:T(8,128)(2,1)S(1)}, bf16[4,64,1024]{2,1,0:T(8,128)(2,1)}, u32[]{:S(2)}) copy-start(bf16[4,64,1024]{2,1,0:T(8,128)(2,1)} %param.19) | copy-start | bytes 1572868
  28.7 22.5 %collective-permute-start.3 = (bf16[160,1024]{1,0:T(8,128)(2,1)}, bf16[160,1024]{1,0:T(8,128)(2,1)S(1)}, u32[]{:S(2)}, u32[]{:S(2)}) collective-permute-start(bf16[160,1024]{1,0:T(8,128)(2,1)} %get-tuple-element.43), channel_id=1, source_target_pairs={{0,4},{4,8},{8,12},{12,0},{16,20},{20,24},{24,28},{28,16},{1,5},{5... | collective-permute-start | bytes 983048 | tf_op jit(solution)/shard_map/ppermute | solution.py:629
  30.2 21.0 %collective-permute-start.4 = (bf16[160,1024]{1,0:T(8,128)(2,1)}, bf16[160,1024]{1,0:T(8,128)(2,1)}, u32[]{:S(2)}, u32[]{:S(2)}) collective-permute-start(bf16[160,1024]{1,0:T(8,128)(2,1)} %get-tuple-element.44), channel_id=1, source_target_pairs={{0,8},{4,12},{8,0},{12,4},{16,24},{20,28},{24,16},{28,20},{1,9},{5... | collective-permute-start | bytes 983048 | tf_op jit(solution)/shard_map/ppermute | solution.py:629
  31.8 19.4 %collective-permute-start.5 = (bf16[160,1024]{1,0:T(8,128)(2,1)}, bf16[160,1024]{1,0:T(8,128)(2,1)}, u32[]{:S(2)}, u32[]{:S(2)}) collective-permute-start(bf16[160,1024]{1,0:T(8,128)(2,1)} %get-tuple-element.45), channel_id=1, source_target_pairs={{0,12},{4,0},{8,4},{12,8},{16,28},{20,16},{24,20},{28,24},{1,13},{... | collective-permute-start | bytes 983048 | tf_op jit(solution)/shard_map/ppermute | solution.py:629
  34.1 17.1 %collective-permute-start = (bf16[128,1024]{1,0:T(8,128)(2,1)}, bf16[128,1024]{1,0:T(8,128)(2,1)}, u32[]{:S(2)}, u32[]{:S(2)}) collective-permute-start(bf16[128,1024]{1,0:T(8,128)(2,1)} %bitcast.5), channel_id=1, source_target_pairs={{0,16},{4,20},{8,24},{12,28},{16,0},{20,4},{24,8},{28,12},{1,17},{... | collective-permute-start | bytes 786440 | tf_op jit(solution)/shard_map/ppermute | solution.py:627
  35.0 3.4 %copy-start = (bf16[1024,4096]{1,0:T(8,128)(2,1)S(1)}, bf16[1024,4096]{1,0:T(8,128)(2,1)}, u32[]{:S(2)}) copy-start(bf16[1024,4096]{1,0:T(8,128)(2,1)} %w_ref.1) | copy-start | bytes 25165828
  38.4 12.8 %copy-start.6 = (bf16[4,64,1024]{2,1,0:T(8,128)(2,1)S(1)}, bf16[4,64,1024]{2,1,0:T(8,128)(2,1)}, u32[]{:S(2)}) copy-start(bf16[4,64,1024]{2,1,0:T(8,128)(2,1)} %param.18) | copy-start | bytes 1572868
  45.4 7.5 %copy-start.1 = (bf16[2,512,1024]{2,1,0:T(8,128)(2,1)}, bf16[2,512,1024]{2,1,0:T(8,128)(2,1)S(1)}, u32[]{:S(2)}) copy-start(bf16[2,512,1024]{2,1,0:T(8,128)(2,1)S(1)} %get-tuple-element.46.keep_ref) | copy-start | bytes 6291460
  45.4 8.1 %copy-start.9 = (bf16[2,64,1024]{2,1,0:T(8,128)(2,1)S(1)}, bf16[2,64,1024]{2,1,0:T(8,128)(2,1)}, u32[]{:S(2)}) copy-start(bf16[2,64,1024]{2,1,0:T(8,128)(2,1)} %get-tuple-element.57) | copy-start | bytes 786436
  51.1 7.3 %collective-permute-start.8 = (bf16[2,512,1024]{2,1,0:T(8,128)(2,1)}, bf16[2,512,1024]{2,1,0:T(8,128)(2,1)}, u32[]{:S(2)}, u32[]{:S(2)}) collective-permute-start(bf16[2,512,1024]{2,1,0:T(8,128)(2,1)} %get-tuple-element.47), channel_id=1, source_target_pairs={{0,1},{1,0},{2,3},{3,2},{4,5},{5,4},{6,7},{7,6},{8,9},{9,8},{10,11... | collective-permute-start | bytes 6291464 | tf_op jit(solution)/shard_map/ppermute | solution.py:634
  52.9 4.0 %collective-permute-start.6 = (f32[320,128]{1,0:T(8,128)S(1)}, f32[320,128]{1,0:T(8,128)S(1)}, u32[]{:S(2)}, u32[]{:S(2)}) collective-permute-start(f32[320,128]{1,0:T(8,128)S(1)} %shard_map.104), channel_id=1, source_target_pairs={{0,1},{1,0},{2,3},{3,2},{4,5},{5,4},{6,7},{7,6},{8,9},{9,8},{10,11... | collective-permute-start | bytes 491528 | tf_op jit(solution)/shard_map/ppermute | solution.py:639
  53.5 15.5 %collective-permute-start.2 = (bf16[128,1024]{1,0:T(8,128)(2,1)S(1)}, bf16[128,1024]{1,0:T(8,128)(2,1)S(1)}, u32[]{:S(2)}, u32[]{:S(2)}) collective-permute-start(bf16[128,1024]{1,0:T(8,128)(2,1)S(1)} %bitcast.17), channel_id=1, source_target_pairs={{0,16},{4,20},{8,24},{12,28},{16,0},{20,4},{24,8},{28,12},{1,17},{... | collective-permute-start | bytes 786440 | tf_op jit(solution)/shard_map/ppermute | solution.py:637
  56.9 5.2 %collective-permute-start.7 = (bf16[320,128]{1,0:T(8,128)(2,1)S(1)}, bf16[320,128]{1,0:T(8,128)(2,1)S(1)}, u32[]{:S(2)}, u32[]{:S(2)}) collective-permute-start(bf16[320,128]{1,0:T(8,128)(2,1)S(1)} %add_convert_fusion.refs_3_), channel_id=1, source_target_pairs={{0,2},{1,3},{2,0},{3,1},{4,6},{5,7},{6,4},{7,5},{8,10},{9,11},{10,... | collective-permute-start | bytes 245768 | tf_op jit(solution)/shard_map/ppermute | solution.py:641
  58.4 1.6 %copy-start.2 = (bf16[2,512,1024]{2,1,0:T(8,128)(2,1)S(1)}, bf16[2,512,1024]{2,1,0:T(8,128)(2,1)}, u32[]{:S(2)}) copy-start(bf16[2,512,1024]{2,1,0:T(8,128)(2,1)} %copy-done.1) | copy-start | bytes 6291460
  62.1 26.3 %collective-permute-start.12 = (bf16[512,1024]{1,0:T(8,128)(2,1)S(1)}, bf16[512,1024]{1,0:T(8,128)(2,1)S(1)}, u32[]{:S(2)}, u32[]{:S(2)}) collective-permute-start(bf16[512,1024]{1,0:T(8,128)(2,1)S(1)} %get-tuple-element.56), channel_id=1, source_target_pairs={{0,2},{1,3},{2,0},{3,1},{4,6},{5,7},{6,4},{7,5},{8,10},{9,11},{10,... | collective-permute-start | bytes 3145736 | tf_op jit(solution)/shard_map/ppermute | solution.py:611
  70.5 9.8 %collective-permute-start.9 = (bf16[160,1024]{1,0:T(8,128)(2,1)S(1)}, bf16[160,1024]{1,0:T(8,128)(2,1)S(1)}, u32[]{:S(2)}, u32[]{:S(2)}) collective-permute-start(bf16[160,1024]{1,0:T(8,128)(2,1)S(1)} %get-tuple-element.52), channel_id=1, source_target_pairs={{0,12},{4,0},{8,4},{12,8},{16,28},{20,16},{24,20},{28,24},{1,13},{... | collective-permute-start | bytes 983048 | tf_op jit(solution)/shard_map/ppermute | solution.py:646
  70.5 16.4 %collective-permute-start.10 = (bf16[160,1024]{1,0:T(8,128)(2,1)S(1)}, bf16[160,1024]{1,0:T(8,128)(2,1)S(1)}, u32[]{:S(2)}, u32[]{:S(2)}) collective-permute-start(bf16[160,1024]{1,0:T(8,128)(2,1)S(1)} %get-tuple-element.53), channel_id=1, source_target_pairs={{0,8},{4,12},{8,0},{12,4},{16,24},{20,28},{24,16},{28,20},{1,9},{5... | collective-permute-start | bytes 983048 | tf_op jit(solution)/shard_map/ppermute | solution.py:646
  72.2 16.1 %collective-permute-start.11 = (bf16[160,1024]{1,0:T(8,128)(2,1)S(1)}, bf16[160,1024]{1,0:T(8,128)(2,1)S(1)}, u32[]{:S(2)}, u32[]{:S(2)}) collective-permute-start(bf16[160,1024]{1,0:T(8,128)(2,1)S(1)} %get-tuple-element.54), channel_id=1, source_target_pairs={{0,4},{4,8},{8,12},{12,0},{16,20},{20,24},{24,28},{28,16},{1,5},{5... | collective-permute-start | bytes 983048 | tf_op jit(solution)/shard_map/ppermute | solution.py:646

commit v2 on v0

--- a/solution.py
+++ b/solution.py
@@ -74,7 +74,7 @@
             [(q_hbm, q_ref), (fr_hbm, fr_ref), (length_hbm, length_ref), (prefix_hbm, prefix_ref)]
         )
     ]
-    for load in [*reversed(small), *loads]:
+    for load in [*reversed(small), *loads[:2]]:
         load.start()
 
     def tile_rows(x):
@@ -225,23 +225,30 @@
 
     for load in [*reversed(small), *loads[:2]]:
         load.wait()
+    for load in loads[2:]:
+        load.start()
     run(scores(first, 0, 0))
     for load in loads[2:]:
         load.wait()
 
-    def body(block, carry):
+    def step(block, ends):
         for h in range(key_heads):
             if h + 1 < key_heads:
                 run(scores(block, h + 1, h + 1), outputs(block, h, h))
+            elif ends:
+                run(outputs(block, h, h))
             elif key_heads > 1:
-                following = jnp.minimum(block + 1, last)
-                run(scores(following, 0, 0), outputs(block, h, h))
+                run(scores(block + 1, 0, 0), outputs(block, h, h))
             else:
                 run(outputs(block, h, h))
-                run(scores(jnp.minimum(block + 1, last), 0, 0))
+                run(scores(block + 1, 0, 0))
+
+    def body(block, carry):
+        step(block, False)
         return carry
 
-    lax.fori_loop(first, first + blocks, body, 0)
+    lax.fori_loop(first, last, body, 0)
+    step(last, True)
 
 
 def attend(lengths, prefixes, queries, prefix, suffix, fresh, steps, first, blocks):
@@ -273,44 +280,27 @@
     )(lengths, prefixes, queries, prefix, suffix, fresh)
 
 
-def project_kernel(core_ref, a_ref, w_ref, send_ref, keep_ref, *, count):
-    step = pl.program_id(0)
-    part = dot_nn(a_ref[...], w_ref[...]).astype(jnp.bfloat16)
-
-    @pl.when(step < count)
-    def _():
-        send_ref[0] = part
-
-    @pl.when(step >= count)
-    def _():
-        keep_ref[0] = part
+def project_kernel(core_ref, a_ref, w_ref, out_ref):
+    del core_ref
+    out_ref[0] = dot_nn(a_ref[...], w_ref[...]).astype(jnp.bfloat16)
 
 
 def project(core, attended, weight, out_width):
     rows, width = attended.shape
     count = weight.shape[1] // out_width // 2
-
-    def column(j, core):
-        parity = jnp.where(j < count, 1 - core[0], core[0])
-        return (0, (j % count) * 2 + parity)
-
-    shape = jax.ShapeDtypeStruct((count, rows, out_width), jnp.bfloat16)
-    return pl.pallas_call(
-        functools.partial(project_kernel, count=count),
+    return pl.pallas_call(
+        project_kernel,
         grid_spec=pltpu.PrefetchScalarGridSpec(
             num_scalar_prefetch=1,
-            grid=(2 * count,),
+            grid=(count,),
             in_specs=[
                 pl.BlockSpec((rows, width), lambda j, core: (0, 0)),
-                pl.BlockSpec((width, out_width), column),
+                pl.BlockSpec((width, out_width), lambda j, core: (0, j * 2 + core[0])),
             ],
-            out_specs=[
-                pl.BlockSpec((1, rows, out_width), lambda j, core: (jnp.minimum(j, count - 1), 0, 0)),
-                pl.BlockSpec((1, rows, out_width), lambda j, core: (jnp.maximum(j - count, 0), 0, 0)),
-            ],
+            out_specs=pl.BlockSpec((1, rows, out_width), lambda j, core: (j, 0, 0)),
         ),
-        out_shape=[shape, shape],
-        compiler_params=pltpu.CompilerParams(vmem_limit_bytes=8 * MIB),
+        out_shape=jax.ShapeDtypeStruct((count, rows, out_width), jnp.bfloat16),
+        compiler_params=pltpu.CompilerParams(vmem_limit_bytes=14 * MIB),
         cost_estimate=BRIEF,
     )(core, attended, weight)
 
@@ -624,15 +614,17 @@
     pieces = [packed[0]] + [
         lax.ppermute(packed[d], "adapter", in_block(d)) for d in range(1, block)
     ]
-    send, keep = project(core, attended, output_projection_weight, out_width)
+    send = project(1 - core, attended, output_projection_weight, out_width)
     chosen = choose(here, adapter_row, block * slots, steps, resident, holders)
     send, chosen = tie((send, chosen))
-    own, *away = pair_sums(chip_index, keep, lax.ppermute(send, "tensor", cores), 1)
+    come = lax.ppermute(send, "tensor", cores)
     pieces[0], shrink, moved = tie((pieces[0], shrink, own_expand))
     expand = lax.ppermute(moved, "adapter", far)
     codes = shrink_rows([own_shrink, shrink], pieces, per_adapter, rank)
     codes = codes + lax.ppermute(codes, "tensor", cores)
-    brief = codes.astype(jnp.bfloat16)
+    brief, attended = tie((codes.astype(jnp.bfloat16), attended))
+    keep = project(core, attended, output_projection_weight, out_width)
+    own, *away = pair_sums(chip_index, keep, come, 1)
     codes = [brief] + [lax.ppermute(brief, "tensor", over_chips(s)) for s in range(1, chips)]
     codes, away = tie((codes, away))
     came = send_over_chips(away, 1)

time: 92.3 us -> 89.8 us (0.973)
  waiting for transfers between devices: 33.9 us -> 28.1 us
  local copies, waits for them, and re-layouts: 7.33 us -> 9.13 us
    ppermute x1, waiting for transfers between devices: 15.3 us -> 6.41 us  [local(): expand = lax.ppermute(moved, 'adapter', far)]
    ppermute x3, waiting for transfers between devices: 1.45 us -> 5.89 us  [local(): lax.ppermute(packed[d], 'adapter', in_block(d))]
    ppermute x3, waiting for transfers between devices: 15.8 us -> 13.9 us  [local(): lax.ppermute(wide[d], 'adapter', in_block(block - d))]
    unnamed x18 -> x20, local copies, waits for them, and re-layouts: 7.33 us -> 9.13 us
    pallas_call x1, Pallas kernels: 20 us -> 21.1 us  [attend(): pl.pallas_call(functools.partial(attend_kernel, steps=steps, group=group,...]
    pallas_call x1 -> x2, Pallas kernels: 7.04 us -> 6.61 us  [project(): pl.pallas_call(project_kernel, grid_spec=pltpu.PrefetchScalarGridSpec(num...]
  transfers between devices with their start and end apart: 12 -> 12, of which waited for: 6 -> 6; matrix products, arithmetic and copies ran while one was open for 0% -> 0% of each run, Pallas kernels for 37% -> 39%
where the time goes in v2:
time: 89.8 us; the launch traced here: 89.4 us
  Pallas kernels  37.9 us (42%)
  waiting for transfers between devices  28.1 us (31%)
  starting transfers between devices  14.2 us (16%)
  local copies, waits for them, and re-layouts  9.13 us (10%)
    pallas_call x1, Pallas kernels, attend(): pl.pallas_call(functools.partial(attend_kernel, steps=steps, group=group,...  21.1 us
    ppermute x3, waiting for transfers between devices, local(): lax.ppermute(wide[d], 'adapter', in_block(block - d))  13.9 us
    unnamed x20, local copies, waits for them, and re-layouts  9.13 us
    pallas_call x2, Pallas kernels, project(): pl.pallas_call(project_kernel, grid_spec=pltpu.PrefetchScalarGridSpec(num...  6.61 us
    ppermute x1, waiting for transfers between devices, local(): expand = lax.ppermute(moved, 'adapter', far)  6.41 us
    ppermute x3, waiting for transfers between devices, local(): lax.ppermute(packed[d], 'adapter', in_block(d))  5.89 us
    ppermute x3, starting transfers between devices, local(): lax.ppermute(packed[d], 'adapter', in_block(d))  4.5 us
    ppermute x1, starting transfers between devices, local(): shrink = lax.ppermute(own_shrink, 'adapter', far)  4.04 us
  transfers between devices with their start and end apart: 12, of which 6 were waited for; matrix products, arithmetic and copies ran while one was open for 0% of the time, Pallas kernels for 39%

profile of v2, /device:TPU:0, one launch (start us, length us, event | category | flops | bytes accessed | tf_op | source)
XLA Modules:
  0.0 89.4 jit_solution(16101181909848127754)
XLA Ops:
  0.0 4.0 %collective-permute-start = (bf16[256,1024]{1,0:T(8,128)(2,1)}, bf16[256,1024]{1,0:T(8,128)(2,1)S(1)}, u32[]{:S(2)}, u32[]{:S(2)}) collective-permute-start(bf16[256,1024]{1,0:T(8,128)(2,1)} %bitcast.10), channel_id=1, source_target_pairs={{0,16},{4,20},{8,24},{12,28},{16,0},{20,4},{24,8},{28,12},{1,17},{... | collective-permute-start | bytes 1572872 | tf_op jit(solution)/shard_map/ppermute | solution.py:607
  4.0 0.0 copy-start.3
  4.0 1.0 %copy-done.3 = bf16[2,128,4,256]{3,2,1,0:T(4,128)(2,1)S(1)} copy-done((bf16[2,128,4,256]{3,2,1,0:T(4,128)(2,1)S(1)}, bf16[2,128,4,256]{3,2,1,0:T(4,128)(2,1)}, u32[]{:S(2)}) %copy-start.3) | copy-done | bytes 524312
  5.1 0.0 copy-start.8
  5.1 0.7 copy-done.8
  5.7 0.0 copy-start.9
  5.7 0.7 copy-done.9
  6.4 0.0 copy-start.2
  6.4 21.1 %shard_map.100.refs_0_.a_ref = bf16[512,1024]{1,0:T(8,128)(2,1)S(1)} custom-call(s32[1,128]{1,0:T(1,128)S(1)} %bitcast.14, s32[1,128]{1,0:T(1,128)S(1)} %bitcast.15, bf16[128,4,1024]{2,1,0:T(4,128)(2,1)} %q_hbm.1, bf16[2,2,2048,256]{3,2,1,0:T(8,128)(2,1)} %kv_hbm.1, bf16[2,128,32,256]{3,2,1,0:T(8,128)(2,1)} %suf_hbm.1, bf16[2,128,4,256]{3,2,1,0:T(4,128)(2,1)S(1)} %copy-done.3), custom_call_target="tpu_custom_call" | custom-call | flops 68719476736 | bytes 134217728 | tf_op jit(solution)/shard_map/pallas_call | solution.py:262
  27.5 0.0 copy-done.2
  27.5 2.2 %shard_map.101 = (bf16[160,1024]{1,0:T(8,128)(2,1)S(1)}, bf16[160,1024]{1,0:T(8,128)(2,1)}, bf16[160,1024]{1,0:T(8,128)(2,1)}, bf16[160,1024]{1,0:T(8,128)(2,1)}) custom-call(s32[1]{0:T(128)} %bitcast.3.here_ref, s32[1,128]{1,0:T(1,128)S(1)} %bitcast.8, bf16[512,1024]{1,0:T(8,128)(2,1)S(1)} %shard_map.100.refs_0_.a_ref), custom_call_target="tpu_custom_call" | custom-call | flops 1024 | bytes 1024 | tf_op jit(solution)/shard_map/pallas_call | solution.py:393
  29.7 0.0 copy-start.6
  29.7 1.5 %collective-permute-start.2 = (bf16[160,1024]{1,0:T(8,128)(2,1)}, bf16[160,1024]{1,0:T(8,128)(2,1)}, u32[]{:S(2)}, u32[]{:S(2)}) collective-permute-start(bf16[160,1024]{1,0:T(8,128)(2,1)} %get-tuple-element.34), channel_id=1, source_target_pairs={{0,4},{4,8},{8,12},{12,0},{16,20},{20,24},{24,28},{28,16},{1,5},{5... | collective-permute-start | bytes 983048 | tf_op jit(solution)/shard_map/ppermute | solution.py:615
  31.3 1.6 %collective-permute-start.3 = (bf16[160,1024]{1,0:T(8,128)(2,1)}, bf16[160,1024]{1,0:T(8,128)(2,1)}, u32[]{:S(2)}, u32[]{:S(2)}) collective-permute-start(bf16[160,1024]{1,0:T(8,128)(2,1)} %get-tuple-element.35), channel_id=1, source_target_pairs={{0,8},{4,12},{8,0},{12,4},{16,24},{20,28},{24,16},{28,20},{1,9},{5... | collective-permute-start | bytes 983048 | tf_op jit(solution)/shard_map/ppermute | solution.py:615
  32.8 1.4 %collective-permute-start.4 = (bf16[160,1024]{1,0:T(8,128)(2,1)}, bf16[160,1024]{1,0:T(8,128)(2,1)}, u32[]{:S(2)}, u32[]{:S(2)}) collective-permute-start(bf16[160,1024]{1,0:T(8,128)(2,1)} %get-tuple-element.36), channel_id=1, source_target_pairs={{0,12},{4,0},{8,4},{12,8},{16,28},{20,16},{24,20},{28,24},{1,13},{... | collective-permute-start | bytes 983048 | tf_op jit(solution)/shard_map/ppermute | solution.py:615
  34.3 0.6 shard_map.103.chosen_ref
  34.8 0.0 copy-done.6
  34.9 0.0 copy-start
  34.9 3.4 %copy-done = bf16[1024,4096]{1,0:T(8,128)(2,1)S(1)} copy-done((bf16[1024,4096]{1,0:T(8,128)(2,1)S(1)}, bf16[1024,4096]{1,0:T(8,128)(2,1)}, u32[]{:S(2)}) %copy-start) | copy-done | bytes 8388632
  38.2 0.0 copy-start.5
  38.2 0.0 copy-start.4
  38.2 0.0 copy-start.7
  38.2 3.8 %shard_map.102 = bf16[2,512,1024]{2,1,0:T(8,128)(2,1)} custom-call(s32[1]{0:T(128)S(6)} %sub.7.core_ref, bf16[512,1024]{1,0:T(8,128)(2,1)S(1)} %shard_map.100.refs_0_.a_ref, bf16[1024,4096]{1,0:T(8,128)(2,1)S(1)} %copy-done), custom_call_target="tpu_custom_call" | custom-call | flops 1024 | bytes 1024 | tf_op jit(solution)/shard_map/pallas_call | solution.py:291
  42.0 0.0 collective-permute-start.7
  42.0 0.0 collective-permute-done.refs_1_
  42.0 0.0 copy-done.5
  42.0 0.4 collective-permute-start.1
  42.5 0.0 collective-permute-done.2.refs_3_
  42.5 0.0 collective-permute-done.3.refs_4_
  42.5 5.9 %collective-permute-done.4.refs_5_ = bf16[160,1024]{1,0:T(8,128)(2,1)} collective-permute-done((bf16[160,1024]{1,0:T(8,128)(2,1)}, bf16[160,1024]{1,0:T(8,128)(2,1)}, u32[]{:S(2)}, u32[]{:S(2)}) %collective-permute-start.4) | collective-permute-done | bytes 327712 | tf_op jit(solution)/shard_map/ppermute | solution.py:615
  48.3 0.0 copy-done.4
  48.3 0.0 copy-done.7
  48.4 1.8 %shard_map.104 = f32[320,128]{1,0:T(8,128)S(1)} custom-call(bf16[256,1024]{1,0:T(8,128)(2,1)S(1)} %bitcast.11, bf16[256,1024]{1,0:T(8,128)(2,1)S(1)} %collective-permute-done.refs_1_, bf16[160,1024]{1,0:T(8,128)(2,1)S(1)} %copy-done.7, bf16[160,1024]{1,0:T(8,128)(2,1)} %collective-permute-done.2.refs_3_, bf16[160,1024]{1,0:T(8,128)(2,1)} %collective-permute-done.3.refs_4_, ...), custom_call_target="tpu_custom_call" | custom-call | flops 68719476736 | bytes 134217728 | tf_op jit(solution)/shard_map/pallas_call | solution.py:440
  50.1 0.1 collective-permute-start.5
  50.2 1.4 %collective-permute-done.5 = f32[320,128]{1,0:T(8,128)S(1)} collective-permute-done((f32[320,128]{1,0:T(8,128)S(1)}, f32[320,128]{1,0:T(8,128)S(1)}, u32[]{:S(2)}, u32[]{:S(2)}) %collective-permute-start.5) | collective-permute-done | bytes 163872 | tf_op jit(solution)/shard_map/ppermute | solution.py:624
  51.6 1.6 %collective-permute-start.6 = (bf16[320,128]{1,0:T(8,128)(2,1)S(1)}, bf16[320,128]{1,0:T(8,128)(2,1)S(1)}, u32[]{:S(2)}, u32[]{:S(2)}) collective-permute-start(bf16[320,128]{1,0:T(8,128)(2,1)S(1)} %add_convert_fusion.refs_2_), channel_id=1, source_target_pairs={{0,2},{1,3},{2,0},{3,1},{4,6},{5,7},{6,4},{7,5},{8,10},{9,11},{10,... | collective-permute-start | bytes 245768 | tf_op jit(solution)/shard_map/ppermute | solution.py:628
  53.2 0.0 copy-start.1
  53.2 3.4 %copy-done.1 = bf16[1024,4096]{1,0:T(8,128)(2,1)S(1)} copy-done((bf16[1024,4096]{1,0:T(8,128)(2,1)S(1)}, bf16[1024,4096]{1,0:T(8,128)(2,1)}, u32[]{:S(2)}) %copy-start.1) | copy-done | bytes 8388632
  56.6 2.8 %shard_map.105.keep_ref = bf16[2,512,1024]{2,1,0:T(8,128)(2,1)S(1)} custom-call(s32[1]{0:T(128)} %bitcast.core_ref, bf16[512,1024]{1,0:T(8,128)(2,1)S(1)} %shard_map.100.refs_0_.a_ref, bf16[1024,4096]{1,0:T(8,128)(2,1)S(1)} %copy-done.1), custom_call_target="tpu_custom_call" | custom-call | flops 1024 | bytes 1024 | tf_op jit(solution)/shard_map/pallas_call | solution.py:291
  59.4 0.0 collective-permute-done.7.come_ref
  59.4 2.1 %shard_map.106 = (bf16[512,1024]{1,0:T(8,128)(2,1)S(1)}, bf16[512,1024]{1,0:T(8,128)(2,1)S(1)}) custom-call(s32[1]{0:T(128)} %bitcast.7.chip_ref, bf16[2,512,1024]{2,1,0:T(8,128)(2,1)S(1)} %shard_map.105.keep_ref, bf16[2,512,1024]{2,1,0:T(8,128)(2,1)} %collective-permute-done.7.come_ref), custom_call_target="tpu_custom_call" | custom-call | flops 1024 | bytes 1024 | tf_op jit(solution)/shard_map/pallas_call | solution.py:326
  61.5 0.0 collective-permute-done.6.refs_3_
  61.5 0.6 collective-permute-start.11
  62.1 6.4 %collective-permute-done.1.refs_1_ = bf16[256,1024]{1,0:T(8,128)(2,1)S(1)} collective-permute-done((bf16[256,1024]{1,0:T(8,128)(2,1)S(1)}, bf16[256,1024]{1,0:T(8,128)(2,1)S(1)}, u32[]{:S(2)}, u32[]{:S(2)}) %collective-permute-start.1) | collective-permute-done | bytes 524320 | tf_op jit(solution)/shard_map/ppermute | solution.py:622
  68.5 0.6 shard_map.107
  69.0 0.7 collective-permute-start.10
  69.7 2.3 %collective-permute-start.8 = (bf16[160,1024]{1,0:T(8,128)(2,1)S(1)}, bf16[160,1024]{1,0:T(8,128)(2,1)S(1)}, u32[]{:S(2)}, u32[]{:S(2)}) collective-permute-start(bf16[160,1024]{1,0:T(8,128)(2,1)S(1)} %get-tuple-element.44), channel_id=1, source_target_pairs={{0,12},{4,0},{8,4},{12,8},{16,28},{20,16},{24,20},{28,24},{1,13},{... | collective-permute-start | bytes 983048 | tf_op jit(solution)/shard_map/ppermute | solution.py:633
  72.0 0.0 collective-permute-start.9
  72.0 11.7 %collective-permute-done.10.refs_3_ = bf16[160,1024]{1,0:T(8,128)(2,1)S(1)} collective-permute-done((bf16[160,1024]{1,0:T(8,128)(2,1)S(1)}, bf16[160,1024]{1,0:T(8,128)(2,1)S(1)}, u32[]{:S(2)}, u32[]{:S(2)}) %collective-permute-start.10) | collective-permute-done | bytes 327712 | tf_op jit(solution)/shard_map/ppermute | solution.py:633
  83.7 2.2 %collective-permute-done.8.refs_1_ = bf16[160,1024]{1,0:T(8,128)(2,1)S(1)} collective-permute-done((bf16[160,1024]{1,0:T(8,128)(2,1)S(1)}, bf16[160,1024]{1,0:T(8,128)(2,1)S(1)}, u32[]{:S(2)}, u32[]{:S(2)}) %collective-permute-start.8) | collective-permute-done | bytes 327712 | tf_op jit(solution)/shard_map/ppermute | solution.py:633
  85.9 0.0 collective-permute-done.9.refs_2_
  85.9 0.5 collective-permute-done.11.refs_5_
  86.5 3.0 %shard_map.108 = bf16[128,4,1024]{2,1,0:T(4,128)(2,1)} custom-call(bf16[512,640]{1,0:T(8,128)(2,1)S(1)} %shard_map.103.chosen_ref, bf16[160,1024]{1,0:T(8,128)(2,1)S(1)} %get-tuple-element.43.refs_0_, bf16[160,1024]{1,0:T(8,128)(2,1)S(1)} %collective-permute-done.8.refs_1_, bf16[160,1024]{1,0:T(8,128)(2,1)S(1)} %collective-permute-done.9.refs_2_, ...), custom_call_target="tpu_custom_call" | custom-call | flops 1024 | bytes 1024 | tf_op jit(solution)/shard_map/pallas_call | solution.py:543
  (1 shorter events, 0.0 us)
Async XLA Ops:
  0.0 42.0 %collective-permute-start = (bf16[256,1024]{1,0:T(8,128)(2,1)}, bf16[256,1024]{1,0:T(8,128)(2,1)S(1)}, u32[]{:S(2)}, u32[]{:S(2)}) collective-permute-start(bf16[256,1024]{1,0:T(8,128)(2,1)} %bitcast.10), channel_id=1, source_target_pairs={{0,16},{4,20},{8,24},{12,28},{16,0},{20,4},{24,8},{28,12},{1,17},{... | collective-permute-start | bytes 1572872 | tf_op jit(solution)/shard_map/ppermute | solution.py:607
  4.0 1.0 %copy-start.3 = (bf16[2,128,4,256]{3,2,1,0:T(4,128)(2,1)S(1)}, bf16[2,128,4,256]{3,2,1,0:T(4,128)(2,1)}, u32[]{:S(2)}) copy-start(bf16[2,128,4,256]{3,2,1,0:T(4,128)(2,1)} %fr_hbm.1) | copy-start | bytes 1572868
  5.1 0.7 copy-start.8
  5.7 0.7 copy-start.9
  6.4 21.1 %copy-start.2 = (s32[128,1]{0,1:T(1,128)S(1)}, s32[128,1]{0,1:T(1,128)}, u32[]{:S(2)}) copy-start(s32[128,1]{0,1:T(1,128)} %param.16) | copy-start | bytes 1540
  29.7 5.1 %copy-start.6 = (bf16[160,1024]{1,0:T(8,128)(2,1)}, bf16[160,1024]{1,0:T(8,128)(2,1)S(1)}, u32[]{:S(2)}) copy-start(bf16[160,1024]{1,0:T(8,128)(2,1)S(1)} %get-tuple-element.33.refs_2_) | copy-start | bytes 983044
  29.7 12.7 %collective-permute-start.2 = (bf16[160,1024]{1,0:T(8,128)(2,1)}, bf16[160,1024]{1,0:T(8,128)(2,1)}, u32[]{:S(2)}, u32[]{:S(2)}) collective-permute-start(bf16[160,1024]{1,0:T(8,128)(2,1)} %get-tuple-element.34), channel_id=1, source_target_pairs={{0,4},{4,8},{8,12},{12,0},{16,20},{20,24},{24,28},{28,16},{1,5},{5... | collective-permute-start | bytes 983048 | tf_op jit(solution)/shard_map/ppermute | solution.py:615
  31.3 11.2 %collective-permute-start.3 = (bf16[160,1024]{1,0:T(8,128)(2,1)}, bf16[160,1024]{1,0:T(8,128)(2,1)}, u32[]{:S(2)}, u32[]{:S(2)}) collective-permute-start(bf16[160,1024]{1,0:T(8,128)(2,1)} %get-tuple-element.35), channel_id=1, source_target_pairs={{0,8},{4,12},{8,0},{12,4},{16,24},{20,28},{24,16},{28,20},{1,9},{5... | collective-permute-start | bytes 983048 | tf_op jit(solution)/shard_map/ppermute | solution.py:615
  32.8 15.5 %collective-permute-start.4 = (bf16[160,1024]{1,0:T(8,128)(2,1)}, bf16[160,1024]{1,0:T(8,128)(2,1)}, u32[]{:S(2)}, u32[]{:S(2)}) collective-permute-start(bf16[160,1024]{1,0:T(8,128)(2,1)} %get-tuple-element.36), channel_id=1, source_target_pairs={{0,12},{4,0},{8,4},{12,8},{16,28},{20,16},{24,20},{28,24},{1,13},{... | collective-permute-start | bytes 983048 | tf_op jit(solution)/shard_map/ppermute | solution.py:615
  34.9 3.4 %copy-start = (bf16[1024,4096]{1,0:T(8,128)(2,1)S(1)}, bf16[1024,4096]{1,0:T(8,128)(2,1)}, u32[]{:S(2)}) copy-start(bf16[1024,4096]{1,0:T(8,128)(2,1)} %w_ref.3) | copy-start | bytes 25165828
  38.2 3.8 %copy-start.5 = (bf16[4,64,1024]{2,1,0:T(8,128)(2,1)S(1)}, bf16[4,64,1024]{2,1,0:T(8,128)(2,1)}, u32[]{:S(2)}) copy-start(bf16[4,64,1024]{2,1,0:T(8,128)(2,1)} %param.19) | copy-start | bytes 1572868
  38.2 10.1 %copy-start.4 = (bf16[4,64,1024]{2,1,0:T(8,128)(2,1)S(1)}, bf16[4,64,1024]{2,1,0:T(8,128)(2,1)}, u32[]{:S(2)}) copy-start(bf16[4,64,1024]{2,1,0:T(8,128)(2,1)} %param.18) | copy-start | bytes 1572868
  38.2 10.1 %copy-start.7 = (bf16[160,1024]{1,0:T(8,128)(2,1)S(1)}, bf16[160,1024]{1,0:T(8,128)(2,1)}, u32[]{:S(2)}) copy-start(bf16[160,1024]{1,0:T(8,128)(2,1)} %copy-done.6) | copy-start | bytes 983044
  42.0 17.4 %collective-permute-start.7 = (bf16[2,512,1024]{2,1,0:T(8,128)(2,1)}, bf16[2,512,1024]{2,1,0:T(8,128)(2,1)}, u32[]{:S(2)}, u32[]{:S(2)}) collective-permute-start(bf16[2,512,1024]{2,1,0:T(8,128)(2,1)} %shard_map.102), channel_id=1, source_target_pairs={{0,1},{1,0},{2,3},{3,2},{4,5},{5,4},{6,7},{7,6},{8,9},{9,8},{10,11... | collective-permute-start | bytes 6291464 | tf_op jit(solution)/shard_map/ppermute | solution.py:620
  42.0 26.4 %collective-permute-start.1 = (bf16[256,1024]{1,0:T(8,128)(2,1)S(1)}, bf16[256,1024]{1,0:T(8,128)(2,1)S(1)}, u32[]{:S(2)}, u32[]{:S(2)}) collective-permute-start(bf16[256,1024]{1,0:T(8,128)(2,1)S(1)} %bitcast.12), channel_id=1, source_target_pairs={{0,16},{4,20},{8,24},{12,28},{16,0},{20,4},{24,8},{28,12},{1,17},{... | collective-permute-start | bytes 1572872 | tf_op jit(solution)/shard_map/ppermute | solution.py:622
  50.1 1.5 %collective-permute-start.5 = (f32[320,128]{1,0:T(8,128)S(1)}, f32[320,128]{1,0:T(8,128)S(1)}, u32[]{:S(2)}, u32[]{:S(2)}) collective-permute-start(f32[320,128]{1,0:T(8,128)S(1)} %shard_map.104), channel_id=1, source_target_pairs={{0,1},{1,0},{2,3},{3,2},{4,5},{5,4},{6,7},{7,6},{8,9},{9,8},{10,11... | collective-permute-start | bytes 491528 | tf_op jit(solution)/shard_map/ppermute | solution.py:624
  51.6 9.9 %collective-permute-start.6 = (bf16[320,128]{1,0:T(8,128)(2,1)S(1)}, bf16[320,128]{1,0:T(8,128)(2,1)S(1)}, u32[]{:S(2)}, u32[]{:S(2)}) collective-permute-start(bf16[320,128]{1,0:T(8,128)(2,1)S(1)} %add_convert_fusion.refs_2_), channel_id=1, source_target_pairs={{0,2},{1,3},{2,0},{3,1},{4,6},{5,7},{6,4},{7,5},{8,10},{9,11},{10,... | collective-permute-start | bytes 245768 | tf_op jit(solution)/shard_map/ppermute | solution.py:628
  53.2 3.4 %copy-start.1 = (bf16[1024,4096]{1,0:T(8,128)(2,1)S(1)}, bf16[1024,4096]{1,0:T(8,128)(2,1)}, u32[]{:S(2)}) copy-start(bf16[1024,4096]{1,0:T(8,128)(2,1)} %w_ref.3) | copy-start | bytes 25165828
  61.5 25.0 %collective-permute-start.11 = (bf16[512,1024]{1,0:T(8,128)(2,1)S(1)}, bf16[512,1024]{1,0:T(8,128)(2,1)S(1)}, u32[]{:S(2)}, u32[]{:S(2)}) collective-permute-start(bf16[512,1024]{1,0:T(8,128)(2,1)S(1)} %get-tuple-element.48), channel_id=1, source_target_pairs={{0,2},{1,3},{2,0},{3,1},{4,6},{5,7},{6,4},{7,5},{8,10},{9,11},{10,... | collective-permute-start | bytes 3145736 | tf_op jit(solution)/shard_map/ppermute | solution.py:600
  69.0 14.7 %collective-permute-start.10 = (bf16[160,1024]{1,0:T(8,128)(2,1)S(1)}, bf16[160,1024]{1,0:T(8,128)(2,1)S(1)}, u32[]{:S(2)}, u32[]{:S(2)}) collective-permute-start(bf16[160,1024]{1,0:T(8,128)(2,1)S(1)} %get-tuple-element.46), channel_id=1, source_target_pairs={{0,4},{4,8},{8,12},{12,0},{16,20},{20,24},{24,28},{28,16},{1,5},{5... | collective-permute-start | bytes 983048 | tf_op jit(solution)/shard_map/ppermute | solution.py:633
  69.7 16.2 %collective-permute-start.8 = (bf16[160,1024]{1,0:T(8,128)(2,1)S(1)}, bf16[160,1024]{1,0:T(8,128)(2,1)S(1)}, u32[]{:S(2)}, u32[]{:S(2)}) collective-permute-start(bf16[160,1024]{1,0:T(8,128)(2,1)S(1)} %get-tuple-element.44), channel_id=1, source_target_pairs={{0,12},{4,0},{8,4},{12,8},{16,28},{20,16},{24,20},{28,24},{1,13},{... | collective-permute-start | bytes 983048 | tf_op jit(solution)/shard_map/ppermute | solution.py:633
  72.0 13.9 %collective-permute-start.9 = (bf16[160,1024]{1,0:T(8,128)(2,1)S(1)}, bf16[160,1024]{1,0:T(8,128)(2,1)S(1)}, u32[]{:S(2)}, u32[]{:S(2)}) collective-permute-start(bf16[160,1024]{1,0:T(8,128)(2,1)S(1)} %get-tuple-element.45), channel_id=1, source_target_pairs={{0,8},{4,12},{8,0},{12,4},{16,24},{20,28},{24,16},{28,20},{1,9},{5... | collective-permute-start | bytes 983048 | tf_op jit(solution)/shard_map/ppermute | solution.py:633

commit v3 on v2

--- a/solution.py
+++ b/solution.py
@@ -74,7 +74,7 @@
             [(q_hbm, q_ref), (fr_hbm, fr_ref), (length_hbm, length_ref), (prefix_hbm, prefix_ref)]
         )
     ]
-    for load in [*reversed(small), *loads[:2]]:
+    for load in [*reversed(small), *loads]:
         load.start()
 
     def tile_rows(x):
@@ -225,30 +225,23 @@
 
     for load in [*reversed(small), *loads[:2]]:
         load.wait()
-    for load in loads[2:]:
-        load.start()
     run(scores(first, 0, 0))
     for load in loads[2:]:
         load.wait()
 
-    def step(block, ends):
+    def body(block, carry):
         for h in range(key_heads):
             if h + 1 < key_heads:
                 run(scores(block, h + 1, h + 1), outputs(block, h, h))
-            elif ends:
-                run(outputs(block, h, h))
             elif key_heads > 1:
-                run(scores(block + 1, 0, 0), outputs(block, h, h))
+                following = jnp.minimum(block + 1, last)
+                run(scores(following, 0, 0), outputs(block, h, h))
             else:
                 run(outputs(block, h, h))
-                run(scores(block + 1, 0, 0))
-
-    def body(block, carry):
-        step(block, False)
+                run(scores(jnp.minimum(block + 1, last), 0, 0))
         return carry
 
-    lax.fori_loop(first, last, body, 0)
-    step(last, True)
+    lax.fori_loop(first, first + blocks, body, 0)
 
 
 def attend(lengths, prefixes, queries, prefix, suffix, fresh, steps, first, blocks):
@@ -275,7 +268,7 @@
             pltpu.VMEM(fresh.shape, fresh.dtype),
             pltpu.SemaphoreType.DMA((8,)),
         ],
-        compiler_params=pltpu.CompilerParams(vmem_limit_bytes=52 * MIB),
+        compiler_params=pltpu.CompilerParams(vmem_limit_bytes=44 * MIB),
         cost_estimate=LENGTHY,
     )(lengths, prefixes, queries, prefix, suffix, fresh)
 

time: 89.8 us -> 91.3 us (1.017)
  local copies, waits for them, and re-layouts: 9.13 us -> 12.5 us
  Pallas kernels: 37.9 us -> 35.9 us
    unnamed x20 -> x24, local copies, waits for them, and re-layouts: 9.13 us -> 12.5 us
    pallas_call x1, Pallas kernels: 21.1 us -> 19.1 us  [attend(): pl.pallas_call(functools.partial(attend_kernel, steps=steps, group=group,...]
  transfers between devices with their start and end apart: 12 -> 12, of which waited for: 6 -> 6; matrix products, arithmetic and copies ran while one was open for 0% -> 0% of each run, Pallas kernels for 39% -> 36%
where the time goes in v3:
time: 91.3 us; the launch traced here: 90.9 us
  Pallas kernels  35.9 us (39%)
  waiting for transfers between devices  28.2 us (31%)
  starting transfers between devices  14.1 us (15%)
  local copies, waits for them, and re-layouts  12.5 us (14%)
    pallas_call x1, Pallas kernels, attend(): pl.pallas_call(functools.partial(attend_kernel, steps=steps, group=group,...  19.1 us
    ppermute x3, waiting for transfers between devices, local(): lax.ppermute(wide[d], 'adapter', in_block(block - d))  13.9 us
    unnamed x24, local copies, waits for them, and re-layouts  12.5 us
    pallas_call x2, Pallas kernels, project(): pl.pallas_call(project_kernel, grid_spec=pltpu.PrefetchScalarGridSpec(num...  6.61 us
    ppermute x1, waiting for transfers between devices, local(): expand = lax.ppermute(moved, 'adapter', far)  6.4 us
    ppermute x3, waiting for transfers between devices, local(): lax.ppermute(packed[d], 'adapter', in_block(d))  5.92 us
    ppermute x3, starting transfers between devices, local(): lax.ppermute(packed[d], 'adapter', in_block(d))  4.5 us
    ppermute x1, starting transfers between devices, local(): shrink = lax.ppermute(own_shrink, 'adapter', far)  4.04 us
  transfers between devices with their start and end apart: 12, of which 6 were waited for; matrix products, arithmetic and copies ran while one was open for 0% of the time, Pallas kernels for 36%

profile of v3, /device:TPU:0, one launch (start us, length us, event | category | flops | bytes accessed | tf_op | source)
XLA Modules:
  0.0 90.9 jit_solution(12759069915139982433)
XLA Ops:
  0.0 4.0 %collective-permute-start = (bf16[256,1024]{1,0:T(8,128)(2,1)}, bf16[256,1024]{1,0:T(8,128)(2,1)S(1)}, u32[]{:S(2)}, u32[]{:S(2)}) collective-permute-start(bf16[256,1024]{1,0:T(8,128)(2,1)} %bitcast.10), channel_id=1, source_target_pairs={{0,16},{4,20},{8,24},{12,28},{16,0},{20,4},{24,8},{28,12},{1,17},{... | collective-permute-start | bytes 1572872 | tf_op jit(solution)/shard_map/ppermute | solution.py:600
  4.0 0.0 copy-start.3
  4.0 2.2 %copy-done.3 = bf16[2,2,2048,256]{3,2,1,0:T(8,128)(2,1)S(1)} copy-done((bf16[2,2,2048,256]{3,2,1,0:T(8,128)(2,1)S(1)}, bf16[2,2,2048,256]{3,2,1,0:T(8,128)(2,1)}, u32[]{:S(2)}) %copy-start.3) | copy-done | bytes 4194328
  6.2 0.0 copy-start.4
  6.2 1.2 %copy-done.4 = bf16[128,4,1024]{2,1,0:T(4,128)(2,1)S(1)} copy-done((bf16[128,4,1024]{2,1,0:T(4,128)(2,1)S(1)}, bf16[128,4,1024]{2,1,0:T(4,128)(2,1)}, u32[]{:S(2)}) %copy-start.4) | copy-done | bytes 1048600
  7.5 0.0 copy-start.5
  7.5 1.0 %copy-done.5 = bf16[2,128,4,256]{3,2,1,0:T(4,128)(2,1)S(1)} copy-done((bf16[2,128,4,256]{3,2,1,0:T(4,128)(2,1)S(1)}, bf16[2,128,4,256]{3,2,1,0:T(4,128)(2,1)}, u32[]{:S(2)}) %copy-start.5) | copy-done | bytes 524312
  8.5 0.0 copy-start.10
  8.5 0.7 copy-done.10
  9.1 0.0 copy-start.11
  9.2 0.7 copy-done.11
  9.8 0.0 copy-start.2
  9.8 19.1 %shard_map.100.refs_0_.a_ref = bf16[512,1024]{1,0:T(8,128)(2,1)S(1)} custom-call(s32[1,128]{1,0:T(1,128)S(1)} %bitcast.14, s32[1,128]{1,0:T(1,128)S(1)} %bitcast.15, bf16[128,4,1024]{2,1,0:T(4,128)(2,1)S(1)} %copy-done.4, bf16[2,2,2048,256]{3,2,1,0:T(8,128)(2,1)S(1)} %copy-done.3, bf16[2,128,32,256]{3,2,1,0:T(8,128)(2,1)} %suf_hbm.1, ...), custom_call_target="tpu_custom_call" | custom-call | flops 68719476736 | bytes 134217728 | tf_op jit(solution)/shard_map/pallas_call | solution.py:255
  29.0 0.0 copy-done.2
  29.0 2.2 %shard_map.101 = (bf16[160,1024]{1,0:T(8,128)(2,1)S(1)}, bf16[160,1024]{1,0:T(8,128)(2,1)}, bf16[160,1024]{1,0:T(8,128)(2,1)}, bf16[160,1024]{1,0:T(8,128)(2,1)}) custom-call(s32[1]{0:T(128)} %bitcast.3.here_ref, s32[1,128]{1,0:T(1,128)S(1)} %bitcast.8, bf16[512,1024]{1,0:T(8,128)(2,1)S(1)} %shard_map.100.refs_0_.a_ref), custom_call_target="tpu_custom_call" | custom-call | flops 1024 | bytes 1024 | tf_op jit(solution)/shard_map/pallas_call | solution.py:386
  31.2 0.0 copy-start.8
  31.2 1.5 %collective-permute-start.2 = (bf16[160,1024]{1,0:T(8,128)(2,1)}, bf16[160,1024]{1,0:T(8,128)(2,1)}, u32[]{:S(2)}, u32[]{:S(2)}) collective-permute-start(bf16[160,1024]{1,0:T(8,128)(2,1)} %get-tuple-element.34), channel_id=1, source_target_pairs={{0,4},{4,8},{8,12},{12,0},{16,20},{20,24},{24,28},{28,16},{1,5},{5... | collective-permute-start | bytes 983048 | tf_op jit(solution)/shard_map/ppermute | solution.py:608
  32.7 1.6 %collective-permute-start.3 = (bf16[160,1024]{1,0:T(8,128)(2,1)}, bf16[160,1024]{1,0:T(8,128)(2,1)}, u32[]{:S(2)}, u32[]{:S(2)}) collective-permute-start(bf16[160,1024]{1,0:T(8,128)(2,1)} %get-tuple-element.35), channel_id=1, source_target_pairs={{0,8},{4,12},{8,0},{12,4},{16,24},{20,28},{24,16},{28,20},{1,9},{5... | collective-permute-start | bytes 983048 | tf_op jit(solution)/shard_map/ppermute | solution.py:608
  34.3 1.4 %collective-permute-start.4 = (bf16[160,1024]{1,0:T(8,128)(2,1)}, bf16[160,1024]{1,0:T(8,128)(2,1)}, u32[]{:S(2)}, u32[]{:S(2)}) collective-permute-start(bf16[160,1024]{1,0:T(8,128)(2,1)} %get-tuple-element.36), channel_id=1, source_target_pairs={{0,12},{4,0},{8,4},{12,8},{16,28},{20,16},{24,20},{28,24},{1,13},{... | collective-permute-start | bytes 983048 | tf_op jit(solution)/shard_map/ppermute | solution.py:608
  35.7 0.6 shard_map.103.chosen_ref
  36.3 0.0 copy-done.8
  36.3 0.0 copy-start
  36.3 3.4 %copy-done = bf16[1024,4096]{1,0:T(8,128)(2,1)S(1)} copy-done((bf16[1024,4096]{1,0:T(8,128)(2,1)S(1)}, bf16[1024,4096]{1,0:T(8,128)(2,1)}, u32[]{:S(2)}) %copy-start) | copy-done | bytes 8388632
  39.7 0.0 copy-start.7
  39.7 0.0 copy-start.6
  39.7 0.0 copy-start.9
  39.7 3.8 %shard_map.102 = bf16[2,512,1024]{2,1,0:T(8,128)(2,1)} custom-call(s32[1]{0:T(128)S(6)} %sub.7.core_ref, bf16[512,1024]{1,0:T(8,128)(2,1)S(1)} %shard_map.100.refs_0_.a_ref, bf16[1024,4096]{1,0:T(8,128)(2,1)S(1)} %copy-done), custom_call_target="tpu_custom_call" | custom-call | flops 1024 | bytes 1024 | tf_op jit(solution)/shard_map/pallas_call | solution.py:284
  43.5 0.0 collective-permute-start.7
  43.5 0.0 collective-permute-done.refs_1_
  43.5 0.0 copy-done.7
  43.5 0.4 collective-permute-start.1
  43.9 0.0 collective-permute-done.2.refs_3_
  43.9 0.0 collective-permute-done.3.refs_4_
  43.9 5.9 %collective-permute-done.4.refs_5_ = bf16[160,1024]{1,0:T(8,128)(2,1)} collective-permute-done((bf16[160,1024]{1,0:T(8,128)(2,1)}, bf16[160,1024]{1,0:T(8,128)(2,1)}, u32[]{:S(2)}, u32[]{:S(2)}) %collective-permute-start.4) | collective-permute-done | bytes 327712 | tf_op jit(solution)/shard_map/ppermute | solution.py:608
  49.8 0.0 copy-done.6
  49.8 0.0 copy-done.9
  49.8 1.8 %shard_map.104 = f32[320,128]{1,0:T(8,128)S(1)} custom-call(bf16[256,1024]{1,0:T(8,128)(2,1)S(1)} %bitcast.11, bf16[256,1024]{1,0:T(8,128)(2,1)S(1)} %collective-permute-done.refs_1_, bf16[160,1024]{1,0:T(8,128)(2,1)S(1)} %copy-done.9, bf16[160,1024]{1,0:T(8,128)(2,1)} %collective-permute-done.2.refs_3_, bf16[160,1024]{1,0:T(8,128)(2,1)} %collective-permute-done.3.refs_4_, ...), custom_call_target="tpu_custom_call" | custom-call | flops 68719476736 | bytes 134217728 | tf_op jit(solution)/shard_map/pallas_call | solution.py:433
  51.6 0.1 collective-permute-start.5
  51.7 1.4 %collective-permute-done.5 = f32[320,128]{1,0:T(8,128)S(1)} collective-permute-done((f32[320,128]{1,0:T(8,128)S(1)}, f32[320,128]{1,0:T(8,128)S(1)}, u32[]{:S(2)}, u32[]{:S(2)}) %collective-permute-start.5) | collective-permute-done | bytes 163872 | tf_op jit(solution)/shard_map/ppermute | solution.py:617
  53.1 1.6 %collective-permute-start.6 = (bf16[320,128]{1,0:T(8,128)(2,1)S(1)}, bf16[320,128]{1,0:T(8,128)(2,1)S(1)}, u32[]{:S(2)}, u32[]{:S(2)}) collective-permute-start(bf16[320,128]{1,0:T(8,128)(2,1)S(1)} %add_convert_fusion.refs_2_), channel_id=1, source_target_pairs={{0,2},{1,3},{2,0},{3,1},{4,6},{5,7},{6,4},{7,5},{8,10},{9,11},{10,... | collective-permute-start | bytes 245768 | tf_op jit(solution)/shard_map/ppermute | solution.py:621
  54.6 0.0 copy-start.1
  54.6 3.4 %copy-done.1 = bf16[1024,4096]{1,0:T(8,128)(2,1)S(1)} copy-done((bf16[1024,4096]{1,0:T(8,128)(2,1)S(1)}, bf16[1024,4096]{1,0:T(8,128)(2,1)}, u32[]{:S(2)}) %copy-start.1) | copy-done | bytes 8388632
  58.0 2.8 %shard_map.105.keep_ref = bf16[2,512,1024]{2,1,0:T(8,128)(2,1)S(1)} custom-call(s32[1]{0:T(128)} %bitcast.core_ref, bf16[512,1024]{1,0:T(8,128)(2,1)S(1)} %shard_map.100.refs_0_.a_ref, bf16[1024,4096]{1,0:T(8,128)(2,1)S(1)} %copy-done.1), custom_call_target="tpu_custom_call" | custom-call | flops 1024 | bytes 1024 | tf_op jit(solution)/shard_map/pallas_call | solution.py:284
  60.8 0.0 collective-permute-done.7.come_ref
  60.9 2.1 %shard_map.106 = (bf16[512,1024]{1,0:T(8,128)(2,1)S(1)}, bf16[512,1024]{1,0:T(8,128)(2,1)S(1)}) custom-call(s32[1]{0:T(128)} %bitcast.7.chip_ref, bf16[2,512,1024]{2,1,0:T(8,128)(2,1)S(1)} %shard_map.105.keep_ref, bf16[2,512,1024]{2,1,0:T(8,128)(2,1)} %collective-permute-done.7.come_ref), custom_call_target="tpu_custom_call" | custom-call | flops 1024 | bytes 1024 | tf_op jit(solution)/shard_map/pallas_call | solution.py:319
  62.9 0.0 collective-permute-done.6.refs_3_
  62.9 0.6 collective-permute-start.11
  63.5 6.4 %collective-permute-done.1.refs_1_ = bf16[256,1024]{1,0:T(8,128)(2,1)S(1)} collective-permute-done((bf16[256,1024]{1,0:T(8,128)(2,1)S(1)}, bf16[256,1024]{1,0:T(8,128)(2,1)S(1)}, u32[]{:S(2)}, u32[]{:S(2)}) %collective-permute-start.1) | collective-permute-done | bytes 524320 | tf_op jit(solution)/shard_map/ppermute | solution.py:615
  69.9 0.6 shard_map.107
  70.5 0.7 collective-permute-start.10
  71.2 2.3 %collective-permute-start.8 = (bf16[160,1024]{1,0:T(8,128)(2,1)S(1)}, bf16[160,1024]{1,0:T(8,128)(2,1)S(1)}, u32[]{:S(2)}, u32[]{:S(2)}) collective-permute-start(bf16[160,1024]{1,0:T(8,128)(2,1)S(1)} %get-tuple-element.44), channel_id=1, source_target_pairs={{0,12},{4,0},{8,4},{12,8},{16,28},{20,16},{24,20},{28,24},{1,13},{... | collective-permute-start | bytes 983048 | tf_op jit(solution)/shard_map/ppermute | solution.py:626
  73.5 0.0 collective-permute-start.9
  73.5 11.7 %collective-permute-done.10.refs_3_ = bf16[160,1024]{1,0:T(8,128)(2,1)S(1)} collective-permute-done((bf16[160,1024]{1,0:T(8,128)(2,1)S(1)}, bf16[160,1024]{1,0:T(8,128)(2,1)S(1)}, u32[]{:S(2)}, u32[]{:S(2)}) %collective-permute-start.10) | collective-permute-done | bytes 327712 | tf_op jit(solution)/shard_map/ppermute | solution.py:626
  85.2 2.2 %collective-permute-done.8.refs_1_ = bf16[160,1024]{1,0:T(8,128)(2,1)S(1)} collective-permute-done((bf16[160,1024]{1,0:T(8,128)(2,1)S(1)}, bf16[160,1024]{1,0:T(8,128)(2,1)S(1)}, u32[]{:S(2)}, u32[]{:S(2)}) %collective-permute-start.8) | collective-permute-done | bytes 327712 | tf_op jit(solution)/shard_map/ppermute | solution.py:626
  87.4 0.0 collective-permute-done.9.refs_2_
  87.4 0.6 collective-permute-done.11.refs_5_
  87.9 3.0 %shard_map.108 = bf16[128,4,1024]{2,1,0:T(4,128)(2,1)} custom-call(bf16[512,640]{1,0:T(8,128)(2,1)S(1)} %shard_map.103.chosen_ref, bf16[160,1024]{1,0:T(8,128)(2,1)S(1)} %get-tuple-element.43.refs_0_, bf16[160,1024]{1,0:T(8,128)(2,1)S(1)} %collective-permute-done.8.refs_1_, bf16[160,1024]{1,0:T(8,128)(2,1)S(1)} %collective-permute-done.9.refs_2_, ...), custom_call_target="tpu_custom_call" | custom-call | flops 1024 | bytes 1024 | tf_op jit(solution)/shard_map/pallas_call | solution.py:536
  (1 shorter events, 0.0 us)
Async XLA Ops:
  0.0 43.5 %collective-permute-start = (bf16[256,1024]{1,0:T(8,128)(2,1)}, bf16[256,1024]{1,0:T(8,128)(2,1)S(1)}, u32[]{:S(2)}, u32[]{:S(2)}) collective-permute-start(bf16[256,1024]{1,0:T(8,128)(2,1)} %bitcast.10), channel_id=1, source_target_pairs={{0,16},{4,20},{8,24},{12,28},{16,0},{20,4},{24,8},{28,12},{1,17},{... | collective-permute-start | bytes 1572872 | tf_op jit(solution)/shard_map/ppermute | solution.py:600
  4.0 2.2 %copy-start.3 = (bf16[2,2,2048,256]{3,2,1,0:T(8,128)(2,1)S(1)}, bf16[2,2,2048,256]{3,2,1,0:T(8,128)(2,1)}, u32[]{:S(2)}) copy-start(bf16[2,2,2048,256]{3,2,1,0:T(8,128)(2,1)} %kv_hbm.1) | copy-start | bytes 12582916
  6.2 1.2 %copy-start.4 = (bf16[128,4,1024]{2,1,0:T(4,128)(2,1)S(1)}, bf16[128,4,1024]{2,1,0:T(4,128)(2,1)}, u32[]{:S(2)}) copy-start(bf16[128,4,1024]{2,1,0:T(4,128)(2,1)} %q_hbm.1) | copy-start | bytes 3145732
  7.5 1.0 %copy-start.5 = (bf16[2,128,4,256]{3,2,1,0:T(4,128)(2,1)S(1)}, bf16[2,128,4,256]{3,2,1,0:T(4,128)(2,1)}, u32[]{:S(2)}) copy-start(bf16[2,128,4,256]{3,2,1,0:T(4,128)(2,1)} %fr_hbm.1) | copy-start | bytes 1572868
  8.5 0.7 copy-start.10
  9.1 0.7 copy-start.11
  9.8 19.2 %copy-start.2 = (s32[128,1]{0,1:T(1,128)S(1)}, s32[128,1]{0,1:T(1,128)}, u32[]{:S(2)}) copy-start(s32[128,1]{0,1:T(1,128)} %param.16) | copy-start | bytes 1540
  31.2 5.1 %copy-start.8 = (bf16[160,1024]{1,0:T(8,128)(2,1)}, bf16[160,1024]{1,0:T(8,128)(2,1)S(1)}, u32[]{:S(2)}) copy-start(bf16[160,1024]{1,0:T(8,128)(2,1)S(1)} %get-tuple-element.33.refs_2_) | copy-start | bytes 983044
  31.2 12.7 %collective-permute-start.2 = (bf16[160,1024]{1,0:T(8,128)(2,1)}, bf16[160,1024]{1,0:T(8,128)(2,1)}, u32[]{:S(2)}, u32[]{:S(2)}) collective-permute-start(bf16[160,1024]{1,0:T(8,128)(2,1)} %get-tuple-element.34), channel_id=1, source_target_pairs={{0,4},{4,8},{8,12},{12,0},{16,20},{20,24},{24,28},{28,16},{1,5},{5... | collective-permute-start | bytes 983048 | tf_op jit(solution)/shard_map/ppermute | solution.py:608
  32.7 11.2 %collective-permute-start.3 = (bf16[160,1024]{1,0:T(8,128)(2,1)}, bf16[160,1024]{1,0:T(8,128)(2,1)}, u32[]{:S(2)}, u32[]{:S(2)}) collective-permute-start(bf16[160,1024]{1,0:T(8,128)(2,1)} %get-tuple-element.35), channel_id=1, source_target_pairs={{0,8},{4,12},{8,0},{12,4},{16,24},{20,28},{24,16},{28,20},{1,9},{5... | collective-permute-start | bytes 983048 | tf_op jit(solution)/shard_map/ppermute | solution.py:608
  34.3 15.5 %collective-permute-start.4 = (bf16[160,1024]{1,0:T(8,128)(2,1)}, bf16[160,1024]{1,0:T(8,128)(2,1)}, u32[]{:S(2)}, u32[]{:S(2)}) collective-permute-start(bf16[160,1024]{1,0:T(8,128)(2,1)} %get-tuple-element.36), channel_id=1, source_target_pairs={{0,12},{4,0},{8,4},{12,8},{16,28},{20,16},{24,20},{28,24},{1,13},{... | collective-permute-start | bytes 983048 | tf_op jit(solution)/shard_map/ppermute | solution.py:608
  36.3 3.4 %copy-start = (bf16[1024,4096]{1,0:T(8,128)(2,1)S(1)}, bf16[1024,4096]{1,0:T(8,128)(2,1)}, u32[]{:S(2)}) copy-start(bf16[1024,4096]{1,0:T(8,128)(2,1)} %w_ref.3) | copy-start | bytes 25165828
  39.7 3.8 %copy-start.7 = (bf16[4,64,1024]{2,1,0:T(8,128)(2,1)S(1)}, bf16[4,64,1024]{2,1,0:T(8,128)(2,1)}, u32[]{:S(2)}) copy-start(bf16[4,64,1024]{2,1,0:T(8,128)(2,1)} %param.19) | copy-start | bytes 1572868
  39.7 10.1 %copy-start.6 = (bf16[4,64,1024]{2,1,0:T(8,128)(2,1)S(1)}, bf16[4,64,1024]{2,1,0:T(8,128)(2,1)}, u32[]{:S(2)}) copy-start(bf16[4,64,1024]{2,1,0:T(8,128)(2,1)} %param.18) | copy-start | bytes 1572868
  39.7 10.1 %copy-start.9 = (bf16[160,1024]{1,0:T(8,128)(2,1)S(1)}, bf16[160,1024]{1,0:T(8,128)(2,1)}, u32[]{:S(2)}) copy-start(bf16[160,1024]{1,0:T(8,128)(2,1)} %copy-done.8) | copy-start | bytes 983044
  43.5 17.4 %collective-permute-start.7 = (bf16[2,512,1024]{2,1,0:T(8,128)(2,1)}, bf16[2,512,1024]{2,1,0:T(8,128)(2,1)}, u32[]{:S(2)}, u32[]{:S(2)}) collective-permute-start(bf16[2,512,1024]{2,1,0:T(8,128)(2,1)} %shard_map.102), channel_id=1, source_target_pairs={{0,1},{1,0},{2,3},{3,2},{4,5},{5,4},{6,7},{7,6},{8,9},{9,8},{10,11... | collective-permute-start | bytes 6291464 | tf_op jit(solution)/shard_map/ppermute | solution.py:613
  43.5 26.4 %collective-permute-start.1 = (bf16[256,1024]{1,0:T(8,128)(2,1)S(1)}, bf16[256,1024]{1,0:T(8,128)(2,1)S(1)}, u32[]{:S(2)}, u32[]{:S(2)}) collective-permute-start(bf16[256,1024]{1,0:T(8,128)(2,1)S(1)} %bitcast.12), channel_id=1, source_target_pairs={{0,16},{4,20},{8,24},{12,28},{16,0},{20,4},{24,8},{28,12},{1,17},{... | collective-permute-start | bytes 1572872 | tf_op jit(solution)/shard_map/ppermute | solution.py:615
  51.6 1.5 %collective-permute-start.5 = (f32[320,128]{1,0:T(8,128)S(1)}, f32[320,128]{1,0:T(8,128)S(1)}, u32[]{:S(2)}, u32[]{:S(2)}) collective-permute-start(f32[320,128]{1,0:T(8,128)S(1)} %shard_map.104), channel_id=1, source_target_pairs={{0,1},{1,0},{2,3},{3,2},{4,5},{5,4},{6,7},{7,6},{8,9},{9,8},{10,11... | collective-permute-start | bytes 491528 | tf_op jit(solution)/shard_map/ppermute | solution.py:617
  53.1 9.9 %collective-permute-start.6 = (bf16[320,128]{1,0:T(8,128)(2,1)S(1)}, bf16[320,128]{1,0:T(8,128)(2,1)S(1)}, u32[]{:S(2)}, u32[]{:S(2)}) collective-permute-start(bf16[320,128]{1,0:T(8,128)(2,1)S(1)} %add_convert_fusion.refs_2_), channel_id=1, source_target_pairs={{0,2},{1,3},{2,0},{3,1},{4,6},{5,7},{6,4},{7,5},{8,10},{9,11},{10,... | collective-permute-start | bytes 245768 | tf_op jit(solution)/shard_map/ppermute | solution.py:621
  54.6 3.4 %copy-start.1 = (bf16[1024,4096]{1,0:T(8,128)(2,1)S(1)}, bf16[1024,4096]{1,0:T(8,128)(2,1)}, u32[]{:S(2)}) copy-start(bf16[1024,4096]{1,0:T(8,128)(2,1)} %w_ref.3) | copy-start | bytes 25165828
  62.9 25.0 %collective-permute-start.11 = (bf16[512,1024]{1,0:T(8,128)(2,1)S(1)}, bf16[512,1024]{1,0:T(8,128)(2,1)S(1)}, u32[]{:S(2)}, u32[]{:S(2)}) collective-permute-start(bf16[512,1024]{1,0:T(8,128)(2,1)S(1)} %get-tuple-element.48), channel_id=1, source_target_pairs={{0,2},{1,3},{2,0},{3,1},{4,6},{5,7},{6,4},{7,5},{8,10},{9,11},{10,... | collective-permute-start | bytes 3145736 | tf_op jit(solution)/shard_map/ppermute | solution.py:593
  70.5 14.7 %collective-permute-start.10 = (bf16[160,1024]{1,0:T(8,128)(2,1)S(1)}, bf16[160,1024]{1,0:T(8,128)(2,1)S(1)}, u32[]{:S(2)}, u32[]{:S(2)}) collective-permute-start(bf16[160,1024]{1,0:T(8,128)(2,1)S(1)} %get-tuple-element.46), channel_id=1, source_target_pairs={{0,4},{4,8},{8,12},{12,0},{16,20},{20,24},{24,28},{28,16},{1,5},{5... | collective-permute-start | bytes 983048 | tf_op jit(solution)/shard_map/ppermute | solution.py:626
  71.2 16.2 %collective-permute-start.8 = (bf16[160,1024]{1,0:T(8,128)(2,1)S(1)}, bf16[160,1024]{1,0:T(8,128)(2,1)S(1)}, u32[]{:S(2)}, u32[]{:S(2)}) collective-permute-start(bf16[160,1024]{1,0:T(8,128)(2,1)S(1)} %get-tuple-element.44), channel_id=1, source_target_pairs={{0,12},{4,0},{8,4},{12,8},{16,28},{20,16},{24,20},{28,24},{1,13},{... | collective-permute-start | bytes 983048 | tf_op jit(solution)/shard_map/ppermute | solution.py:626
  73.5 13.9 %collective-permute-start.9 = (bf16[160,1024]{1,0:T(8,128)(2,1)S(1)}, bf16[160,1024]{1,0:T(8,128)(2,1)S(1)}, u32[]{:S(2)}, u32[]{:S(2)}) collective-permute-start(bf16[160,1024]{1,0:T(8,128)(2,1)S(1)} %get-tuple-element.45), channel_id=1, source_target_pairs={{0,8},{4,12},{8,0},{12,4},{16,24},{20,28},{24,16},{28,20},{1,9},{5... | collective-permute-start | bytes 983048 | tf_op jit(solution)/shard_map/ppermute | solution.py:626

commit v4 on v3

--- a/solution.py
+++ b/solution.py
@@ -268,7 +268,7 @@
             pltpu.VMEM(fresh.shape, fresh.dtype),
             pltpu.SemaphoreType.DMA((8,)),
         ],
-        compiler_params=pltpu.CompilerParams(vmem_limit_bytes=44 * MIB),
+        compiler_params=pltpu.CompilerParams(vmem_limit_bytes=60 * MIB),
         cost_estimate=LENGTHY,
     )(lengths, prefixes, queries, prefix, suffix, fresh)
 

time: 91.3 us -> 90.4 us (level)
  local copies, waits for them, and re-layouts: 12.5 us -> 9.97 us
  Pallas kernels: 35.9 us -> 38 us
    unnamed x24 -> x20, local copies, waits for them, and re-layouts: 12.5 us -> 9.97 us
    pallas_call x1, Pallas kernels: 19.1 us -> 21.2 us  [attend(): pl.pallas_call(functools.partial(attend_kernel, steps=steps, group=group,...]
    ppermute x3, waiting for transfers between devices: 5.92 us -> 4.67 us  [local(): lax.ppermute(packed[d], 'adapter', in_block(d))]
    ppermute x1, waiting for transfers between devices: 6.4 us -> 7.59 us  [local(): expand = lax.ppermute(moved, 'adapter', far)]
  transfers between devices with their start and end apart: 12 -> 12, of which waited for: 6 -> 5; matrix products, arithmetic and copies ran while one was open for 0% -> 0% of each run, Pallas kernels for 36% -> 39%
where the time goes in v4:
time: 90.4 us; the launch traced here: 90 us
  Pallas kernels  38 us (42%)
  waiting for transfers between devices  27.8 us (31%)
  starting transfers between devices  14.1 us (16%)
  local copies, waits for them, and re-layouts  9.97 us (11%)
    pallas_call x1, Pallas kernels, attend(): pl.pallas_call(functools.partial(attend_kernel, steps=steps, group=group,...  21.2 us
    ppermute x3, waiting for transfers between devices, local(): lax.ppermute(wide[d], 'adapter', in_block(block - d))  14.1 us
    unnamed x20, local copies, waits for them, and re-layouts  9.97 us
    ppermute x1, waiting for transfers between devices, local(): expand = lax.ppermute(moved, 'adapter', far)  7.59 us
    pallas_call x2, Pallas kernels, project(): pl.pallas_call(project_kernel, grid_spec=pltpu.PrefetchScalarGridSpec(num...  6.61 us
    ppermute x3, waiting for transfers between devices, local(): lax.ppermute(packed[d], 'adapter', in_block(d))  4.67 us
    ppermute x3, starting transfers between devices, local(): lax.ppermute(packed[d], 'adapter', in_block(d))  4.5 us
    ppermute x1, starting transfers between devices, local(): shrink = lax.ppermute(own_shrink, 'adapter', far)  4.04 us
  transfers between devices with their start and end apart: 12, of which 5 were waited for; matrix products, arithmetic and copies ran while one was open for 0% of the time, Pallas kernels for 39%

profile of v4, /device:TPU:0, one launch (start us, length us, event | category | flops | bytes accessed | tf_op | source)
XLA Modules:
  0.0 90.0 jit_solution(4692953226751300464)
XLA Ops:
  0.0 4.0 %collective-permute-start = (bf16[256,1024]{1,0:T(8,128)(2,1)}, bf16[256,1024]{1,0:T(8,128)(2,1)S(1)}, u32[]{:S(2)}, u32[]{:S(2)}) collective-permute-start(bf16[256,1024]{1,0:T(8,128)(2,1)} %bitcast.10), channel_id=1, source_target_pairs={{0,16},{4,20},{8,24},{12,28},{16,0},{20,4},{24,8},{28,12},{1,17},{... | collective-permute-start | bytes 1572872 | tf_op jit(solution)/shard_map/ppermute | solution.py:600
  4.0 0.0 copy-start.5
  4.0 21.2 %shard_map.100.refs_0_.a_ref = bf16[512,1024]{1,0:T(8,128)(2,1)} custom-call(s32[1,128]{1,0:T(1,128)} %bitcast.14, s32[1,128]{1,0:T(1,128)} %bitcast.15, bf16[128,4,1024]{2,1,0:T(4,128)(2,1)} %q_hbm.1, bf16[2,2,2048,256]{3,2,1,0:T(8,128)(2,1)} %kv_hbm.1, bf16[2,128,32,256]{3,2,1,0:T(8,128)(2,1)} %suf_hbm.1, bf16[2,128,4,256]{3,2,1,0:T(4,128)(2,1)} %fr_hbm.1), custom_call_target="tpu_custom_call" | custom-call | flops 68719476736 | bytes 134217728 | tf_op jit(solution)/shard_map/pallas_call | solution.py:255
  25.3 0.0 copy-done.5
  25.3 0.0 copy-start.2
  25.3 1.2 %copy-done.2 = bf16[512,1024]{1,0:T(8,128)(2,1)S(1)} copy-done((bf16[512,1024]{1,0:T(8,128)(2,1)S(1)}, bf16[512,1024]{1,0:T(8,128)(2,1)}, u32[]{:S(2)}) %copy-start.2) | copy-done | bytes 1048600
  26.5 2.2 %shard_map.101 = (bf16[160,1024]{1,0:T(8,128)(2,1)S(1)}, bf16[160,1024]{1,0:T(8,128)(2,1)}, bf16[160,1024]{1,0:T(8,128)(2,1)}, bf16[160,1024]{1,0:T(8,128)(2,1)}) custom-call(s32[1]{0:T(128)} %bitcast.3.here_ref, s32[1,128]{1,0:T(1,128)S(1)} %bitcast.8, bf16[512,1024]{1,0:T(8,128)(2,1)S(1)} %copy-done.2), custom_call_target="tpu_custom_call" | custom-call | flops 1024 | bytes 1024 | tf_op jit(solution)/shard_map/pallas_call | solution.py:386
  28.7 0.0 copy-start.8
  28.7 0.7 copy-done.8
  29.5 1.5 %collective-permute-start.2 = (bf16[160,1024]{1,0:T(8,128)(2,1)}, bf16[160,1024]{1,0:T(8,128)(2,1)}, u32[]{:S(2)}, u32[]{:S(2)}) collective-permute-start(bf16[160,1024]{1,0:T(8,128)(2,1)} %get-tuple-element.34), channel_id=1, source_target_pairs={{0,4},{4,8},{8,12},{12,0},{16,20},{20,24},{24,28},{28,16},{1,5},{5... | collective-permute-start | bytes 983048 | tf_op jit(solution)/shard_map/ppermute | solution.py:608
  31.0 1.6 %collective-permute-start.3 = (bf16[160,1024]{1,0:T(8,128)(2,1)}, bf16[160,1024]{1,0:T(8,128)(2,1)}, u32[]{:S(2)}, u32[]{:S(2)}) collective-permute-start(bf16[160,1024]{1,0:T(8,128)(2,1)} %get-tuple-element.35), channel_id=1, source_target_pairs={{0,8},{4,12},{8,0},{12,4},{16,24},{20,28},{24,16},{28,20},{1,9},{5... | collective-permute-start | bytes 983048 | tf_op jit(solution)/shard_map/ppermute | solution.py:608
  32.6 1.4 %collective-permute-start.4 = (bf16[160,1024]{1,0:T(8,128)(2,1)}, bf16[160,1024]{1,0:T(8,128)(2,1)}, u32[]{:S(2)}, u32[]{:S(2)}) collective-permute-start(bf16[160,1024]{1,0:T(8,128)(2,1)} %get-tuple-element.36), channel_id=1, source_target_pairs={{0,12},{4,0},{8,4},{12,8},{16,28},{20,16},{24,20},{28,24},{1,13},{... | collective-permute-start | bytes 983048 | tf_op jit(solution)/shard_map/ppermute | solution.py:608
  34.0 0.6 shard_map.103.chosen_ref
  34.6 0.0 copy-start
  34.6 3.4 %copy-done = bf16[1024,4096]{1,0:T(8,128)(2,1)S(1)} copy-done((bf16[1024,4096]{1,0:T(8,128)(2,1)S(1)}, bf16[1024,4096]{1,0:T(8,128)(2,1)}, u32[]{:S(2)}) %copy-start) | copy-done | bytes 8388632
  37.9 0.0 copy-start.3
  37.9 1.2 %copy-done.3 = bf16[512,1024]{1,0:T(8,128)(2,1)S(1)} copy-done((bf16[512,1024]{1,0:T(8,128)(2,1)S(1)}, bf16[512,1024]{1,0:T(8,128)(2,1)}, u32[]{:S(2)}) %copy-start.3) | copy-done | bytes 1048600
  39.2 0.0 copy-start.7
  39.2 0.0 copy-start.6
  39.2 0.0 copy-start.9
  39.2 3.8 %shard_map.102 = bf16[2,512,1024]{2,1,0:T(8,128)(2,1)} custom-call(s32[1]{0:T(128)S(6)} %sub.7.core_ref, bf16[512,1024]{1,0:T(8,128)(2,1)S(1)} %copy-done.3, bf16[1024,4096]{1,0:T(8,128)(2,1)S(1)} %copy-done), custom_call_target="tpu_custom_call" | custom-call | flops 1024 | bytes 1024 | tf_op jit(solution)/shard_map/pallas_call | solution.py:284
  43.0 0.0 collective-permute-start.7
  43.0 0.0 collective-permute-done.refs_1_
  43.0 0.0 copy-done.7
  43.0 0.0 copy-start.4
  43.0 0.4 collective-permute-start.1
  43.4 0.0 collective-permute-done.2.refs_3_
  43.4 0.0 collective-permute-done.3.refs_4_
  43.4 4.7 %collective-permute-done.4.refs_5_ = bf16[160,1024]{1,0:T(8,128)(2,1)} collective-permute-done((bf16[160,1024]{1,0:T(8,128)(2,1)}, bf16[160,1024]{1,0:T(8,128)(2,1)}, u32[]{:S(2)}, u32[]{:S(2)}) %collective-permute-start.4) | collective-permute-done | bytes 327712 | tf_op jit(solution)/shard_map/ppermute | solution.py:608
  48.1 0.0 copy-done.6
  48.1 0.0 copy-done.9
  48.1 1.8 %shard_map.104 = f32[320,128]{1,0:T(8,128)S(1)} custom-call(bf16[256,1024]{1,0:T(8,128)(2,1)S(1)} %bitcast.11, bf16[256,1024]{1,0:T(8,128)(2,1)S(1)} %collective-permute-done.refs_1_, bf16[160,1024]{1,0:T(8,128)(2,1)S(1)} %copy-done.9, bf16[160,1024]{1,0:T(8,128)(2,1)} %collective-permute-done.2.refs_3_, bf16[160,1024]{1,0:T(8,128)(2,1)} %collective-permute-done.3.refs_4_, ...), custom_call_target="tpu_custom_call" | custom-call | flops 68719476736 | bytes 134217728 | tf_op jit(solution)/shard_map/pallas_call | solution.py:433
  49.9 0.1 collective-permute-start.5
  49.9 1.4 %collective-permute-done.5 = f32[320,128]{1,0:T(8,128)S(1)} collective-permute-done((f32[320,128]{1,0:T(8,128)S(1)}, f32[320,128]{1,0:T(8,128)S(1)}, u32[]{:S(2)}, u32[]{:S(2)}) %collective-permute-start.5) | collective-permute-done | bytes 163872 | tf_op jit(solution)/shard_map/ppermute | solution.py:617
  51.3 1.6 %collective-permute-start.6 = (bf16[320,128]{1,0:T(8,128)(2,1)S(1)}, bf16[320,128]{1,0:T(8,128)(2,1)S(1)}, u32[]{:S(2)}, u32[]{:S(2)}) collective-permute-start(bf16[320,128]{1,0:T(8,128)(2,1)S(1)} %add_convert_fusion.refs_2_), channel_id=1, source_target_pairs={{0,2},{1,3},{2,0},{3,1},{4,6},{5,7},{6,4},{7,5},{8,10},{9,11},{10,... | collective-permute-start | bytes 245768 | tf_op jit(solution)/shard_map/ppermute | solution.py:621
  52.9 0.0 copy-done.4
  52.9 0.0 copy-start.1
  52.9 3.4 %copy-done.1 = bf16[1024,4096]{1,0:T(8,128)(2,1)S(1)} copy-done((bf16[1024,4096]{1,0:T(8,128)(2,1)S(1)}, bf16[1024,4096]{1,0:T(8,128)(2,1)}, u32[]{:S(2)}) %copy-start.1) | copy-done | bytes 8388632
  56.3 2.8 %shard_map.105.keep_ref = bf16[2,512,1024]{2,1,0:T(8,128)(2,1)S(1)} custom-call(s32[1]{0:T(128)} %bitcast.core_ref, bf16[512,1024]{1,0:T(8,128)(2,1)S(1)} %copy-done.4, bf16[1024,4096]{1,0:T(8,128)(2,1)S(1)} %copy-done.1), custom_call_target="tpu_custom_call" | custom-call | flops 1024 | bytes 1024 | tf_op jit(solution)/shard_map/pallas_call | solution.py:284
  59.1 0.0 collective-permute-done.7.come_ref
  59.1 2.1 %shard_map.106 = (bf16[512,1024]{1,0:T(8,128)(2,1)S(1)}, bf16[512,1024]{1,0:T(8,128)(2,1)S(1)}) custom-call(s32[1]{0:T(128)} %bitcast.7.chip_ref, bf16[2,512,1024]{2,1,0:T(8,128)(2,1)S(1)} %shard_map.105.keep_ref, bf16[2,512,1024]{2,1,0:T(8,128)(2,1)} %collective-permute-done.7.come_ref), custom_call_target="tpu_custom_call" | custom-call | flops 1024 | bytes 1024 | tf_op jit(solution)/shard_map/pallas_call | solution.py:319
  61.2 0.0 collective-permute-done.6.refs_3_
  61.2 0.6 collective-permute-start.11
  61.8 7.6 %collective-permute-done.1.refs_1_ = bf16[256,1024]{1,0:T(8,128)(2,1)S(1)} collective-permute-done((bf16[256,1024]{1,0:T(8,128)(2,1)S(1)}, bf16[256,1024]{1,0:T(8,128)(2,1)S(1)}, u32[]{:S(2)}, u32[]{:S(2)}) %collective-permute-start.1) | collective-permute-done | bytes 524320 | tf_op jit(solution)/shard_map/ppermute | solution.py:615
  69.4 0.6 shard_map.107
  69.9 0.7 collective-permute-start.10
  70.6 2.3 %collective-permute-start.8 = (bf16[160,1024]{1,0:T(8,128)(2,1)S(1)}, bf16[160,1024]{1,0:T(8,128)(2,1)S(1)}, u32[]{:S(2)}, u32[]{:S(2)}) collective-permute-start(bf16[160,1024]{1,0:T(8,128)(2,1)S(1)} %get-tuple-element.44), channel_id=1, source_target_pairs={{0,12},{4,0},{8,4},{12,8},{16,28},{20,16},{24,20},{28,24},{1,13},{... | collective-permute-start | bytes 983048 | tf_op jit(solution)/shard_map/ppermute | solution.py:626
  72.9 0.0 collective-permute-start.9
  72.9 11.9 %collective-permute-done.10.refs_3_ = bf16[160,1024]{1,0:T(8,128)(2,1)S(1)} collective-permute-done((bf16[160,1024]{1,0:T(8,128)(2,1)S(1)}, bf16[160,1024]{1,0:T(8,128)(2,1)S(1)}, u32[]{:S(2)}, u32[]{:S(2)}) %collective-permute-start.10) | collective-permute-done | bytes 327712 | tf_op jit(solution)/shard_map/ppermute | solution.py:626
  84.8 2.2 %collective-permute-done.8.refs_1_ = bf16[160,1024]{1,0:T(8,128)(2,1)S(1)} collective-permute-done((bf16[160,1024]{1,0:T(8,128)(2,1)S(1)}, bf16[160,1024]{1,0:T(8,128)(2,1)S(1)}, u32[]{:S(2)}, u32[]{:S(2)}) %collective-permute-start.8) | collective-permute-done | bytes 327712 | tf_op jit(solution)/shard_map/ppermute | solution.py:626
  87.0 0.0 collective-permute-done.9.refs_2_
  87.1 0.0 collective-permute-done.11.refs_5_
  87.1 3.0 %shard_map.108 = bf16[128,4,1024]{2,1,0:T(4,128)(2,1)} custom-call(bf16[512,640]{1,0:T(8,128)(2,1)S(1)} %shard_map.103.chosen_ref, bf16[160,1024]{1,0:T(8,128)(2,1)S(1)} %get-tuple-element.43.refs_0_, bf16[160,1024]{1,0:T(8,128)(2,1)S(1)} %collective-permute-done.8.refs_1_, bf16[160,1024]{1,0:T(8,128)(2,1)S(1)} %collective-permute-done.9.refs_2_, ...), custom_call_target="tpu_custom_call" | custom-call | flops 1024 | bytes 1024 | tf_op jit(solution)/shard_map/pallas_call | solution.py:536
  (1 shorter events, 0.0 us)
Async XLA Ops:
  0.0 43.0 %collective-permute-start = (bf16[256,1024]{1,0:T(8,128)(2,1)}, bf16[256,1024]{1,0:T(8,128)(2,1)S(1)}, u32[]{:S(2)}, u32[]{:S(2)}) collective-permute-start(bf16[256,1024]{1,0:T(8,128)(2,1)} %bitcast.10), channel_id=1, source_target_pairs={{0,16},{4,20},{8,24},{12,28},{16,0},{20,4},{24,8},{28,12},{1,17},{... | collective-permute-start | bytes 1572872 | tf_op jit(solution)/shard_map/ppermute | solution.py:600
  4.0 21.2 %copy-start.5 = (s32[128,1]{0,1:T(1,128)S(1)}, s32[128,1]{0,1:T(1,128)}, u32[]{:S(2)}) copy-start(s32[128,1]{0,1:T(1,128)} %param.16) | copy-start | bytes 1540
  25.3 1.2 %copy-start.2 = (bf16[512,1024]{1,0:T(8,128)(2,1)S(1)}, bf16[512,1024]{1,0:T(8,128)(2,1)}, u32[]{:S(2)}) copy-start(bf16[512,1024]{1,0:T(8,128)(2,1)} %shard_map.100.refs_0_.a_ref) | copy-start | bytes 3145732
  28.7 0.7 copy-start.8
  29.5 13.9 %collective-permute-start.2 = (bf16[160,1024]{1,0:T(8,128)(2,1)}, bf16[160,1024]{1,0:T(8,128)(2,1)}, u32[]{:S(2)}, u32[]{:S(2)}) collective-permute-start(bf16[160,1024]{1,0:T(8,128)(2,1)} %get-tuple-element.34), channel_id=1, source_target_pairs={{0,4},{4,8},{8,12},{12,0},{16,20},{20,24},{24,28},{28,16},{1,5},{5... | collective-permute-start | bytes 983048 | tf_op jit(solution)/shard_map/ppermute | solution.py:608
  31.0 12.4 %collective-permute-start.3 = (bf16[160,1024]{1,0:T(8,128)(2,1)}, bf16[160,1024]{1,0:T(8,128)(2,1)}, u32[]{:S(2)}, u32[]{:S(2)}) collective-permute-start(bf16[160,1024]{1,0:T(8,128)(2,1)} %get-tuple-element.35), channel_id=1, source_target_pairs={{0,8},{4,12},{8,0},{12,4},{16,24},{20,28},{24,16},{28,20},{1,9},{5... | collective-permute-start | bytes 983048 | tf_op jit(solution)/shard_map/ppermute | solution.py:608
  32.6 15.5 %collective-permute-start.4 = (bf16[160,1024]{1,0:T(8,128)(2,1)}, bf16[160,1024]{1,0:T(8,128)(2,1)}, u32[]{:S(2)}, u32[]{:S(2)}) collective-permute-start(bf16[160,1024]{1,0:T(8,128)(2,1)} %get-tuple-element.36), channel_id=1, source_target_pairs={{0,12},{4,0},{8,4},{12,8},{16,28},{20,16},{24,20},{28,24},{1,13},{... | collective-permute-start | bytes 983048 | tf_op jit(solution)/shard_map/ppermute | solution.py:608
  34.6 3.4 %copy-start = (bf16[1024,4096]{1,0:T(8,128)(2,1)S(1)}, bf16[1024,4096]{1,0:T(8,128)(2,1)}, u32[]{:S(2)}) copy-start(bf16[1024,4096]{1,0:T(8,128)(2,1)} %w_ref.3) | copy-start | bytes 25165828
  37.9 1.2 %copy-start.3 = (bf16[512,1024]{1,0:T(8,128)(2,1)S(1)}, bf16[512,1024]{1,0:T(8,128)(2,1)}, u32[]{:S(2)}) copy-start(bf16[512,1024]{1,0:T(8,128)(2,1)} %shard_map.100.refs_0_.a_ref) | copy-start | bytes 3145732
  39.2 3.8 %copy-start.7 = (bf16[4,64,1024]{2,1,0:T(8,128)(2,1)S(1)}, bf16[4,64,1024]{2,1,0:T(8,128)(2,1)}, u32[]{:S(2)}) copy-start(bf16[4,64,1024]{2,1,0:T(8,128)(2,1)} %param.19) | copy-start | bytes 1572868
  39.2 8.9 %copy-start.6 = (bf16[4,64,1024]{2,1,0:T(8,128)(2,1)S(1)}, bf16[4,64,1024]{2,1,0:T(8,128)(2,1)}, u32[]{:S(2)}) copy-start(bf16[4,64,1024]{2,1,0:T(8,128)(2,1)} %param.18) | copy-start | bytes 1572868
  39.2 8.9 %copy-start.9 = (bf16[160,1024]{1,0:T(8,128)(2,1)S(1)}, bf16[160,1024]{1,0:T(8,128)(2,1)}, u32[]{:S(2)}) copy-start(bf16[160,1024]{1,0:T(8,128)(2,1)} %copy-done.8) | copy-start | bytes 983044
  43.0 16.2 %collective-permute-start.7 = (bf16[2,512,1024]{2,1,0:T(8,128)(2,1)}, bf16[2,512,1024]{2,1,0:T(8,128)(2,1)}, u32[]{:S(2)}, u32[]{:S(2)}) collective-permute-start(bf16[2,512,1024]{2,1,0:T(8,128)(2,1)} %shard_map.102), channel_id=1, source_target_pairs={{0,1},{1,0},{2,3},{3,2},{4,5},{5,4},{6,7},{7,6},{8,9},{9,8},{10,11... | collective-permute-start | bytes 6291464 | tf_op jit(solution)/shard_map/ppermute | solution.py:613
  43.0 9.9 %copy-start.4 = (bf16[512,1024]{1,0:T(8,128)(2,1)S(1)}, bf16[512,1024]{1,0:T(8,128)(2,1)}, u32[]{:S(2)}) copy-start(bf16[512,1024]{1,0:T(8,128)(2,1)} %shard_map.100.refs_0_.a_ref) | copy-start | bytes 3145732
  43.0 26.4 %collective-permute-start.1 = (bf16[256,1024]{1,0:T(8,128)(2,1)S(1)}, bf16[256,1024]{1,0:T(8,128)(2,1)S(1)}, u32[]{:S(2)}, u32[]{:S(2)}) collective-permute-start(bf16[256,1024]{1,0:T(8,128)(2,1)S(1)} %bitcast.12), channel_id=1, source_target_pairs={{0,16},{4,20},{8,24},{12,28},{16,0},{20,4},{24,8},{28,12},{1,17},{... | collective-permute-start | bytes 1572872 | tf_op jit(solution)/shard_map/ppermute | solution.py:615
  49.9 1.5 %collective-permute-start.5 = (f32[320,128]{1,0:T(8,128)S(1)}, f32[320,128]{1,0:T(8,128)S(1)}, u32[]{:S(2)}, u32[]{:S(2)}) collective-permute-start(f32[320,128]{1,0:T(8,128)S(1)} %shard_map.104), channel_id=1, source_target_pairs={{0,1},{1,0},{2,3},{3,2},{4,5},{5,4},{6,7},{7,6},{8,9},{9,8},{10,11... | collective-permute-start | bytes 491528 | tf_op jit(solution)/shard_map/ppermute | solution.py:617
  51.3 9.9 %collective-permute-start.6 = (bf16[320,128]{1,0:T(8,128)(2,1)S(1)}, bf16[320,128]{1,0:T(8,128)(2,1)S(1)}, u32[]{:S(2)}, u32[]{:S(2)}) collective-permute-start(bf16[320,128]{1,0:T(8,128)(2,1)S(1)} %add_convert_fusion.refs_2_), channel_id=1, source_target_pairs={{0,2},{1,3},{2,0},{3,1},{4,6},{5,7},{6,4},{7,5},{8,10},{9,11},{10,... | collective-permute-start | bytes 245768 | tf_op jit(solution)/shard_map/ppermute | solution.py:621
  52.9 3.4 %copy-start.1 = (bf16[1024,4096]{1,0:T(8,128)(2,1)S(1)}, bf16[1024,4096]{1,0:T(8,128)(2,1)}, u32[]{:S(2)}) copy-start(bf16[1024,4096]{1,0:T(8,128)(2,1)} %w_ref.3) | copy-start | bytes 25165828
  61.2 25.8 %collective-permute-start.11 = (bf16[512,1024]{1,0:T(8,128)(2,1)S(1)}, bf16[512,1024]{1,0:T(8,128)(2,1)S(1)}, u32[]{:S(2)}, u32[]{:S(2)}) collective-permute-start(bf16[512,1024]{1,0:T(8,128)(2,1)S(1)} %get-tuple-element.48), channel_id=1, source_target_pairs={{0,2},{1,3},{2,0},{3,1},{4,6},{5,7},{6,4},{7,5},{8,10},{9,11},{10,... | collective-permute-start | bytes 3145736 | tf_op jit(solution)/shard_map/ppermute | solution.py:593
  69.9 14.9 %collective-permute-start.10 = (bf16[160,1024]{1,0:T(8,128)(2,1)S(1)}, bf16[160,1024]{1,0:T(8,128)(2,1)S(1)}, u32[]{:S(2)}, u32[]{:S(2)}) collective-permute-start(bf16[160,1024]{1,0:T(8,128)(2,1)S(1)} %get-tuple-element.46), channel_id=1, source_target_pairs={{0,4},{4,8},{8,12},{12,0},{16,20},{20,24},{24,28},{28,16},{1,5},{5... | collective-permute-start | bytes 983048 | tf_op jit(solution)/shard_map/ppermute | solution.py:626
  70.6 16.4 %collective-permute-start.8 = (bf16[160,1024]{1,0:T(8,128)(2,1)S(1)}, bf16[160,1024]{1,0:T(8,128)(2,1)S(1)}, u32[]{:S(2)}, u32[]{:S(2)}) collective-permute-start(bf16[160,1024]{1,0:T(8,128)(2,1)S(1)} %get-tuple-element.44), channel_id=1, source_target_pairs={{0,12},{4,0},{8,4},{12,8},{16,28},{20,16},{24,20},{28,24},{1,13},{... | collective-permute-start | bytes 983048 | tf_op jit(solution)/shard_map/ppermute | solution.py:626
  72.9 14.1 %collective-permute-start.9 = (bf16[160,1024]{1,0:T(8,128)(2,1)S(1)}, bf16[160,1024]{1,0:T(8,128)(2,1)S(1)}, u32[]{:S(2)}, u32[]{:S(2)}) collective-permute-start(bf16[160,1024]{1,0:T(8,128)(2,1)S(1)} %get-tuple-element.45), channel_id=1, source_target_pairs={{0,8},{4,12},{8,0},{12,4},{16,24},{20,28},{24,16},{28,20},{1,9},{5... | collective-permute-start | bytes 983048 | tf_op jit(solution)/shard_map/ppermute | solution.py:626

commit v5 on v4

--- a/solution.py
+++ b/solution.py
@@ -268,7 +268,7 @@
             pltpu.VMEM(fresh.shape, fresh.dtype),
             pltpu.SemaphoreType.DMA((8,)),
         ],
-        compiler_params=pltpu.CompilerParams(vmem_limit_bytes=60 * MIB),
+        compiler_params=pltpu.CompilerParams(vmem_limit_bytes=52 * MIB),
         cost_estimate=LENGTHY,
     )(lengths, prefixes, queries, prefix, suffix, fresh)
 

time: 90.4 us -> 88.6 us (0.980)
  Pallas kernels: 38 us -> 36.8 us
    pallas_call x1, Pallas kernels: 21.2 us -> 20 us  [attend(): pl.pallas_call(functools.partial(attend_kernel, steps=steps, group=group,...]
    ppermute x3, waiting for transfers between devices: 4.67 us -> 5.89 us  [local(): lax.ppermute(packed[d], 'adapter', in_block(d))]
    ppermute x1, waiting for transfers between devices: 7.59 us -> 6.41 us  [local(): expand = lax.ppermute(moved, 'adapter', far)]
  transfers between devices with their start and end apart: 12 -> 12, of which waited for: 5 -> 6; matrix products, arithmetic and copies ran while one was open for 0% -> 0% of each run, Pallas kernels for 39% -> 38%
where the time goes in v5:
time: 88.6 us; the launch traced here: 88.3 us
  Pallas kernels  36.8 us (42%)
  waiting for transfers between devices  28.1 us (32%)
  starting transfers between devices  14.2 us (16%)
  local copies, waits for them, and re-layouts  9.13 us (10%)
    pallas_call x1, Pallas kernels, attend(): pl.pallas_call(functools.partial(attend_kernel, steps=steps, group=group,...  20 us
    ppermute x3, waiting for transfers between devices, local(): lax.ppermute(wide[d], 'adapter', in_block(block - d))  13.9 us
    unnamed x20, local copies, waits for them, and re-layouts  9.13 us
    pallas_call x2, Pallas kernels, project(): pl.pallas_call(project_kernel, grid_spec=pltpu.PrefetchScalarGridSpec(num...  6.61 us
    ppermute x1, waiting for transfers between devices, local(): expand = lax.ppermute(moved, 'adapter', far)  6.41 us
    ppermute x3, waiting for transfers between devices, local(): lax.ppermute(packed[d], 'adapter', in_block(d))  5.89 us
    ppermute x3, starting transfers between devices, local(): lax.ppermute(packed[d], 'adapter', in_block(d))  4.5 us
    ppermute x1, starting transfers between devices, local(): shrink = lax.ppermute(own_shrink, 'adapter', far)  4.04 us
  transfers between devices with their start and end apart: 12, of which 6 were waited for; matrix products, arithmetic and copies ran while one was open for 0% of the time, Pallas kernels for 38%

profile of v5, /device:TPU:0, one launch (start us, length us, event | category | flops | bytes accessed | tf_op | source)
XLA Modules:
  0.0 88.3 jit_solution(3371593492242251109)
XLA Ops:
  0.0 4.0 %collective-permute-start = (bf16[256,1024]{1,0:T(8,128)(2,1)}, bf16[256,1024]{1,0:T(8,128)(2,1)S(1)}, u32[]{:S(2)}, u32[]{:S(2)}) collective-permute-start(bf16[256,1024]{1,0:T(8,128)(2,1)} %bitcast.10), channel_id=1, source_target_pairs={{0,16},{4,20},{8,24},{12,28},{16,0},{20,4},{24,8},{28,12},{1,17},{... | collective-permute-start | bytes 1572872 | tf_op jit(solution)/shard_map/ppermute | solution.py:600
  4.0 0.0 copy-start.3
  4.0 1.0 %copy-done.3 = bf16[2,128,4,256]{3,2,1,0:T(4,128)(2,1)S(1)} copy-done((bf16[2,128,4,256]{3,2,1,0:T(4,128)(2,1)S(1)}, bf16[2,128,4,256]{3,2,1,0:T(4,128)(2,1)}, u32[]{:S(2)}) %copy-start.3) | copy-done | bytes 524312
  5.1 0.0 copy-start.8
  5.1 0.7 copy-done.8
  5.7 0.0 copy-start.9
  5.7 0.7 copy-done.9
  6.4 0.0 copy-start.2
  6.4 20.0 %shard_map.100.refs_0_.a_ref = bf16[512,1024]{1,0:T(8,128)(2,1)S(1)} custom-call(s32[1,128]{1,0:T(1,128)S(1)} %bitcast.14, s32[1,128]{1,0:T(1,128)S(1)} %bitcast.15, bf16[128,4,1024]{2,1,0:T(4,128)(2,1)} %q_hbm.1, bf16[2,2,2048,256]{3,2,1,0:T(8,128)(2,1)} %kv_hbm.1, bf16[2,128,32,256]{3,2,1,0:T(8,128)(2,1)} %suf_hbm.1, bf16[2,128,4,256]{3,2,1,0:T(4,128)(2,1)S(1)} %copy-done.3), custom_call_target="tpu_custom_call" | custom-call | flops 68719476736 | bytes 134217728 | tf_op jit(solution)/shard_map/pallas_call | solution.py:255
  26.4 0.0 copy-done.2
  26.4 2.2 %shard_map.101 = (bf16[160,1024]{1,0:T(8,128)(2,1)S(1)}, bf16[160,1024]{1,0:T(8,128)(2,1)}, bf16[160,1024]{1,0:T(8,128)(2,1)}, bf16[160,1024]{1,0:T(8,128)(2,1)}) custom-call(s32[1]{0:T(128)} %bitcast.3.here_ref, s32[1,128]{1,0:T(1,128)S(1)} %bitcast.8, bf16[512,1024]{1,0:T(8,128)(2,1)S(1)} %shard_map.100.refs_0_.a_ref), custom_call_target="tpu_custom_call" | custom-call | flops 1024 | bytes 1024 | tf_op jit(solution)/shard_map/pallas_call | solution.py:386
  28.6 0.0 copy-start.6
  28.6 1.5 %collective-permute-start.2 = (bf16[160,1024]{1,0:T(8,128)(2,1)}, bf16[160,1024]{1,0:T(8,128)(2,1)}, u32[]{:S(2)}, u32[]{:S(2)}) collective-permute-start(bf16[160,1024]{1,0:T(8,128)(2,1)} %get-tuple-element.34), channel_id=1, source_target_pairs={{0,4},{4,8},{8,12},{12,0},{16,20},{20,24},{24,28},{28,16},{1,5},{5... | collective-permute-start | bytes 983048 | tf_op jit(solution)/shard_map/ppermute | solution.py:608
  30.2 1.6 %collective-permute-start.3 = (bf16[160,1024]{1,0:T(8,128)(2,1)}, bf16[160,1024]{1,0:T(8,128)(2,1)}, u32[]{:S(2)}, u32[]{:S(2)}) collective-permute-start(bf16[160,1024]{1,0:T(8,128)(2,1)} %get-tuple-element.35), channel_id=1, source_target_pairs={{0,8},{4,12},{8,0},{12,4},{16,24},{20,28},{24,16},{28,20},{1,9},{5... | collective-permute-start | bytes 983048 | tf_op jit(solution)/shard_map/ppermute | solution.py:608
  31.7 1.4 %collective-permute-start.4 = (bf16[160,1024]{1,0:T(8,128)(2,1)}, bf16[160,1024]{1,0:T(8,128)(2,1)}, u32[]{:S(2)}, u32[]{:S(2)}) collective-permute-start(bf16[160,1024]{1,0:T(8,128)(2,1)} %get-tuple-element.36), channel_id=1, source_target_pairs={{0,12},{4,0},{8,4},{12,8},{16,28},{20,16},{24,20},{28,24},{1,13},{... | collective-permute-start | bytes 983048 | tf_op jit(solution)/shard_map/ppermute | solution.py:608
  33.1 0.6 shard_map.103.chosen_ref
  33.7 0.0 copy-done.6
  33.7 0.0 copy-start
  33.7 3.4 %copy-done = bf16[1024,4096]{1,0:T(8,128)(2,1)S(1)} copy-done((bf16[1024,4096]{1,0:T(8,128)(2,1)S(1)}, bf16[1024,4096]{1,0:T(8,128)(2,1)}, u32[]{:S(2)}) %copy-start) | copy-done | bytes 8388632
  37.1 0.0 copy-start.5
  37.1 0.0 copy-start.4
  37.1 0.0 copy-start.7
  37.1 3.8 %shard_map.102 = bf16[2,512,1024]{2,1,0:T(8,128)(2,1)} custom-call(s32[1]{0:T(128)S(6)} %sub.7.core_ref, bf16[512,1024]{1,0:T(8,128)(2,1)S(1)} %shard_map.100.refs_0_.a_ref, bf16[1024,4096]{1,0:T(8,128)(2,1)S(1)} %copy-done), custom_call_target="tpu_custom_call" | custom-call | flops 1024 | bytes 1024 | tf_op jit(solution)/shard_map/pallas_call | solution.py:284
  40.9 0.0 collective-permute-start.7
  40.9 0.0 collective-permute-done.refs_1_
  40.9 0.0 copy-done.5
  40.9 0.4 collective-permute-start.1
  41.3 0.0 collective-permute-done.2.refs_3_
  41.3 0.0 collective-permute-done.3.refs_4_
  41.3 5.9 %collective-permute-done.4.refs_5_ = bf16[160,1024]{1,0:T(8,128)(2,1)} collective-permute-done((bf16[160,1024]{1,0:T(8,128)(2,1)}, bf16[160,1024]{1,0:T(8,128)(2,1)}, u32[]{:S(2)}, u32[]{:S(2)}) %collective-permute-start.4) | collective-permute-done | bytes 327712 | tf_op jit(solution)/shard_map/ppermute | solution.py:608
  47.2 0.0 copy-done.4
  47.2 0.0 copy-done.7
  47.2 1.8 %shard_map.104 = f32[320,128]{1,0:T(8,128)S(1)} custom-call(bf16[256,1024]{1,0:T(8,128)(2,1)S(1)} %bitcast.11, bf16[256,1024]{1,0:T(8,128)(2,1)S(1)} %collective-permute-done.refs_1_, bf16[160,1024]{1,0:T(8,128)(2,1)S(1)} %copy-done.7, bf16[160,1024]{1,0:T(8,128)(2,1)} %collective-permute-done.2.refs_3_, bf16[160,1024]{1,0:T(8,128)(2,1)} %collective-permute-done.3.refs_4_, ...), custom_call_target="tpu_custom_call" | custom-call | flops 68719476736 | bytes 134217728 | tf_op jit(solution)/shard_map/pallas_call | solution.py:433
  49.0 0.1 collective-permute-start.5
  49.1 1.4 %collective-permute-done.5 = f32[320,128]{1,0:T(8,128)S(1)} collective-permute-done((f32[320,128]{1,0:T(8,128)S(1)}, f32[320,128]{1,0:T(8,128)S(1)}, u32[]{:S(2)}, u32[]{:S(2)}) %collective-permute-start.5) | collective-permute-done | bytes 163872 | tf_op jit(solution)/shard_map/ppermute | solution.py:617
  50.5 1.6 %collective-permute-start.6 = (bf16[320,128]{1,0:T(8,128)(2,1)S(1)}, bf16[320,128]{1,0:T(8,128)(2,1)S(1)}, u32[]{:S(2)}, u32[]{:S(2)}) collective-permute-start(bf16[320,128]{1,0:T(8,128)(2,1)S(1)} %add_convert_fusion.refs_2_), channel_id=1, source_target_pairs={{0,2},{1,3},{2,0},{3,1},{4,6},{5,7},{6,4},{7,5},{8,10},{9,11},{10,... | collective-permute-start | bytes 245768 | tf_op jit(solution)/shard_map/ppermute | solution.py:621
  52.1 0.0 copy-start.1
  52.1 3.4 %copy-done.1 = bf16[1024,4096]{1,0:T(8,128)(2,1)S(1)} copy-done((bf16[1024,4096]{1,0:T(8,128)(2,1)S(1)}, bf16[1024,4096]{1,0:T(8,128)(2,1)}, u32[]{:S(2)}) %copy-start.1) | copy-done | bytes 8388632
  55.4 2.8 %shard_map.105.keep_ref = bf16[2,512,1024]{2,1,0:T(8,128)(2,1)S(1)} custom-call(s32[1]{0:T(128)} %bitcast.core_ref, bf16[512,1024]{1,0:T(8,128)(2,1)S(1)} %shard_map.100.refs_0_.a_ref, bf16[1024,4096]{1,0:T(8,128)(2,1)S(1)} %copy-done.1), custom_call_target="tpu_custom_call" | custom-call | flops 1024 | bytes 1024 | tf_op jit(solution)/shard_map/pallas_call | solution.py:284
  58.3 0.0 collective-permute-done.7.come_ref
  58.3 2.1 %shard_map.106 = (bf16[512,1024]{1,0:T(8,128)(2,1)S(1)}, bf16[512,1024]{1,0:T(8,128)(2,1)S(1)}) custom-call(s32[1]{0:T(128)} %bitcast.7.chip_ref, bf16[2,512,1024]{2,1,0:T(8,128)(2,1)S(1)} %shard_map.105.keep_ref, bf16[2,512,1024]{2,1,0:T(8,128)(2,1)} %collective-permute-done.7.come_ref), custom_call_target="tpu_custom_call" | custom-call | flops 1024 | bytes 1024 | tf_op jit(solution)/shard_map/pallas_call | solution.py:319
  60.4 0.0 collective-permute-done.6.refs_3_
  60.4 0.6 collective-permute-start.11
  61.0 6.4 %collective-permute-done.1.refs_1_ = bf16[256,1024]{1,0:T(8,128)(2,1)S(1)} collective-permute-done((bf16[256,1024]{1,0:T(8,128)(2,1)S(1)}, bf16[256,1024]{1,0:T(8,128)(2,1)S(1)}, u32[]{:S(2)}, u32[]{:S(2)}) %collective-permute-start.1) | collective-permute-done | bytes 524320 | tf_op jit(solution)/shard_map/ppermute | solution.py:615
  67.4 0.6 shard_map.107
  67.9 0.7 collective-permute-start.10
  68.6 2.3 %collective-permute-start.8 = (bf16[160,1024]{1,0:T(8,128)(2,1)S(1)}, bf16[160,1024]{1,0:T(8,128)(2,1)S(1)}, u32[]{:S(2)}, u32[]{:S(2)}) collective-permute-start(bf16[160,1024]{1,0:T(8,128)(2,1)S(1)} %get-tuple-element.44), channel_id=1, source_target_pairs={{0,12},{4,0},{8,4},{12,8},{16,28},{20,16},{24,20},{28,24},{1,13},{... | collective-permute-start | bytes 983048 | tf_op jit(solution)/shard_map/ppermute | solution.py:626
  70.9 0.0 collective-permute-start.9
  70.9 11.7 %collective-permute-done.10.refs_3_ = bf16[160,1024]{1,0:T(8,128)(2,1)S(1)} collective-permute-done((bf16[160,1024]{1,0:T(8,128)(2,1)S(1)}, bf16[160,1024]{1,0:T(8,128)(2,1)S(1)}, u32[]{:S(2)}, u32[]{:S(2)}) %collective-permute-start.10) | collective-permute-done | bytes 327712 | tf_op jit(solution)/shard_map/ppermute | solution.py:626
  82.6 2.2 %collective-permute-done.8.refs_1_ = bf16[160,1024]{1,0:T(8,128)(2,1)S(1)} collective-permute-done((bf16[160,1024]{1,0:T(8,128)(2,1)S(1)}, bf16[160,1024]{1,0:T(8,128)(2,1)S(1)}, u32[]{:S(2)}, u32[]{:S(2)}) %collective-permute-start.8) | collective-permute-done | bytes 327712 | tf_op jit(solution)/shard_map/ppermute | solution.py:626
  84.8 0.0 collective-permute-done.9.refs_2_
  84.8 0.5 collective-permute-done.11.refs_5_
  85.4 3.0 %shard_map.108 = bf16[128,4,1024]{2,1,0:T(4,128)(2,1)} custom-call(bf16[512,640]{1,0:T(8,128)(2,1)S(1)} %shard_map.103.chosen_ref, bf16[160,1024]{1,0:T(8,128)(2,1)S(1)} %get-tuple-element.43.refs_0_, bf16[160,1024]{1,0:T(8,128)(2,1)S(1)} %collective-permute-done.8.refs_1_, bf16[160,1024]{1,0:T(8,128)(2,1)S(1)} %collective-permute-done.9.refs_2_, ...), custom_call_target="tpu_custom_call" | custom-call | flops 1024 | bytes 1024 | tf_op jit(solution)/shard_map/pallas_call | solution.py:536
  (1 shorter events, 0.0 us)
Async XLA Ops:
  0.0 40.9 %collective-permute-start = (bf16[256,1024]{1,0:T(8,128)(2,1)}, bf16[256,1024]{1,0:T(8,128)(2,1)S(1)}, u32[]{:S(2)}, u32[]{:S(2)}) collective-permute-start(bf16[256,1024]{1,0:T(8,128)(2,1)} %bitcast.10), channel_id=1, source_target_pairs={{0,16},{4,20},{8,24},{12,28},{16,0},{20,4},{24,8},{28,12},{1,17},{... | collective-permute-start | bytes 1572872 | tf_op jit(solution)/shard_map/ppermute | solution.py:600
  4.0 1.0 %copy-start.3 = (bf16[2,128,4,256]{3,2,1,0:T(4,128)(2,1)S(1)}, bf16[2,128,4,256]{3,2,1,0:T(4,128)(2,1)}, u32[]{:S(2)}) copy-start(bf16[2,128,4,256]{3,2,1,0:T(4,128)(2,1)} %fr_hbm.1) | copy-start | bytes 1572868
  5.1 0.7 copy-start.8
  5.7 0.7 copy-start.9
  6.4 20.0 %copy-start.2 = (s32[128,1]{0,1:T(1,128)S(1)}, s32[128,1]{0,1:T(1,128)}, u32[]{:S(2)}) copy-start(s32[128,1]{0,1:T(1,128)} %param.16) | copy-start | bytes 1540
  28.6 5.1 %copy-start.6 = (bf16[160,1024]{1,0:T(8,128)(2,1)}, bf16[160,1024]{1,0:T(8,128)(2,1)S(1)}, u32[]{:S(2)}) copy-start(bf16[160,1024]{1,0:T(8,128)(2,1)S(1)} %get-tuple-element.33.refs_2_) | copy-start | bytes 983044
  28.6 12.7 %collective-permute-start.2 = (bf16[160,1024]{1,0:T(8,128)(2,1)}, bf16[160,1024]{1,0:T(8,128)(2,1)}, u32[]{:S(2)}, u32[]{:S(2)}) collective-permute-start(bf16[160,1024]{1,0:T(8,128)(2,1)} %get-tuple-element.34), channel_id=1, source_target_pairs={{0,4},{4,8},{8,12},{12,0},{16,20},{20,24},{24,28},{28,16},{1,5},{5... | collective-permute-start | bytes 983048 | tf_op jit(solution)/shard_map/ppermute | solution.py:608
  30.2 11.2 %collective-permute-start.3 = (bf16[160,1024]{1,0:T(8,128)(2,1)}, bf16[160,1024]{1,0:T(8,128)(2,1)}, u32[]{:S(2)}, u32[]{:S(2)}) collective-permute-start(bf16[160,1024]{1,0:T(8,128)(2,1)} %get-tuple-element.35), channel_id=1, source_target_pairs={{0,8},{4,12},{8,0},{12,4},{16,24},{20,28},{24,16},{28,20},{1,9},{5... | collective-permute-start | bytes 983048 | tf_op jit(solution)/shard_map/ppermute | solution.py:608
  31.7 15.5 %collective-permute-start.4 = (bf16[160,1024]{1,0:T(8,128)(2,1)}, bf16[160,1024]{1,0:T(8,128)(2,1)}, u32[]{:S(2)}, u32[]{:S(2)}) collective-permute-start(bf16[160,1024]{1,0:T(8,128)(2,1)} %get-tuple-element.36), channel_id=1, source_target_pairs={{0,12},{4,0},{8,4},{12,8},{16,28},{20,16},{24,20},{28,24},{1,13},{... | collective-permute-start | bytes 983048 | tf_op jit(solution)/shard_map/ppermute | solution.py:608
  33.7 3.4 %copy-start = (bf16[1024,4096]{1,0:T(8,128)(2,1)S(1)}, bf16[1024,4096]{1,0:T(8,128)(2,1)}, u32[]{:S(2)}) copy-start(bf16[1024,4096]{1,0:T(8,128)(2,1)} %w_ref.3) | copy-start | bytes 25165828
  37.1 3.8 %copy-start.5 = (bf16[4,64,1024]{2,1,0:T(8,128)(2,1)S(1)}, bf16[4,64,1024]{2,1,0:T(8,128)(2,1)}, u32[]{:S(2)}) copy-start(bf16[4,64,1024]{2,1,0:T(8,128)(2,1)} %param.19) | copy-start | bytes 1572868
  37.1 10.1 %copy-start.4 = (bf16[4,64,1024]{2,1,0:T(8,128)(2,1)S(1)}, bf16[4,64,1024]{2,1,0:T(8,128)(2,1)}, u32[]{:S(2)}) copy-start(bf16[4,64,1024]{2,1,0:T(8,128)(2,1)} %param.18) | copy-start | bytes 1572868
  37.1 10.1 %copy-start.7 = (bf16[160,1024]{1,0:T(8,128)(2,1)S(1)}, bf16[160,1024]{1,0:T(8,128)(2,1)}, u32[]{:S(2)}) copy-start(bf16[160,1024]{1,0:T(8,128)(2,1)} %copy-done.6) | copy-start | bytes 983044
  40.9 17.4 %collective-permute-start.7 = (bf16[2,512,1024]{2,1,0:T(8,128)(2,1)}, bf16[2,512,1024]{2,1,0:T(8,128)(2,1)}, u32[]{:S(2)}, u32[]{:S(2)}) collective-permute-start(bf16[2,512,1024]{2,1,0:T(8,128)(2,1)} %shard_map.102), channel_id=1, source_target_pairs={{0,1},{1,0},{2,3},{3,2},{4,5},{5,4},{6,7},{7,6},{8,9},{9,8},{10,11... | collective-permute-start | bytes 6291464 | tf_op jit(solution)/shard_map/ppermute | solution.py:613
  40.9 26.4 %collective-permute-start.1 = (bf16[256,1024]{1,0:T(8,128)(2,1)S(1)}, bf16[256,1024]{1,0:T(8,128)(2,1)S(1)}, u32[]{:S(2)}, u32[]{:S(2)}) collective-permute-start(bf16[256,1024]{1,0:T(8,128)(2,1)S(1)} %bitcast.12), channel_id=1, source_target_pairs={{0,16},{4,20},{8,24},{12,28},{16,0},{20,4},{24,8},{28,12},{1,17},{... | collective-permute-start | bytes 1572872 | tf_op jit(solution)/shard_map/ppermute | solution.py:615
  49.0 1.5 %collective-permute-start.5 = (f32[320,128]{1,0:T(8,128)S(1)}, f32[320,128]{1,0:T(8,128)S(1)}, u32[]{:S(2)}, u32[]{:S(2)}) collective-permute-start(f32[320,128]{1,0:T(8,128)S(1)} %shard_map.104), channel_id=1, source_target_pairs={{0,1},{1,0},{2,3},{3,2},{4,5},{5,4},{6,7},{7,6},{8,9},{9,8},{10,11... | collective-permute-start | bytes 491528 | tf_op jit(solution)/shard_map/ppermute | solution.py:617
  50.5 9.9 %collective-permute-start.6 = (bf16[320,128]{1,0:T(8,128)(2,1)S(1)}, bf16[320,128]{1,0:T(8,128)(2,1)S(1)}, u32[]{:S(2)}, u32[]{:S(2)}) collective-permute-start(bf16[320,128]{1,0:T(8,128)(2,1)S(1)} %add_convert_fusion.refs_2_), channel_id=1, source_target_pairs={{0,2},{1,3},{2,0},{3,1},{4,6},{5,7},{6,4},{7,5},{8,10},{9,11},{10,... | collective-permute-start | bytes 245768 | tf_op jit(solution)/shard_map/ppermute | solution.py:621
  52.1 3.4 %copy-start.1 = (bf16[1024,4096]{1,0:T(8,128)(2,1)S(1)}, bf16[1024,4096]{1,0:T(8,128)(2,1)}, u32[]{:S(2)}) copy-start(bf16[1024,4096]{1,0:T(8,128)(2,1)} %w_ref.3) | copy-start | bytes 25165828
  60.4 25.0 %collective-permute-start.11 = (bf16[512,1024]{1,0:T(8,128)(2,1)S(1)}, bf16[512,1024]{1,0:T(8,128)(2,1)S(1)}, u32[]{:S(2)}, u32[]{:S(2)}) collective-permute-start(bf16[512,1024]{1,0:T(8,128)(2,1)S(1)} %get-tuple-element.48), channel_id=1, source_target_pairs={{0,2},{1,3},{2,0},{3,1},{4,6},{5,7},{6,4},{7,5},{8,10},{9,11},{10,... | collective-permute-start | bytes 3145736 | tf_op jit(solution)/shard_map/ppermute | solution.py:593
  67.9 14.7 %collective-permute-start.10 = (bf16[160,1024]{1,0:T(8,128)(2,1)S(1)}, bf16[160,1024]{1,0:T(8,128)(2,1)S(1)}, u32[]{:S(2)}, u32[]{:S(2)}) collective-permute-start(bf16[160,1024]{1,0:T(8,128)(2,1)S(1)} %get-tuple-element.46), channel_id=1, source_target_pairs={{0,4},{4,8},{8,12},{12,0},{16,20},{20,24},{24,28},{28,16},{1,5},{5... | collective-permute-start | bytes 983048 | tf_op jit(solution)/shard_map/ppermute | solution.py:626
  68.6 16.2 %collective-permute-start.8 = (bf16[160,1024]{1,0:T(8,128)(2,1)S(1)}, bf16[160,1024]{1,0:T(8,128)(2,1)S(1)}, u32[]{:S(2)}, u32[]{:S(2)}) collective-permute-start(bf16[160,1024]{1,0:T(8,128)(2,1)S(1)} %get-tuple-element.44), channel_id=1, source_target_pairs={{0,12},{4,0},{8,4},{12,8},{16,28},{20,16},{24,20},{28,24},{1,13},{... | collective-permute-start | bytes 983048 | tf_op jit(solution)/shard_map/ppermute | solution.py:626
  70.9 13.9 %collective-permute-start.9 = (bf16[160,1024]{1,0:T(8,128)(2,1)S(1)}, bf16[160,1024]{1,0:T(8,128)(2,1)S(1)}, u32[]{:S(2)}, u32[]{:S(2)}) collective-permute-start(bf16[160,1024]{1,0:T(8,128)(2,1)S(1)} %get-tuple-element.45), channel_id=1, source_target_pairs={{0,8},{4,12},{8,0},{12,4},{16,24},{20,28},{24,16},{28,20},{1,9},{5... | collective-permute-start | bytes 983048 | tf_op jit(solution)/shard_map/ppermute | solution.py:626
